TPU v7x, 32 devices: a whole 2x2x4 slice. The times are simulated.
32 devices in a mesh: doc: 2 (over core), seq: 4 (over y, x), mp: 4 (over z).
Axes of the slice: x: 2, y: 2, z: 4, core: 2. Of those that a mesh axis runs over, the one named last changes fastest.
Arguments:
- hidden_in: bfloat16 [6144, 2048], P(('doc', 'seq')), may hold values from -6 to 6
- cotangent: bfloat16 [6144, 2048], P(('doc', 'seq')), may hold values from -6 to 6
- segment_ids: int32 [6144], P(('doc', 'seq')), may hold values from 0 to 4, as said below
- padding: int32 [6144], P(('doc', 'seq')), may hold values 0 or 1
- span_order: int32 [8], replicated, may hold values from 0 to 7, as said below
- gain_attn: float32 [2048], replicated, may hold values from 0.1 to 1.9
- gain_mlp: float32 [2048], replicated, may hold values from 0.1 to 1.9
- w_query: bfloat16 [2048, 2048], P(None, 'mp'), may hold values from -0.125 to 0.125
- w_key: bfloat16 [2048, 2048], P(None, 'mp'), may hold values from -0.125 to 0.125
- w_value: bfloat16 [2048, 2048], P(None, 'mp'), may hold values from -0.125 to 0.125
- w_out: bfloat16 [2048, 2048], P('mp'), may hold values from -0.125 to 0.125
- w_gate: bfloat16 [2048, 5632], P(None, 'mp'), may hold values from -0.125 to 0.125
- w_up: bfloat16 [2048, 5632], P(None, 'mp'), may hold values from -0.125 to 0.125
- w_down: bfloat16 [5632, 2048], P('mp'), may hold values from -0.078125 to 0.078125
- a_query: float32 [2048, 16], replicated, may hold values from -0.125 to 0.125
- b_query: float32 [16, 2048], P(None, 'mp'), may hold values from -0.3 to 0.3
- m_query: float32 [2048], P('mp'), may hold values from 0.5 to 2
- a_key: float32 [2048, 16], replicated, may hold values from -0.125 to 0.125
- b_key: float32 [16, 2048], P(None, 'mp'), may hold values from -0.3 to 0.3
- m_key: float32 [2048], P('mp'), may hold values from 0.5 to 2
- a_value: float32 [2048, 16], replicated, may hold values from -0.125 to 0.125
- b_value: float32 [16, 2048], P(None, 'mp'), may hold values from -0.3 to 0.3
- m_value: float32 [2048], P('mp'), may hold values from 0.5 to 2
- a_out: float32 [2048, 16], P('mp'), may hold values from -0.125 to 0.125
- b_out: float32 [16, 2048], replicated, may hold values from -0.3 to 0.3
- m_out: float32 [2048], replicated, may hold values from 8 to 32
- a_gate: float32 [2048, 16], replicated, may hold values from -0.125 to 0.125
- b_gate: float32 [16, 5632], P(None, 'mp'), may hold values from -0.3 to 0.3
- m_gate: float32 [5632], P('mp'), may hold values from 0.5 to 2
- a_up: float32 [2048, 16], replicated, may hold values from -0.125 to 0.125
- b_up: float32 [16, 5632], P(None, 'mp'), may hold values from -0.3 to 0.3
- m_up: float32 [5632], P('mp'), may hold values from 0.5 to 2
- a_down: float32 [5632, 16], P('mp'), may hold values from -0.078125 to 0.078125
- b_down: float32 [16, 2048], replicated, may hold values from -0.3 to 0.3
- m_down: float32 [2048], replicated, may hold values from 0.5 to 2
Outputs:
- result: float32 [6144, 2048], P(('doc', 'seq', 'mp'))
- grad_input: float32 [6144, 2048], P(('doc', 'seq', 'mp'))
- grad_a_query: float32 [2048, 16], replicated
- grad_b_query: float32 [16, 2048], P(None, 'mp')
- grad_m_query: float32 [2048], P('mp')
- grad_a_key: float32 [2048, 16], replicated
- grad_b_key: float32 [16, 2048], P(None, 'mp')
- grad_m_key: float32 [2048], P('mp')
- grad_a_value: float32 [2048, 16], replicated
- grad_b_value: float32 [16, 2048], P(None, 'mp')
- grad_m_value: float32 [2048], P('mp')
- grad_a_out: float32 [2048, 16], P('mp')
- grad_b_out: float32 [16, 2048], replicated
- grad_m_out: float32 [2048], replicated
- grad_a_gate: float32 [2048, 16], replicated
- grad_b_gate: float32 [16, 5632], P(None, 'mp')
- grad_m_gate: float32 [5632], P('mp')
- grad_a_up: float32 [2048, 16], replicated
- grad_b_up: float32 [16, 5632], P(None, 'mp')
- grad_m_up: float32 [5632], P('mp')
- grad_a_down: float32 [5632, 16], P('mp')
- grad_b_down: float32 [16, 2048], replicated
- grad_m_down: float32 [2048], replicated
Inputs may be any that keep to these rules, and one draw needn't show every extreme that they name: `span_order`: each slot holds a different span of its group. `segment_ids`: within each group of 3072 rows, read by positions, document numbers never fall; one document of each group has rows in every span.
All inputs are finite; a program needn't handle non-finite values. No bound on the sum of `padding` on one device may be relied on, other than what follows from the above.
Results may differ from a plain program's by a relative error of at most 0.033.
Values may be sent and summed in bfloat16 or wider, within the bound.
No kernel may reach another device: no remote copies, remote signals or barrier semaphores. Data moves between devices by JAX's collectives and lax.ppermute only.
A program may use at most 448 MiB of HBM per device.

v0:
```python
import functools
import math

import jax
import jax.numpy as jnp
import numpy as np
from jax import lax
from jax.experimental import pallas as pl
from jax.experimental.pallas import tpu as pltpu
from jax.sharding import PartitionSpec as P

HD = 128
RANK = 16
ALPHA = 32
HALF = HD // 2
SCALING = ALPHA / RANK
INV_ROOT = HD ** (-0.5)
EPS = 1e-05
ROPE_BASE = 10000.0
MASKED = -1e30
CHUNKS = 2
MIB = 1 << 20
VMEM_LIMIT = 56 * MIB

f32 = jnp.float32
bf16 = jnp.bfloat16


def dot(left, right):
    return jnp.dot(left, right, preferred_element_type=f32)


def dot_nt(left, right):
    return lax.dot_general(left, right, (((1,), (1,)), ((), ())), preferred_element_type=f32)


def dot_tn(left, right):
    return lax.dot_general(left, right, (((0,), (0,)), ((), ())), preferred_element_type=f32)


def whole_spec(array):
    rank = len(array.shape)
    return pl.BlockSpec(tuple(array.shape), lambda *_: (0,) * rank)


def cost(flops, moved):
    return pl.CostEstimate(flops=1, bytes_accessed=1, transcendentals=0)


def swap(value, axis, distance):
    size = lax.axis_size(axis)
    return lax.ppermute(value, axis, [(i, i ^ distance) for i in range(size)])


def butterfly(value, axes):
    for axis in axes:
        distance = 1
        while distance < lax.axis_size(axis):
            value = lax.optimization_barrier(value + swap(value, axis, distance))
            distance *= 2
    return value


def doc_halve(value):
    doc = lax.axis_index("doc")
    half = value.shape[0] // 2
    mine = lax.dynamic_slice_in_dim(value, doc * half, half, 0)
    other = lax.dynamic_slice_in_dim(value, (1 - doc) * half, half, 0)
    return lax.optimization_barrier(mine + swap(other, "doc", 1))


def doc_join(mine):
    doc = lax.axis_index("doc")
    other = swap(mine, "doc", 1)
    first = jnp.where(doc == 0, mine, other)
    second = jnp.where(doc == 0, other, mine)
    return jnp.concatenate([first, second], axis=0)


def spread_sum(value, peers, axes):
    me = lax.rem(lax.axis_index("seq"), peers)
    parts = value.reshape(peers, -1, value.shape[-1])
    piece = lambda index: lax.dynamic_index_in_dim(parts, index, 0, keepdims=False)
    mine = piece(me).astype(f32)
    for d in range(1, peers):
        mine = mine + swap(piece(me ^ d), "seq", d).astype(f32)
    mine = lax.optimization_barrier(mine.astype(bf16))
    distance = peers
    while distance < lax.axis_size("seq"):
        mine = lax.optimization_barrier(mine + swap(mine, "seq", distance))
        distance *= 2
    return butterfly(mine, axes)


def spread_join(mine, peers):
    me = lax.rem(lax.axis_index("seq"), peers)
    found = [mine] + [swap(mine, "seq", d) for d in range(1, peers)]
    return jnp.concatenate([pick_blocks(found, me ^ i) for i in range(peers)], axis=0)


def after(values, *earlier):
    tied = lax.optimization_barrier((tuple(values), earlier))
    return tied[0]


def line_step(rights, lefts, step, *earlier):
    size = lax.axis_size("mp")
    right, left = rights[-1], lefts[-1]
    if earlier:
        right, left = after([right, left], *earlier)
    right_pairs = [(i, i + 1) for i in range(step - 1, size - 1)]
    left_pairs = [(i, i - 1) for i in range(1, size - step + 1)]
    rights.append(lax.ppermute(right, "mp", right_pairs))
    lefts.append(lax.ppermute(left, "mp", left_pairs))


def line_blocks(rights, lefts):
    size = lax.axis_size("mp")
    k = lax.axis_index("mp")
    return [rights[0]] + [
        jnp.where(k + c < size, lefts[c], rights[size - c]) for c in range(1, size)
    ]


def seq_exchange(blocks):
    return [blocks[0]] + [swap(blocks[d], "seq", d) for d in range(1, len(blocks))]


def key_marks(code):
    lane = lax.broadcasted_iota(jnp.int32, (code.shape[0], HD), 1)
    segment, real = code >> 1, code & 1
    wrong = (lane < 16) & (lane != segment)
    absent = (lane == 16) & (real == 0)
    return jnp.where(wrong | absent, MASKED, 0.0).astype(bf16)


def query_marks(code):
    lane = lax.broadcasted_iota(jnp.int32, (code.shape[0], HD), 1)
    segment = code >> 1
    return jnp.where((lane == segment) | (lane == 16), 1.0, 0.0).astype(bf16)


def diagonal_scores(keys, query, first_key=0):
    marked = dot_nt(keys, query)
    plain = dot_nt(keys[:, :HD], query[:, :HD])
    key_id = lax.broadcasted_iota(jnp.int32, marked.shape, 0) + first_key
    query_id = lax.broadcasted_iota(jnp.int32, marked.shape, 1)
    return jnp.where(
        key_id < query_id, marked, jnp.where(key_id == query_id, plain, MASKED)
    )


def block_readers(groups, heads, kv_refs, code_refs):
    if groups == 1:
        return (
            lambda g, d, rows: heads[d][0, rows, :],
            lambda g, d, rows: heads[d][1, rows, :],
            lambda g, d, rows: code_refs[d][rows, :],
        )
    return (
        lambda g, d, rows: kv_refs[0][g, d, 0, rows, :],
        lambda g, d, rows: kv_refs[0][g, d, 1, rows, :],
        lambda g, d, rows: kv_refs[1][g, d, rows, :],
    )


def taker(refs):
    refs = list(refs)

    def take(count):
        taken = refs[:count]
        del refs[:count]
        return taken

    return take


def forward_kernel(meta, scalars, *refs):
    peers, groups, span, pieces, chunks, n_extra = meta
    take = taker(refs)
    heads, code_refs, kv_refs = take(peers), take(peers), take(n_extra)
    o_refs, (lse_ref,) = take(peers), take(1)
    q_all, o_all, k_all, v_turned = take(4)
    key_of, value_of, key_code_of = block_readers(groups, heads, kv_refs, code_refs)
    n_query = 2 * peers

    for g in range(groups):
        for d in range(peers):
            for half in range(2):
                rows = pl.ds(half * span, span)
                place = scalars[n_query + (g * peers + d) * 2 + half]
                at = pl.ds(pl.multiple_of(place * span, HD), span)
                k_all[at, :HD] = key_of(g, d, rows)
                k_all[at, HD:] = key_marks(key_code_of(g, d, rows))
                v_turned[:, at] = value_of(g, d, rows).astype(f32).T.astype(bf16)
    for d in range(peers):
        for half in range(2):
            rows = pl.ds(half * span, span)
            q_all[2 * d + half, :, :HD] = heads[d][2, rows, :]
            q_all[2 * d + half, :, HD:] = query_marks(code_refs[d][rows, :])

    def one_span(i, carry):
        place = scalars[i]
        query = q_all[i]
        at = pl.ds(pl.multiple_of(place * span, HD), span)
        scores = diagonal_scores(k_all[at, :], query)
        peak = jnp.max(scores, axis=0, keepdims=True)
        weights = jnp.exp((scores - peak) * INV_ROOT)
        total = jnp.sum(weights, axis=0, keepdims=True)
        out = dot(v_turned[:, at], weights.astype(bf16))

        def key_span(j, state):
            peak, total, out = state
            at = pl.ds(pl.multiple_of(j * span, HD), span)
            scores = dot_nt(k_all[at, :], query)
            new_peak = jnp.maximum(peak, jnp.max(scores, axis=0, keepdims=True))
            fade = jnp.exp((peak - new_peak) * INV_ROOT)
            weights = jnp.exp((scores - new_peak) * INV_ROOT)
            total = total * fade + jnp.sum(weights, axis=0, keepdims=True)
            out = out * fade + dot(v_turned[:, at], weights.astype(bf16))
            return (new_peak, total, out)

        peak, total, out = lax.fori_loop(0, place, key_span, (peak, total, out))
        lse_ref[i] = peak * INV_ROOT + jnp.log(total)
        o_all[i] = (out / total).T.astype(bf16)
        return carry

    lax.fori_loop(0, n_query, one_span, 0)
    share = 2 * span // pieces
    part = share // chunks
    for d in range(peers):
        for piece in range(pieces):
            for c in range(chunks):
                row = piece * share + c * part
                to = (c * pieces + piece) * part
                o_refs[d][to : to + part, :] = o_all[
                    2 * d + row // span, row % span : row % span + part, :
                ]


def place_rows(scalars, peers, span):
    for d in range(peers):
        for half in range(2):
            place = scalars[2 * d + half]
            at = pl.ds(pl.multiple_of(place * span, HD), span)
            yield d, half, pl.ds(half * span, span), at


def piece_rows(peers, span, pieces, chunks):
    share = 2 * span // pieces
    part = share // chunks
    for d in range(peers):
        for piece in range(pieces):
            for c in range(chunks):
                row = piece * share + c * part
                yield d, piece, c, pl.ds((c * pieces + piece) * part, part), row, part


def forward_group_kernel(meta, scalars, *refs):
    peers, _, span, pieces, chunks, _ = meta
    take = taker(refs)
    heads, code_refs = take(peers), take(peers)
    o_refs, (lse_ref,) = take(peers), take(1)
    q_all, o_all, k_all, v_turned = take(4)
    tile = 2 * span

    for d, half, rows, at in place_rows(scalars, peers, span):
        code = code_refs[d][rows, :]
        k_all[at, :HD] = heads[d][0, rows, :]
        k_all[at, HD:] = key_marks(code)
        v_turned[:, at] = heads[d][1, rows, :].astype(f32).T.astype(bf16)
        q_all[at, :HD] = heads[d][2, rows, :]
        q_all[at, HD:] = query_marks(code)

    for m in range(peers):
        here = slice(m * tile, (m + 1) * tile)
        query = q_all[here, :]
        scores = diagonal_scores(k_all[here, :], query)
        peak = jnp.max(scores, axis=0, keepdims=True)
        weights = jnp.exp((scores - peak) * INV_ROOT)
        total = jnp.sum(weights, axis=0, keepdims=True)
        out = dot(v_turned[:, here], weights.astype(bf16))

        def key_tile(j, state):
            peak, total, out = state
            at = pl.ds(pl.multiple_of(j * tile, HD), tile)
            scores = dot_nt(k_all[at, :], query)
            new_peak = jnp.maximum(peak, jnp.max(scores, axis=0, keepdims=True))
            fade = jnp.exp((peak - new_peak) * INV_ROOT)
            weights = jnp.exp((scores - new_peak) * INV_ROOT)
            total = total * fade + jnp.sum(weights, axis=0, keepdims=True)
            out = out * fade + dot(v_turned[:, at], weights.astype(bf16))
            return (new_peak, total, out)

        if m:
            steps = m * tile // tile
            peak, total, out = lax.fori_loop(0, steps, key_tile, (peak, total, out))
        lse_ref[m] = peak * INV_ROOT + jnp.log(total)
        o_all[here, :] = (out / total).T.astype(bf16)

    for d, piece, c, to, row, part in piece_rows(peers, span, pieces, chunks):
        place = scalars[2 * d + row // span] * span + row % span
        o_refs[d][to, :] = o_all[pl.ds(pl.multiple_of(place, 32), part), :]


def backward_group_kernel(meta, scalars, *refs):
    peers, groups, span, pieces, chunks, _ = meta
    take = taker(refs)
    heads, code_refs = take(peers), take(peers)
    o_refs, do_refs, (lse_ref,) = take(peers), take(peers), take(1)
    grad_refs = take(peers)
    q_all, o_all, do_all, k_all, k_turned, v_all, dk_all, dv_all = take(8)
    own_piece = scalars[4 * peers]
    tile = 2 * span
    share = 2 * span // pieces

    for d, half, rows, at in place_rows(scalars, peers, span):
        code = code_refs[d][rows, :]
        key = heads[d][0, rows, :]
        k_all[at, :HD] = key
        k_all[at, HD:] = key_marks(code)
        k_turned[:, at] = key.astype(f32).T.astype(bf16)
        v_all[at, :] = heads[d][1, rows, :]
        q_all[at, :HD] = heads[d][2, rows, :]
        q_all[at, HD:] = query_marks(code)
    for d, piece, c, source, row, part in piece_rows(peers, span, pieces, chunks):
        place = scalars[2 * d + row // span] * span + row % span
        o_all[pl.ds(pl.multiple_of(place, 32), part), :] = o_refs[d][source, :]
        row = lax.rem(own_piece + pieces - piece, pieces) * share + c * part
        late = row >= span
        place = scalars[2 * d + late.astype(jnp.int32)] * span + row - jnp.where(late, span, 0)
        do_all[pl.ds(pl.multiple_of(place, 32), part), :] = do_refs[d][source, :]

    for m in range(peers):
        here = slice(m * tile, (m + 1) * tile)
        query = q_all[here, :]
        grad = do_all[here, :]
        product = grad.astype(f32) * o_all[here, :].astype(f32)
        high, rest = split_low(product)
        ones = jnp.ones((16, HD), bf16)
        delta = (dot_nt(ones, high) + dot_nt(ones, rest))[:1, :]
        lse = lse_ref[m]

        def key_tile(at, scores, dq_turned, first):
            probs = jnp.exp(scores * INV_ROOT - lse)
            grad_score = (probs * (dot_nt(v_all[at, :], grad) - delta)).astype(bf16)
            dv = dot(probs.astype(bf16), grad)
            dk = dot(grad_score, query[:, :HD])
            if first:
                dv_all[at, :] = dv
                dk_all[at, :] = dk
            else:
                dv_all[at, :] += dv
                dk_all[at, :] += dk
            return dq_turned + dot(k_turned[:, at], grad_score)

        dq_turned = jnp.zeros((HD, tile), f32)
        for t in range(tile // tile):
            at = pl.ds(m * tile + t * tile, tile)
            scores = diagonal_scores(k_all[at, :], query, t * tile)
            dq_turned = key_tile(at, scores, dq_turned, True)

        def step(j, dq_turned):
            at = pl.ds(pl.multiple_of(j * tile, HD), tile)
            return key_tile(at, dot_nt(k_all[at, :], query), dq_turned, False)

        if m:
            dq_turned = lax.fori_loop(0, m * tile // tile, step, dq_turned)
        o_all[here, :] = (dq_turned * INV_ROOT).T.astype(bf16)

    for d, half, rows, at in place_rows(scalars, peers, span):
        grad_refs[d][0, rows, :] = (dk_all[at, :] * INV_ROOT).astype(bf16)
        grad_refs[d][1, rows, :] = dv_all[at, :].astype(bf16)
        grad_refs[d][2, rows, :] = o_all[at, :]


def attention_forward(scalars, heads, codes, extra, groups, pieces, chunks):
    peers = len(heads)
    rows = heads[0].shape[1]
    span = rows // 2
    key_rows = groups * peers * rows
    meta = (peers, groups, span, pieces, chunks, len(extra))
    operands = [*heads, *codes, *extra]
    out_shape = [jax.ShapeDtypeStruct((rows, HD), bf16)] * peers
    n_query = 2 * peers if groups > 1 else peers
    out_shape.append(jax.ShapeDtypeStruct((n_query, 1, 2 * peers * span // n_query), f32))
    if groups == 1:
        body, q_shape, o_shape = forward_group_kernel, (key_rows, 2 * HD), (key_rows, HD)
    else:
        body, q_shape, o_shape = (
            forward_kernel,
            (2 * peers, span, 2 * HD),
            (2 * peers, span, HD),
        )
    outs = pl.pallas_call(
        functools.partial(body, meta),
        grid_spec=pltpu.PrefetchScalarGridSpec(
            num_scalar_prefetch=1,
            grid=(1,),
            in_specs=[whole_spec(x) for x in operands],
            out_specs=[whole_spec(x) for x in out_shape],
            scratch_shapes=[
                pltpu.VMEM(q_shape, bf16),
                pltpu.VMEM(o_shape, bf16),
                pltpu.VMEM((key_rows, 2 * HD), bf16),
                pltpu.VMEM((HD, key_rows), bf16),
            ],
        ),
        out_shape=out_shape,
        compiler_params=pltpu.CompilerParams(vmem_limit_bytes=VMEM_LIMIT),
        cost_estimate=cost(6 * peers * rows * key_rows // 2 * HD, 8 * key_rows * HD),
        name="attend",
    )(scalars, *operands)
    return outs[:-1], outs[-1]


def backward_kernel(meta, scalars, *refs):
    peers, groups, span, pieces, chunks, n_extra = meta
    take = taker(refs)
    heads, code_refs, kv_refs = take(peers), take(peers), take(n_extra)
    o_refs, do_refs, (lse_ref,) = take(peers), take(peers), take(1)
    grad_refs = take(peers)
    dkv_refs = take(1 if groups > 1 else 0)
    q_all, o_all, do_all, k_all, k_turned, v_all, dk_all, dv_all = take(8)
    key_of, value_of, key_code_of = block_readers(groups, heads, kv_refs, code_refs)
    n_query = 2 * peers
    own_piece = scalars[n_query + 2 * groups * peers]

    for g in range(groups):
        for d in range(peers):
            for half in range(2):
                rows = pl.ds(half * span, span)
                place = scalars[n_query + (g * peers + d) * 2 + half]
                at = pl.ds(pl.multiple_of(place * span, HD), span)
                key = key_of(g, d, rows)
                k_all[at, :HD] = key
                k_all[at, HD:] = key_marks(key_code_of(g, d, rows))
                k_turned[:, at] = key.astype(f32).T.astype(bf16)
                v_all[at, :] = value_of(g, d, rows)
    dk_all[...] = jnp.zeros_like(dk_all)
    dv_all[...] = jnp.zeros_like(dv_all)
    share = 2 * span // pieces
    part = share // chunks
    for d in range(peers):
        for half in range(2):
            rows = pl.ds(half * span, span)
            q_all[2 * d + half, :, :HD] = heads[d][2, rows, :]
            q_all[2 * d + half, :, HD:] = query_marks(code_refs[d][rows, :])
        for piece in range(pieces):
            origin = lax.rem(own_piece + pieces - piece, pieces)
            for c in range(chunks):
                source = pl.ds((c * pieces + piece) * part, part)
                row = (2 * d * span) + piece * share + c * part
                o_all[row : row + part, :] = o_refs[d][source, :]
                row = (2 * d * span) + origin * share + c * part
                do_all[pl.ds(pl.multiple_of(row, 16), part), :] = do_refs[d][source, :]

    def one_span(i, carry):
        place = scalars[i]
        query = q_all[i]
        rows = pl.ds(pl.multiple_of(i * span, HD), span)
        grad = do_all[rows, :]
        product = grad.astype(f32) * o_all[rows, :].astype(f32)
        high = product.astype(bf16)
        rest = (product - high.astype(f32)).astype(bf16)
        ones = jnp.ones((16, HD), bf16)
        delta = (dot_nt(ones, high) + dot_nt(ones, rest))[:1, :]
        lse = lse_ref[i]

        def key_span(at, scores, dq_turned):
            probs = jnp.exp(scores * INV_ROOT - lse)
            grad_prob = dot_nt(v_all[at, :], grad)
            grad_score = (probs * (grad_prob - delta)).astype(bf16)
            dv_all[at, :] += dot(probs.astype(bf16), grad)
            dk_all[at, :] += dot(grad_score, query[:, :HD])
            return dq_turned + dot(k_turned[:, at], grad_score)

        at = pl.ds(pl.multiple_of(place * span, HD), span)
        dq_turned = key_span(
            at, diagonal_scores(k_all[at, :], query), jnp.zeros((HD, span), f32)
        )

        def step(j, dq_turned):
            at = pl.ds(pl.multiple_of(j * span, HD), span)
            return key_span(at, dot_nt(k_all[at, :], query), dq_turned)

        dq_turned = lax.fori_loop(0, place, step, dq_turned)
        o_all[rows, :] = (dq_turned * INV_ROOT).T.astype(bf16)
        return carry

    lax.fori_loop(0, n_query, one_span, 0)
    at_query = 2 if groups == 1 else 0
    for d in range(peers):
        grad_refs[d][at_query] = o_all[2 * d * span : 2 * (d + 1) * span, :]
    for g in range(groups):
        for d in range(peers):
            for half in range(2):
                rows = pl.ds(half * span, span)
                place = scalars[n_query + (g * peers + d) * 2 + half]
                at = pl.ds(pl.multiple_of(place * span, HD), span)
                grad_key = (dk_all[at, :] * INV_ROOT).astype(bf16)
                grad_value = dv_all[at, :].astype(bf16)
                if groups == 1:
                    grad_refs[d][0, rows, :] = grad_key
                    grad_refs[d][1, rows, :] = grad_value
                else:
                    dkv_refs[0][g, d, 0, rows, :] = grad_key
                    dkv_refs[0][g, d, 1, rows, :] = grad_value


def attention_backward(scalars, heads, codes, extra, o, grads, lse, groups, pieces, chunks):
    peers = len(heads)
    rows = heads[0].shape[1]
    span = rows // 2
    key_rows = groups * peers * rows
    meta = (peers, groups, span, pieces, chunks, len(extra))
    operands = [*heads, *codes, *extra, *o, *grads, lse]
    parts = 3 if groups == 1 else 1
    out_shape = [jax.ShapeDtypeStruct((parts, rows, HD), bf16)] * peers
    if groups > 1:
        out_shape.append(jax.ShapeDtypeStruct(extra[0].shape, bf16))
    if groups == 1:
        body, q_shape = backward_group_kernel, (key_rows, 2 * HD)
    else:
        body, q_shape = backward_kernel, (2 * peers, span, 2 * HD)
    outs = pl.pallas_call(
        functools.partial(body, meta),
        grid_spec=pltpu.PrefetchScalarGridSpec(
            num_scalar_prefetch=1,
            grid=(1,),
            in_specs=[whole_spec(x) for x in operands],
            out_specs=[whole_spec(x) for x in out_shape],
            scratch_shapes=[
                pltpu.VMEM(q_shape, bf16),
                pltpu.VMEM((peers * rows, HD), bf16),
                pltpu.VMEM((peers * rows, HD), bf16),
                pltpu.VMEM((key_rows, 2 * HD), bf16),
                pltpu.VMEM((HD, key_rows), bf16),
                pltpu.VMEM((key_rows, HD), bf16),
                pltpu.VMEM((key_rows, HD), f32),
                pltpu.VMEM((key_rows, HD), f32),
            ],
        ),
        out_shape=out_shape,
        compiler_params=pltpu.CompilerParams(vmem_limit_bytes=VMEM_LIMIT),
        cost_estimate=cost(14 * peers * rows * key_rows // 2 * HD, 16 * key_rows * HD),
        name="attend_back",
    )(scalars, *operands)
    if groups == 1:
        return outs, None
    return outs[:peers], outs[peers]


def split_low(value):
    high = value.astype(bf16)
    return high, (value - high.astype(f32)).astype(bf16)


def low_rank(a_t, b):
    a_high, a_rest = split_low(a_t)
    b_high, b_rest = split_low(b * SCALING)
    a_cat = jnp.concatenate([a_high, a_rest, a_high], axis=0)
    b_cat = jnp.concatenate([b_high, b_high, b_rest], axis=0)
    return dot_tn(a_cat, b_cat)


def separate(both):
    rows, width = both.shape
    both = both.reshape(rows, -1, 2, HD)
    return both[:, :, 0].reshape(rows, width // 2), both[:, :, 1].reshape(rows, width // 2)


def merge_kernel(starts, out_w, out_a, out_b, down_w, down_a, down_b, gate_w, up_w, gate_a, up_a,
                 gate_b, up_b, gate_m, up_m, out_square, out_cross, down_square, down_cross,
                 down_low, pair_low, pair_cross, pair_column, pair_scale, mixed_m, mixed_b):
    step = pl.program_id(0)
    down_start, pair_start = starts

    def columns(w_ref, a_ref, b_ref, square_ref, cross_ref, low_ref):
        merged = w_ref[...].astype(f32) + low_rank(a_ref[...], b_ref[...])
        low = merged.astype(bf16)
        if low_ref is not None:
            low_ref[...] = low
        square_ref[...] = jnp.sum(merged * merged, axis=0, keepdims=True)
        cross_ref[...] = dot(a_ref[...].astype(bf16), low)

    @pl.when(step < down_start)
    def _():
        columns(out_w, out_a, out_b, out_square, out_cross, None)

    @pl.when((step >= down_start) & (step < pair_start))
    def _():
        columns(down_w, down_a, down_b, down_square, down_cross, down_low)

    sides = ((gate_w, gate_a, gate_b, gate_m), (up_w, up_a, up_b, up_m))
    blocks = [
        (side, slice(j * HD, (j + 1) * HD), pl.ds((2 * j + side) * HD, HD))
        for side in range(2)
        for j in range(gate_w.shape[1] // HD)
    ]

    @pl.when(step == pair_start)
    def _():
        pair_column[...] = jnp.zeros_like(pair_column)
        pair_cross[...] = jnp.zeros_like(pair_cross)
        for side, source, at in blocks:
            mixed_b[:, at] = sides[side][2][:, source]
            mixed_m[:, at] = sides[side][3][:, source]

    @pl.when(step >= pair_start)
    def _():
        results = []
        for w_ref, a_ref, b_ref, _ in sides:
            merged = w_ref[...].astype(f32) + low_rank(a_ref[...], b_ref[...])
            low = merged.astype(bf16)
            square = jnp.sum(merged * merged, axis=0, keepdims=True)
            results.append((low, square, dot(a_ref[...].astype(bf16), low)))
        for side, source, at in blocks:
            low, square, cross = results[side]
            pair_low[:, at] = low[:, source]
            pair_column[:, at] += square[:, source]
            pair_cross[:, at] += cross[:, source]

    @pl.when(step == pl.num_programs(0) - 1)
    def _():
        column = jnp.sqrt(pair_column[...])
        pair_column[...] = column
        pair_scale[...] = mixed_m[...] / column


def merge_others(out, down, gate, up):
    step = 8 * HD
    rows = 2 * HD
    near, wide = out[0].shape
    ff = down[0].shape[0]
    depth, width = gate[0].shape
    n_columns = wide // step
    starts = (n_columns, 2 * n_columns)
    n_pair = depth // rows
    at_out = lambda i: jnp.minimum(i, n_columns - 1)
    at_down = lambda i: jnp.clip(i - starts[0], 0, n_columns - 1)
    at_pair = lambda i: jnp.clip(i - starts[1], 0, n_pair - 1)
    cut = lambda height, at: pl.BlockSpec((height, step), lambda i: (0, at(i)))
    fixed = lambda *shape: pl.BlockSpec(shape, lambda i: (0,) * len(shape))
    pair_rows = lambda lanes: pl.BlockSpec((rows, lanes), lambda i: (at_pair(i), 0))
    turned = pl.BlockSpec((RANK, rows), lambda i: (0, at_pair(i)))
    shape = jax.ShapeDtypeStruct
    return pl.pallas_call(
        functools.partial(merge_kernel, starts),
        grid=(starts[1] + n_pair,),
        in_specs=[
            cut(near, at_out),
            fixed(RANK, near),
            cut(RANK, at_out),
            cut(ff, at_down),
            fixed(RANK, ff),
            cut(RANK, at_down),
            pair_rows(width),
            pair_rows(width),
            turned,
            turned,
            fixed(RANK, width),
            fixed(RANK, width),
            fixed(1, width),
            fixed(1, width),
        ],
        out_specs=[
            cut(1, at_out),
            cut(RANK, at_out),
            cut(1, at_down),
            cut(RANK, at_down),
            cut(ff, at_down),
            pair_rows(2 * width),
            fixed(RANK, 2 * width),
            fixed(1, 2 * width),
            fixed(1, 2 * width),
            fixed(1, 2 * width),
            fixed(RANK, 2 * width),
        ],
        out_shape=[
            shape((1, wide), f32),
            shape((RANK, wide), f32),
            shape((1, wide), f32),
            shape((RANK, wide), f32),
            shape((ff, wide), bf16),
            shape((depth, 2 * width), bf16),
            shape((RANK, 2 * width), f32),
            shape((1, 2 * width), f32),
            shape((1, 2 * width), f32),
            shape((1, 2 * width), f32),
            shape((RANK, 2 * width), f32),
        ],
        compiler_params=pltpu.CompilerParams(vmem_limit_bytes=VMEM_LIMIT),
        cost_estimate=cost(4 * depth * width * RANK, 8 * depth * width),
        name="merge_others",
    )(*out, *down, gate[0], up[0], gate[1], up[1], gate[2], up[2], gate[3], up[3])


def heads_kernel(scalars, x_ref, gain_ref, a_ref, b_ref, m_ref, cos_ref, sin_ref,
                 wk_hbm, wv_hbm, wq_hbm, *refs):
    take = taker(refs)
    peers = len(refs) - 12
    blocks = take(peers)
    normed_ref, low_ref, raw_ref, column_ref, scale_ref, cross_ref = take(6)
    x_all, w_all, merged_all, column_now, scale_now, sem = take(6)
    step = pl.program_id(0)
    rows = x_ref.shape[0]
    sources = (wk_hbm, wv_hbm, wq_hbm)

    def copy(number):
        return pltpu.make_async_copy(sources[number], w_all.at[number], sem.at[number])

    def merge(layer):
        slot = lax.rem(layer, 2)
        merged = w_all[layer].astype(f32) + low_rank(a_ref[layer], b_ref[layer])
        low = merged.astype(bf16)
        merged_all[slot] = low
        low_ref[...] = low
        column = jnp.sqrt(jnp.sum(merged * merged, axis=0, keepdims=True))
        scale = m_ref[layer] / column
        column_ref[...] = column
        scale_ref[...] = scale
        scale_now[slot] = scale

    @pl.when(step == 0)
    def _():
        for number in range(3):
            copy(number).start()
        part = rows // 4
        for i in range(4):
            at = pl.ds(i * part, part)
            x = x_ref[at, :].astype(f32)
            inverse = lax.rsqrt(jnp.mean(x * x, axis=-1, keepdims=True) + EPS)
            normed = (x * inverse * gain_ref[...]).astype(bf16)
            x_all[at, :] = normed
            normed_ref[at, :] = normed
        x_all[rows:, :] = a_ref[0].astype(bf16)
        copy(0).wait()
        merge(0)

    for number in (1, 2):

        @pl.when(step == number)
        def _(number=number):
            copy(number).wait()

    @pl.when(step > 0)
    def _():
        layer = step - 1
        slot = lax.rem(layer, 2)
        product = dot(x_all[...], merged_all[slot])
        scale = scale_now[slot]
        x_next = a_ref[jnp.minimum(step, 2)].astype(bf16)
        merge(jnp.minimum(step, 2))
        cross_ref[...] = product[rows:, :]
        raw = product[:rows, :]
        raw_ref[...] = raw.astype(bf16)
        value = raw * scale
        for t in range(peers):
            head = value[:, t * HD : (t + 1) * HD]
            rotated = head * cos_ref[...] + pltpu.roll(head, HALF, 1) * sin_ref[...]
            head = jnp.where(layer != 1, rotated, head).astype(bf16)
            place = t ^ scalars[0]
            for d, block in enumerate(blocks):

                @pl.when(place == d)
                def _(block=block, head=head):
                    block[layer] = head

        x_all[rows:, :] = x_next


def project_heads(order, x, gain, weights, a_t, b, m, cosine, sine):
    rows, depth = x.shape
    width = weights[0].shape[1]
    heads = width // HD
    merged_at = lambda i, s: (0, jnp.minimum(i, 2))
    done_at = lambda i, s: (0, jnp.maximum(i - 1, 0))
    fixed = lambda *shape: pl.BlockSpec(shape, lambda i, s: (0,) * len(shape))
    out_shape = [jax.ShapeDtypeStruct((3, rows, HD), bf16)] * heads
    out_shape += [
        jax.ShapeDtypeStruct((rows, depth), bf16),
        jax.ShapeDtypeStruct((depth, 3 * width), bf16),
        jax.ShapeDtypeStruct((rows, 3 * width), bf16),
        jax.ShapeDtypeStruct((1, 3 * width), f32),
        jax.ShapeDtypeStruct((1, 3 * width), f32),
        jax.ShapeDtypeStruct((RANK, 3 * width), f32),
    ]
    outs = pl.pallas_call(
        heads_kernel,
        grid_spec=pltpu.PrefetchScalarGridSpec(
            num_scalar_prefetch=1,
            grid=(4,),
            in_specs=[
                fixed(rows, depth),
                fixed(1, depth),
                fixed(3, RANK, depth),
                fixed(3, RANK, width),
                fixed(3, 1, width),
                fixed(rows, HD),
                fixed(rows, HD),
            ]
            + [pl.BlockSpec(memory_space=pl.ANY)] * 3,
            out_specs=[fixed(3, rows, HD)] * heads
            + [
                fixed(rows, depth),
                pl.BlockSpec((depth, width), merged_at),
                pl.BlockSpec((rows, width), done_at),
                pl.BlockSpec((1, width), merged_at),
                pl.BlockSpec((1, width), merged_at),
                pl.BlockSpec((RANK, width), done_at),
            ],
            scratch_shapes=[
                pltpu.VMEM((rows + RANK, depth), bf16),
                pltpu.VMEM((3, depth, width), bf16),
                pltpu.VMEM((2, depth, width), bf16),
                pltpu.VMEM((2, 1, width), f32),
                pltpu.VMEM((2, 1, width), f32),
                pltpu.SemaphoreType.DMA((3,)),
            ],
        ),
        out_shape=out_shape,
        compiler_params=pltpu.CompilerParams(vmem_limit_bytes=VMEM_LIMIT),
        cost_estimate=cost(6 * rows * depth * width, 16 * rows * depth),
        name="project_heads",
    )(order, x, gain, a_t, b, m, cosine, sine, *weights)
    return outs[:heads], *outs[heads:]


def assemble_kernel(peers, chunks, scalars, *refs):
    take = taker(refs)
    heads = take(peers)
    out_ref, down_ref, a_ref = take(3)
    near_refs = refs[peers + 3 :]
    width = a_ref.shape[1]
    parts = out_ref.shape[1] // width
    part = heads[0].shape[0] // chunks
    for d in range(peers):
        at = pl.ds(pl.multiple_of((scalars[0] ^ d) * HD, HD), HD)
        for c in range(chunks):
            near_refs[c][:part, at] = heads[d][c * part : (c + 1) * part, :]
    rows = []
    for ref in (out_ref, down_ref):
        high = ref[...].astype(bf16).astype(f32)
        for value in (high, ref[...] - high):
            rows += [value[:, j * width : (j + 1) * width] for j in range(parts)]
    near_refs[0][part : part + RANK, :] = jnp.concatenate(rows, axis=0).astype(bf16)
    near_refs[0][part + RANK :, :] = a_ref[...].astype(bf16)


def assemble(order, heads, square_out, square_down, a_t, chunks):
    peers = len(heads)
    part = heads[0].shape[0] // chunks
    width = peers * HD
    operands = [*heads, square_out, square_down, a_t]
    heights = [part + 2 * RANK] + [part] * (chunks - 1)
    out_shape = [jax.ShapeDtypeStruct((height, width), bf16) for height in heights]
    return pl.pallas_call(
        functools.partial(assemble_kernel, peers, chunks),
        grid_spec=pltpu.PrefetchScalarGridSpec(
            num_scalar_prefetch=1,
            grid=(1,),
            in_specs=[whole_spec(x) for x in operands],
            out_specs=[whole_spec(x) for x in out_shape],
        ),
        out_shape=out_shape,
        compiler_params=pltpu.CompilerParams(vmem_limit_bytes=VMEM_LIMIT),
        cost_estimate=cost(0, 0),
        name="assemble",
    )(order, *operands)


def unpack_kernel(size, scalars, *refs):
    take = taker(refs)
    blocks, m_refs = take(size), take(2)
    column_refs, scale_refs, (a_ref,) = take(2), take(2), take(1)
    width = blocks[0].shape[1]
    total = jnp.zeros((RANK, width), f32)
    for device in range(size):
        value = blocks[0][:RANK, :]
        for c in range(1, size):
            here = lax.rem(scalars[0] + c, size) == device
            value = jnp.where(here, blocks[c][:RANK, :], value)
        total = total + value.astype(f32)
    for side in range(2):
        for j in range(size):
            row = 2 * side * size + j
            square = total[row : row + 1, :] + total[row + size : row + size + 1, :]
            at = slice(j * width, (j + 1) * width)
            column = jnp.sqrt(square)
            column_refs[side][:, at] = column
            scale_refs[side][:, at] = m_refs[side][:, at] / column
    for c in range(size):
        device = lax.rem(scalars[0] + c, size)
        at = pl.ds(pl.multiple_of(device * width, HD), width)
        a_ref[:, at] = blocks[c][RANK:, :]


def unpack(k, blocks, rows, m_out, m_down):
    size = len(blocks)
    width = blocks[0].shape[1]
    wide = size * width
    row = jax.ShapeDtypeStruct((1, wide), f32)
    out_shape = [row] * 4 + [jax.ShapeDtypeStruct((RANK, wide), bf16)]
    tail = pl.BlockSpec((2 * RANK, width), lambda i, s: (rows // (2 * RANK), 0))
    return pl.pallas_call(
        functools.partial(unpack_kernel, size),
        grid_spec=pltpu.PrefetchScalarGridSpec(
            num_scalar_prefetch=1,
            grid=(1,),
            in_specs=[tail] * size + [whole_spec(m_out), whole_spec(m_down)],
            out_specs=[whole_spec(x) for x in out_shape],
        ),
        out_shape=out_shape,
        compiler_params=pltpu.CompilerParams(vmem_limit_bytes=VMEM_LIMIT),
        cost_estimate=cost(0, 0),
        name="unpack",
    )(k, *blocks, m_out, m_down)


def out_kernel(scalars, *refs):
    take = taker(refs)
    size = len(refs) - 13
    x_refs = take(size)
    w_ref, a_ref, hid_ref, b_ref, scale_ref, gain_ref = take(6)
    hnorm_ref, resid_ref, raw_own_ref, low_ref, own_ref = take(5)
    total, through = take(2)
    step = pl.program_id(0)

    @pl.when(step == 0)
    def _():
        total[...] = jnp.zeros_like(total)
        through[...] = jnp.zeros_like(through)

    for c, x_ref in enumerate(x_refs):

        @pl.when(step == c)
        def _(x_ref=x_ref):
            x = x_ref[...]
            total[...] += dot(x, w_ref[...])
            through[...] += dot_nt(x, a_ref[...])
            part, width = own_ref.shape[0], x_ref.shape[1]
            mine = pl.ds(pl.multiple_of(scalars[0] * part, 16), part)
            device = lax.rem(scalars[0] + c, size)
            at = pl.ds(pl.multiple_of(device * width, HD), width)
            own_ref[:, at] = x_ref[mine, :]

    @pl.when(step == size - 1)
    def _():
        part = hid_ref.shape[2]
        for piece in range(size):
            at = pl.ds(piece * part, part)
            low = through[at, :].astype(bf16)
            raw = total[at, :] + dot(low, b_ref[...])
            resid = hid_ref[piece, 0].astype(f32) + raw * scale_ref[...]
            inverse = lax.rsqrt(jnp.mean(resid * resid, axis=-1, keepdims=True) + EPS)
            hnorm_ref[at, :] = (resid * inverse * gain_ref[...]).astype(bf16)

            @pl.when(scalars[0] == piece)
            def _(resid=resid, raw=raw, low=low):
                resid_ref[...] = resid
                raw_own_ref[...] = raw
                low_ref[...] = low


def out_project(k, chunk, x, w, a_t, hidden, b2, scale, gain):
    size = len(x)
    width, wide = x[0].shape[1], w.shape[1]
    part = hidden.shape[2]
    rows = size * part
    fixed = lambda *shape: pl.BlockSpec(shape, lambda i, s: (0,) * len(shape))
    return pl.pallas_call(
        out_kernel,
        grid_spec=pltpu.PrefetchScalarGridSpec(
            num_scalar_prefetch=1,
            grid=(size,),
            in_specs=[fixed(rows, width)] * size
            + [
                pl.BlockSpec((width, wide), lambda i, s: (lax.rem(i + s[0], size), 0)),
                pl.BlockSpec((RANK, width), lambda i, s: (0, lax.rem(i + s[0], size))),
                pl.BlockSpec((size, 1, part, wide), lambda i, s: (0, chunk, 0, 0)),
                fixed(RANK, wide),
                fixed(1, wide),
                fixed(1, wide),
            ],
            out_specs=[
                fixed(rows, wide),
                fixed(part, wide),
                fixed(part, wide),
                fixed(part, RANK),
                fixed(part, size * width),
            ],
            scratch_shapes=[
                pltpu.VMEM((rows, wide), f32),
                pltpu.VMEM((rows, RANK), f32),
            ],
        ),
        out_shape=[
            jax.ShapeDtypeStruct((rows, wide), bf16),
            jax.ShapeDtypeStruct((part, wide), f32),
            jax.ShapeDtypeStruct((part, wide), f32),
            jax.ShapeDtypeStruct((part, RANK), bf16),
            jax.ShapeDtypeStruct((part, size * width), bf16),
        ],
        compiler_params=pltpu.CompilerParams(vmem_limit_bytes=VMEM_LIMIT),
        cost_estimate=cost(2 * rows * width * size * wide, 2 * width * size * wide),
        name="out_project",
    )(k, *x, w, a_t, hidden, b2, scale, gain)


def hidden_kernel(sizes, hnorm_ref, cot_ref, down_scale_ref, scale_ref, w_hbm, wd_hbm,
                  act_ref, dz_ref, g_ref, dh_ref, total, w_all, wd_all, dz_down, sem, down_sem):
    rows = hnorm_ref.shape[0]
    starts = [sum(sizes[:j]) for j in range(len(sizes))]

    def copies(j):
        both = pl.ds(2 * starts[j], 2 * sizes[j])
        one = pl.ds(starts[j], sizes[j])
        return (
            pltpu.make_async_copy(wd_hbm.at[one, :], wd_all.at[one, :], down_sem.at[j]),
            pltpu.make_async_copy(w_hbm.at[:, both], w_all.at[:, both], sem.at[j]),
        )

    for j in range(len(sizes)):
        for copy in copies(j):
            copy.start()
    part = rows // cot_ref.shape[0]
    for i in range(cot_ref.shape[0]):
        cot = cot_ref[i, 0].astype(f32)
        dz_down[i * part : (i + 1) * part, :] = (cot * down_scale_ref[...]).astype(bf16)

    def products(j):
        for copy in copies(j):
            copy.wait()
        both = slice(2 * starts[j], 2 * (starts[j] + sizes[j]))
        one = slice(starts[j], starts[j] + sizes[j])
        return dot(hnorm_ref[...], w_all[:, both]), dot_nt(dz_down[...], wd_all[one, :])

    ready = products(0)
    for j in range(len(sizes)):
        v, dact_all = ready
        if j + 1 < len(sizes):
            ready = products(j + 1)
        for i in range(sizes[j] // HD):
            hidden = starts[j] + i * HD
            gate_at = slice(2 * hidden, 2 * hidden + HD)
            up_at = slice(2 * hidden + HD, 2 * hidden + 2 * HD)
            raw_gate = v[:, 2 * i * HD : (2 * i + 1) * HD]
            raw_up = v[:, (2 * i + 1) * HD : (2 * i + 2) * HD]
            dact = dact_all[:, i * HD : (i + 1) * HD]
            scale_gate, scale_up = scale_ref[:, gate_at], scale_ref[:, up_at]
            gate = raw_gate * scale_gate
            up = raw_up * scale_up
            sigmoid = 1.0 / (1.0 + jnp.exp(-gate))
            silu = gate * sigmoid
            dgate = dact * up * (sigmoid + silu * (1.0 - sigmoid))
            dup = dact * silu
            act_ref[:, hidden : hidden + HD] = (silu * up).astype(bf16)
            g_ref[:, gate_at] = jnp.sum(dgate * raw_gate, axis=0, keepdims=True)
            g_ref[:, up_at] = jnp.sum(dup * raw_up, axis=0, keepdims=True)
            dz_ref[:, gate_at] = (dgate * scale_gate).astype(bf16)
            dz_ref[:, up_at] = (dup * scale_up).astype(bf16)
        both = slice(2 * starts[j], 2 * (starts[j] + sizes[j]))
        product = dot_nt(dz_ref[:, both], w_all[:, both])
        if j == 0:
            total[...] = product
        elif j + 1 < len(sizes):
            total[...] += product
        else:
            dh_ref[...] = (total[...] + product).astype(bf16)


def feed_forward(chunk, hnorm, cotangent, down_scale, scale, w, wd):
    rows, depth = hnorm.shape
    ff = wd.shape[0]
    size, _, part, _ = cotangent.shape
    sizes = [2 * HD] * (ff // (2 * HD)) + [HD] * (ff // HD % 2)
    fixed = lambda *shape: pl.BlockSpec(shape, lambda i: (0,) * len(shape))
    return pl.pallas_call(
        functools.partial(hidden_kernel, sizes),
        grid=(1,),
        in_specs=[
            fixed(rows, depth),
            pl.BlockSpec((size, 1, part, depth), lambda i: (0, chunk, 0, 0)),
            fixed(1, depth),
            fixed(1, 2 * ff),
            pl.BlockSpec(memory_space=pl.ANY),
            pl.BlockSpec(memory_space=pl.ANY),
        ],
        out_specs=[fixed(rows, ff), fixed(rows, 2 * ff), fixed(1, 2 * ff), fixed(rows, depth)],
        out_shape=[
            jax.ShapeDtypeStruct((rows, ff), bf16),
            jax.ShapeDtypeStruct((rows, 2 * ff), bf16),
            jax.ShapeDtypeStruct((1, 2 * ff), f32),
            jax.ShapeDtypeStruct((rows, depth), bf16),
        ],
        scratch_shapes=[
            pltpu.VMEM((rows, depth), f32),
            pltpu.VMEM((depth, 2 * ff), bf16),
            pltpu.VMEM((ff, depth), bf16),
            pltpu.VMEM((rows, depth), bf16),
            pltpu.SemaphoreType.DMA((len(sizes),)),
            pltpu.SemaphoreType.DMA((len(sizes),)),
        ],
        compiler_params=pltpu.CompilerParams(vmem_limit_bytes=VMEM_LIMIT),
        cost_estimate=cost(10 * rows * depth * ff, 6 * depth * ff),
        name="feed_forward",
    )(hnorm, cotangent, down_scale, scale, w, wd)


def back_out_kernel(scalars, *refs):
    take = taker(refs)
    earlier = take(len(refs) - 18)
    piece_ref, cot_ref, resid_ref, raw_ref, gain_ref, scale_ref = take(6)
    b_ref, own_ref, low_ref, w_ref, a_ref = take(5)
    dattn_ref, dresid_ref, dz_ref, g_ref, ap_ref, pb_ref = take(6)
    (through,) = take(1)

    @pl.when(pl.program_id(0) == 0)
    def _():
        grad = piece_ref[...].astype(f32)
        resid = resid_ref[...]
        inverse = lax.rsqrt(jnp.mean(resid * resid, axis=-1, keepdims=True) + EPS)
        scaled = grad * gain_ref[...]
        lean = jnp.mean(resid * scaled, axis=-1, keepdims=True)
        dresid = cot_ref[0, 0].astype(f32) + inverse * scaled
        dresid = dresid - resid * (inverse * inverse * inverse * lean)
        dresid_ref[...] = dresid
        dz = (dresid * scale_ref[...]).astype(bf16)
        dz_ref[...] = dz
        through[...] = dot_nt(dz, b_ref[...]).astype(bf16)
        sums = [
            jnp.sum(dresid * raw_ref[...], axis=0, keepdims=True),
            dot_tn(low_ref[...], dz),
            dot_tn(through[...], own_ref[...]),
        ]
        for i, ref in enumerate((g_ref, ap_ref, pb_ref)):
            ref[...] = sums[i] + earlier[i][...] if earlier else sums[i]

    dattn = dot_nt(dz_ref[...], w_ref[...]) + dot(through[...], a_ref[...])
    dattn_ref[0] = dattn.astype(bf16)


def back_out(k, chunk, piece, cotangent, resid, raw, gain, scale, b, own, low, w, a2_t, earlier):
    size = cotangent.shape[0]
    part, wide = resid.shape
    width = w.shape[0] // size
    fixed = lambda *shape: pl.BlockSpec(shape, lambda i, s: (0,) * len(shape))
    return pl.pallas_call(
        back_out_kernel,
        grid_spec=pltpu.PrefetchScalarGridSpec(
            num_scalar_prefetch=1,
            grid=(size,),
            in_specs=[fixed(*x.shape) for x in earlier]
            + [
                fixed(part, wide),
                pl.BlockSpec((1, 1, part, wide), lambda i, s: (s[0], chunk, 0, 0)),
                fixed(part, wide),
                fixed(part, wide),
                fixed(1, wide),
                fixed(1, wide),
                fixed(RANK, wide),
                fixed(*own.shape),
                fixed(part, RANK),
                pl.BlockSpec((width, wide), lambda i, s: (lax.rem(i + s[0], size), 0)),
                pl.BlockSpec((RANK, width), lambda i, s: (0, lax.rem(i + s[0], size))),
            ],
            out_specs=[
                pl.BlockSpec((1, part, width), lambda i, s: (i, 0, 0)),
                fixed(part, wide),
                fixed(part, wide),
                fixed(1, wide),
                fixed(RANK, wide),
                fixed(RANK, size * width),
            ],
            scratch_shapes=[pltpu.VMEM((part, RANK), bf16)],
        ),
        out_shape=[
            jax.ShapeDtypeStruct((size, part, width), bf16),
            jax.ShapeDtypeStruct((part, wide), f32),
            jax.ShapeDtypeStruct((part, wide), bf16),
            jax.ShapeDtypeStruct((1, wide), f32),
            jax.ShapeDtypeStruct((RANK, wide), f32),
            jax.ShapeDtypeStruct((RANK, size * width), f32),
        ],
        compiler_params=pltpu.CompilerParams(vmem_limit_bytes=VMEM_LIMIT),
        cost_estimate=cost(2 * part * width * size * wide, 2 * width * size * wide),
        name="back_out",
    )(k, *earlier, piece, cotangent, resid, raw, gain, scale, b, own, low, w, a2_t)


def unproject_kernel(heads, scalars, cos_ref, sin_ref, raw_ref, scale_ref, w_ref, *refs):
    take = taker(refs)
    grads = take(heads)
    dz_ref, g_ref, out_ref = refs[heads:]
    width = heads * HD

    @pl.when(pl.program_id(0) == 0)
    def _():
        for layer in range(3):
            for d in range(heads):
                at = pl.ds(pl.multiple_of(layer * width + (scalars[0] ^ d) * HD, HD), HD)
                grad = grads[d][layer].astype(f32)
                if layer != 1:
                    grad = grad * cos_ref[...] - pltpu.roll(grad, HALF, 1) * sin_ref[...]
                raw = raw_ref[:, at].astype(f32)
                g_ref[:, at] = jnp.sum(grad * raw, axis=0, keepdims=True)
                dz_ref[:, at] = (grad * scale_ref[:, at]).astype(bf16)

    out_ref[...] = dot_nt(dz_ref[...], w_ref[...]).astype(bf16)


def unproject(order, cosine, sine, raw, scale, w, grads):
    operands = [cosine, sine, raw, scale]
    rows, wide = raw.shape
    depth = w.shape[0]
    step = 2 * HD
    return pl.pallas_call(
        functools.partial(unproject_kernel, len(grads)),
        grid_spec=pltpu.PrefetchScalarGridSpec(
            num_scalar_prefetch=1,
            grid=(depth // step,),
            in_specs=[whole_spec(x) for x in operands]
            + [pl.BlockSpec((step, wide), lambda i, s: (i, 0))]
            + [whole_spec(x) for x in grads],
            out_specs=[
                whole_spec(raw),
                whole_spec(scale),
                pl.BlockSpec((rows, step), lambda i, s: (0, i)),
            ],
        ),
        out_shape=[
            jax.ShapeDtypeStruct(raw.shape, bf16),
            jax.ShapeDtypeStruct(scale.shape, f32),
            jax.ShapeDtypeStruct((rows, depth), bf16),
        ],
        compiler_params=pltpu.CompilerParams(vmem_limit_bytes=VMEM_LIMIT),
        cost_estimate=cost(2 * rows * wide * depth, 2 * wide * depth),
        name="unproject",
    )(order, *operands, w, *grads)


def shares_kernel(count, chunks, span, *refs):
    take = taker(refs)
    x_refs, dz_refs = take(chunks), take(chunks)
    a_ref, b_ref, w_ref, cross_ref, g_ref, m_ref, column_ref = take(7)
    share_a_ref, share_b_ref = take(2)
    low, up, radial = take(3)
    step = pl.program_id(0)
    wide = b_ref.shape[1]

    @pl.when(step == 0)
    def _():
        up[...] = jnp.zeros_like(up)
        radial[...] = jnp.zeros_like(radial)
        for c in range(chunks):
            low[c] = dot_nt(x_refs[c][...], a_ref[...]).astype(bf16)

    shrink = g_ref[...] * m_ref[...] / (column_ref[...] * column_ref[...] * column_ref[...])
    shape = (count * RANK, wide)
    column = lax.broadcasted_iota(jnp.int32, shape, 1) + step * wide
    layer_of = lax.rem(column // span, count)
    own = (lax.broadcasted_iota(jnp.int32, shape, 0) // RANK) == layer_of
    b_pad = jnp.where(own, jnp.concatenate([b_ref[...]] * count, axis=0), 0.0)
    b_low = b_pad.astype(bf16)
    ap = jnp.zeros(shape, f32)
    for c in range(chunks):
        dz = dz_refs[c][...]
        up[c] += dot_nt(dz, b_low)
        ap += dot_tn(low[c], dz)
    radial[...] += dot_nt((b_pad * shrink).astype(bf16), w_ref[...])
    ap = jnp.where(own, ap, 0.0)
    picked = ap[:RANK]
    for i in range(1, count):
        picked = picked + ap[i * RANK : (i + 1) * RANK]
    share_b_ref[...] = (SCALING * (picked - cross_ref[...] * shrink)).astype(bf16)

    @pl.when(step == pl.num_programs(0) - 1)
    def _():
        total = -radial[...]
        for c in range(chunks):
            total = total + dot_tn(up[c].astype(bf16), x_refs[c][...])
        share_a_ref[...] = (SCALING * total).astype(bf16)


def layer_shares(inputs, a_t, dz, b, span, merged, cross, g, magnitude, column):
    chunks = len(inputs)
    rows, depth = inputs[0].shape
    width = dz[0].shape[1]
    count = a_t.shape[0] // RANK
    step = 2 * HD
    columns = lambda height: pl.BlockSpec((height, step), lambda i: (0, i))
    fixed = lambda x: pl.BlockSpec(x.shape, lambda i: (0, 0))
    return pl.pallas_call(
        functools.partial(shares_kernel, count, chunks, span),
        grid=(width // step,),
        in_specs=[fixed(x) for x in inputs]
        + [columns(rows)] * chunks
        + [fixed(a_t), columns(RANK), columns(depth), columns(RANK)]
        + [columns(1)] * 3,
        out_specs=[fixed(a_t), columns(RANK)],
        out_shape=[
            jax.ShapeDtypeStruct(a_t.shape, bf16),
            jax.ShapeDtypeStruct((RANK, width), bf16),
        ],
        scratch_shapes=[
            pltpu.VMEM((chunks, rows, count * RANK), bf16),
            pltpu.VMEM((chunks, rows, count * RANK), f32),
            pltpu.VMEM(a_t.shape, f32),
        ],
        compiler_params=pltpu.CompilerParams(vmem_limit_bytes=VMEM_LIMIT),
        cost_estimate=cost(rows * depth * 64, depth * width),
        name="shares",
    )(*inputs, *dz, a_t.astype(bf16), b, merged, cross, g, magnitude, column)


def down_kernel(chunks, *refs):
    take = taker(refs)
    act_refs = take(chunks)
    w_ref, cot_ref, scale_ref, a_ref, b_ref = take(5)
    raw_ref, g_ref, ap_ref, pb_ref = take(4)
    low, up = take(2)
    step = pl.program_id(0)
    rows = act_refs[0].shape[0]
    size, _, part, wide = cot_ref.shape

    @pl.when(step == 0)
    def _():
        up[...] = jnp.zeros_like(up)
        for c in range(chunks):
            low[c] = dot_nt(act_refs[c][...], a_ref[...]).astype(bf16)

    g = jnp.zeros((1, wide), f32)
    ap = jnp.zeros((RANK, wide), f32)
    b_low = b_ref[...].astype(bf16)
    for c in range(chunks):
        raw = dot(act_refs[c][...], w_ref[...])
        raw_ref[:, c] = raw.astype(bf16).reshape(size, part, wide)
        cot = cot_ref[:, c].reshape(rows, wide).astype(f32)
        g += jnp.sum(cot * raw, axis=0, keepdims=True)
        dz = (cot * scale_ref[...]).astype(bf16)
        up[c] += dot_nt(dz, b_low)
        ap += dot_tn(low[c], dz)
    g_ref[...] = g
    ap_ref[...] = ap.astype(bf16)

    @pl.when(step == pl.num_programs(0) - 1)
    def _():
        total = jnp.zeros(pb_ref.shape, f32)
        for c in range(chunks):
            total = total + dot_tn(up[c].astype(bf16), act_refs[c][...])
        pb_ref[...] = total.astype(bf16)


def down_project(acts, w, cotangent, scale, a_t, b):
    chunks = len(acts)
    rows, ff = acts[0].shape
    wide = w.shape[1]
    step = 2 * HD
    size, _, part, _ = cotangent.shape
    columns = lambda height: pl.BlockSpec((height, step), lambda i: (0, i))
    fixed = lambda *shape: pl.BlockSpec(shape, lambda i: (0,) * len(shape))
    view = pl.BlockSpec((size, chunks, part, step), lambda i: (0, 0, 0, i))
    return pl.pallas_call(
        functools.partial(down_kernel, chunks),
        grid=(wide // step,),
        in_specs=[fixed(rows, ff)] * chunks
        + [columns(ff), view, columns(1), fixed(RANK, ff), columns(RANK)],
        out_specs=[view, columns(1), columns(RANK), fixed(RANK, ff)],
        out_shape=[
            jax.ShapeDtypeStruct(cotangent.shape, bf16),
            jax.ShapeDtypeStruct((1, wide), f32),
            jax.ShapeDtypeStruct((RANK, wide), bf16),
            jax.ShapeDtypeStruct((RANK, ff), bf16),
        ],
        scratch_shapes=[
            pltpu.VMEM((chunks, rows, RANK), bf16),
            pltpu.VMEM((chunks, rows, RANK), f32),
        ],
        compiler_params=pltpu.CompilerParams(vmem_limit_bytes=VMEM_LIMIT),
        cost_estimate=cost(2 * chunks * rows * ff * wide, 2 * ff * wide),
        name="down_project",
    )(*acts, w, cotangent, scale, a_t.astype(bf16), b)


def pack_kernel(plan, scalars, *refs):
    out_ref = refs[-1]
    out_ref[...] = jnp.zeros_like(out_ref)
    row = 0
    for ref, (parts, placed) in zip(refs[:-1], plan):
        height, width = ref.shape
        wide = width // parts
        short = -height % RANK
        lanes = slice(0, wide)
        if placed:
            lanes = pl.ds(pl.multiple_of(scalars[0] * wide, HD), wide)
        if height == 1:
            value = [ref[:, i * wide : (i + 1) * wide].astype(f32) for i in range(parts)]
            value.append(jnp.zeros((RANK - parts, wide), f32))
            out_ref[row : row + RANK, lanes] = jnp.concatenate(value, axis=0).astype(bf16)
            row += RANK
        else:
            for i in range(parts):
                value = ref[:, i * wide : (i + 1) * wide].astype(bf16)
                out_ref[row : row + height, lanes] = value
                row += height


def pack(k, height, width, *entries):
    arrays = [x for x, _, _ in entries]
    plan = [(parts, placed) for _, parts, placed in entries]
    return pl.pallas_call(
        functools.partial(pack_kernel, plan),
        grid_spec=pltpu.PrefetchScalarGridSpec(
            num_scalar_prefetch=1,
            grid=(1,),
            in_specs=[whole_spec(x) for x in arrays],
            out_specs=pl.BlockSpec((height, width), lambda i, s: (0, 0)),
        ),
        out_shape=jax.ShapeDtypeStruct((height, width), bf16),
        compiler_params=pltpu.CompilerParams(vmem_limit_bytes=VMEM_LIMIT),
        cost_estimate=cost(height * width, 4 * height * width),
        name="pack",
    )(k, *arrays)


def span_positions(row_ids, span_order, span_len):
    slot_ids = row_ids // span_len
    slot_table = jnp.arange(span_order.shape[0], dtype=jnp.int32)
    picked = jnp.sum(
        jnp.where(slot_ids[:, None] == slot_table[None, :], span_order[None, :], 0), axis=1
    )
    return picked * span_len + row_ids % span_len


def rotary_tables(positions):
    lane = np.arange(HD)
    frequency = (ROPE_BASE ** (-2.0 * (lane % HALF) / HD)).astype(np.float32)
    sign = np.where(lane < HALF, -1.0, 1.0).astype(np.float32)
    angles = positions.astype(f32)[:, None] * frequency[None, :]
    return jnp.cos(angles), jnp.sin(angles) * sign[None, :]


def pick_blocks(blocks, index):
    out = blocks[0]
    for i in range(1, len(blocks)):
        out = jnp.where(index == i, blocks[i], out)
    return out


def inverse_rms(values):
    return lax.rsqrt(jnp.mean(values * values, axis=-1, keepdims=True) + EPS)


def rms_backward(values, gain_vec, grad_in):
    inverse = inverse_rms(values)
    scaled = grad_in * gain_vec
    return inverse * scaled - values * inverse * inverse * inverse * jnp.mean(
        values * scaled, axis=-1, keepdims=True
    )


def per_device(
    hidden_in,
    cotangent,
    segment_ids,
    padding,
    span_order,
    gain_attn,
    gain_mlp,
    w_query,
    w_key,
    w_value,
    w_out,
    w_gate,
    w_up,
    w_down,
    a_query,
    b_query,
    m_query,
    a_key,
    b_key,
    m_key,
    a_value,
    b_value,
    m_value,
    a_out,
    b_out,
    m_out,
    a_gate,
    b_gate,
    m_gate,
    a_up,
    b_up,
    m_up,
    a_down,
    b_down,
    m_down,
):
    rows, width = hidden_in.shape
    span_len = rows // 2
    near_width = w_query.shape[1]
    peers = near_width // HD
    n_mp = lax.axis_size("mp")
    n_seq = lax.axis_size("seq")
    n_doc = lax.axis_size("doc")
    groups = n_seq // peers
    copies = n_seq * n_doc
    share = rows // n_mp
    chunks = CHUNKS
    part = share // chunks
    k = lax.axis_index("mp")
    doc = lax.axis_index("doc")
    seq = lax.axis_index("seq")
    me = lax.rem(seq, peers)
    my_group = seq // peers
    order = jnp.reshape(me, (1,)).astype(jnp.int32)
    k_scalar = jnp.reshape(k, (1,)).astype(jnp.int32)

    slice_rows = near_width // n_doc
    wo_slice = lax.dynamic_slice_in_dim(w_out, doc * slice_rows, slice_rows, 0)
    wo_all = lax.all_gather(wo_slice, ("mp", "doc"), axis=0, tiled=True)

    slots = [
        2 * (my_group * peers + (me ^ d)) + half for d in range(peers) for half in range(2)
    ]
    slots += [
        2 * (g * peers + (me ^ d)) + half
        for g in range(groups)
        for d in range(peers)
        for half in range(2)
    ]
    slots = jnp.stack(slots)
    table = jnp.arange(span_order.shape[0], dtype=jnp.int32)
    places = jnp.sum(jnp.where(slots[:, None] == table[None, :], span_order[None, :], 0), axis=1)
    scalars = jnp.concatenate([places, k_scalar]).astype(jnp.int32)
    row_ids = jnp.arange(rows, dtype=jnp.int32) + seq * rows
    cosine, sine = rotary_tables(span_positions(row_ids, span_order, span_len))
    codes = seq_exchange([segment_ids * 2 + padding] * peers)
    (hidden_next,) = after([hidden_in], *codes)

    a_heads = jnp.stack([a_key.T, a_value.T, a_query.T])
    b_heads = [b_key, b_value, b_query]
    m_heads = jnp.concatenate([m_key, m_value, m_query])[None, :]
    blocks, normed, wh_low, raw_heads, column_heads, scale_heads, cross_heads = project_heads(
        order,
        hidden_next,
        gain_attn[None, :],
        (w_key, w_value, w_query),
        a_heads,
        jnp.stack(b_heads),
        jnp.stack([m_key, m_value, m_query])[:, None, :],
        cosine,
        sine,
    )
    heads = seq_exchange(blocks)

    codes = [x.reshape(rows, 1) for x in codes]
    w_out_next, w_down_next, w_gate_next, w_up_next = after(
        [w_out, w_down, w_gate, w_up], raw_heads
    )
    (
        square_out,
        cross_out,
        square_down,
        cross_down,
        wd_low,
        wgu_low,
        cross_gu,
        column_gu,
        scale_gu,
        m_gu,
        b_gu,
    ) = merge_others(
        (w_out_next, a_out.T, b_out),
        (w_down_next, a_down.T, b_down),
        (w_gate_next, a_gate.T, b_gate, m_gate[None, :]),
        (w_up_next, a_up.T, b_up, m_up[None, :]),
    )

    extra = []
    if groups > 1:
        members = [[g * peers + i for g in range(groups)] for i in range(peers)]
        gather = lambda x: lax.all_gather(
            x[None], "seq", axis=0, tiled=True, axis_index_groups=members
        )
        extra = [gather(jnp.stack([x[:2] for x in heads])), gather(jnp.stack(codes))]
    heads_next = after(heads, square_out)
    o_blocks, lse = attention_forward(
        scalars, heads_next, codes, extra, groups, n_mp, chunks
    )
    o_heads = seq_exchange(o_blocks)
    near_chunks = assemble(order, o_heads, square_out, square_down, a_out.T, chunks)

    def chunked(values):
        return values.reshape(n_mp, chunks, part, values.shape[-1])

    hid_view, cot_view = chunked(hidden_in), chunked(cotangent)
    b_out_low = b_out.astype(bf16)
    acts, hnorms, dz_gus, dh_chunks = [], [], [], []
    resid_own, raw_out_own, out_low_own, near_own = [], [], [], []
    g_gu = 0.0
    lines = ([near_chunks[0]], [near_chunks[0]])
    for step in range(1, n_mp):
        line_step(*lines, step)
    gathered_chunks = [line_blocks(*lines)]
    for c in range(1, chunks):
        (near_next,) = after([near_chunks[c]], *gathered_chunks[0])
        others = lax.all_gather(near_next, "mp", axis=0)
        gathered_chunks.append(
            [near_chunks[c]]
            + [
                lax.dynamic_index_in_dim(others, lax.rem(k + i, n_mp), 0, keepdims=False)
                for i in range(1, n_mp)
            ]
        )
    column_out, column_down, scale_out, scale_down, a_out_low = unpack(
        k_scalar, gathered_chunks[0], n_mp * part, m_out[None, :], m_down[None, :]
    )
    a_out_twice = SCALING * a_out_low
    for c in range(chunks):
        gathered = gathered_chunks[c]
        if c > 0:
            gathered = after(gathered, dh_chunks[-1])
        hnorm, resid, raw_out, out_low, own = out_project(
            k_scalar,
            c,
            gathered,
            wo_all,
            a_out_low,
            hid_view,
            (SCALING * b_out).astype(bf16),
            scale_out,
            gain_mlp[None, :],
        )
        act, dz_gu, g, dh = feed_forward(
            c, hnorm, cot_view, scale_down, scale_gu, wgu_low, wd_low
        )
        g_gu = g_gu + g
        dh_chunks.append(dh)
        acts.append(act)
        hnorms.append(hnorm)
        dz_gus.append(dz_gu)
        resid_own.append(resid)
        raw_out_own.append(raw_out)
        out_low_own.append(out_low)
        near_own.append(own)

    def scatter(parts):
        return lax.psum_scatter(parts, "mp", scatter_dimension=0, tiled=True)

    pieces = [scatter(x) for x in dh_chunks]

    arrived, dresid_own, dz_out = [], [], []
    out_sums = ()
    earlier = dh_chunks[-1]
    for c in range(chunks):
        (own_piece,) = after([pieces[c]], earlier)
        dattn, dresid, dz, *out_sums = back_out(
            k_scalar,
            c,
            own_piece,
            cot_view,
            resid_own[c],
            raw_out_own[c],
            gain_mlp[None, :],
            scale_out,
            b_out_low,
            near_own[c],
            out_low_own[c],
            wo_all,
            a_out_twice,
            out_sums,
        )
        arrived.append(dattn[0])
        for shift in range(1, n_mp):
            pairs = [(i, (i + shift) % n_mp) for i in range(n_mp)]
            arrived.append(lax.ppermute(dattn[shift], "mp", pairs))
        dresid_own.append(dresid)
        dz_out.append(dz)
        earlier = dz
        if c == 0:
            acts_next = after(acts, dz)
            raw_down, g_down, ap_down, pb_down = down_project(
                acts_next, wd_low, cot_view, scale_down, a_down.T, b_down
            )
            earlier = (g_down, *arrived[1:])
    arrived = jnp.concatenate(arrived, axis=0)
    by_head = [arrived[:, h * HD : (h + 1) * HD] for h in range(peers)]
    grad_blocks = seq_exchange([pick_blocks(by_head, me ^ d) for d in range(peers)])
    dresid_own = jnp.concatenate(dresid_own, axis=0)
    g_out, ap_out, pb_out = out_sums

    grads, dkv = attention_backward(
        scalars, heads_next, codes, extra, o_blocks, grad_blocks, lse, groups, n_mp, chunks
    )
    if groups > 1:
        members = [[g * peers + i for g in range(groups)] for i in range(peers)]
        dkv = lax.psum_scatter(
            dkv, "seq", scatter_dimension=0, tiled=True, axis_index_groups=members
        )
        grads = [jnp.concatenate([dkv[0, d], grads[d]], axis=0) for d in range(peers)]
    head_grads = seq_exchange(grads)

    hnorms_next, dz_gus_next = after([tuple(hnorms), tuple(dz_gus)], grads[0])
    share_a_gu, share_b_gu = layer_shares(
        hnorms_next,
        jnp.concatenate([a_gate.T, a_up.T], axis=0),
        dz_gus_next,
        b_gu,
        HD,
        wgu_low,
        cross_gu,
        g_gu,
        m_gu,
        column_gu,
    )
    (raw_down,) = after([raw_down], *grad_blocks)
    down_own = scatter(raw_down.reshape(rows, width))
    head_grads = after(head_grads, share_a_gu)

    dz_heads, g_heads, dnormed = unproject(
        order, cosine, sine, raw_heads, scale_heads, wh_low, head_grads
    )
    dnormed_own = scatter(dnormed)

    (down_own,) = after([down_own], dnormed)
    result = jnp.concatenate(resid_own, axis=0) + down_own.astype(f32) * scale_down
    hidden_own = lax.dynamic_slice_in_dim(hidden_in, k * share, share, 0).astype(f32)

    early_rows = pack(
        k_scalar,
        48,
        share_b_gu.shape[1],
        (share_b_gu, 1, False),
        (pb_down, 1, False),
        (g_gu, 1, False),
    )
    (early_rows,) = after([early_rows], dnormed)
    early_rows = doc_join(butterfly(doc_halve(early_rows), ["seq"])).astype(f32)

    share_a_heads, share_b_heads = layer_shares(
        [normed],
        a_heads.reshape(3 * RANK, width),
        [dz_heads],
        jnp.concatenate(b_heads, axis=1),
        near_width,
        wh_low,
        cross_heads,
        g_heads,
        m_heads,
        column_heads,
    )
    late = pack(
        k_scalar,
        256,
        width,
        (share_a_gu, 1, False),
        (ap_down, 1, False),
        (cross_out / copies, 1, False),
        (cross_down / copies, 1, False),
        (ap_out, 1, False),
        (jnp.concatenate([g_down, g_out], axis=1), 2, False),
        (pb_out, 1, False),
        (share_a_heads, 1, False),
        (share_b_heads, 3, True),
        (g_heads, 3, True),
    )
    late = spread_join(spread_sum(doc_halve(late), peers, ["mp"]), peers)
    (late,) = after([late], dnormed_own)
    late = doc_join(late).astype(f32)
    early, late = late[:128], late[128:]
    late_columns = late[3 * RANK : 7 * RANK]
    late_own = lax.dynamic_slice_in_dim(late_columns, k * near_width, near_width, 1)

    grad_input = dresid_own + rms_backward(
        hidden_own, gain_attn, dnormed_own.astype(f32)
    )

    def rank_rows(array, index):
        return array[index * RANK : (index + 1) * RANK]

    ff = w_gate.shape[1]
    total_g_down, total_g_out = early[96:97], early[97:98]
    shrink_out = total_g_out * m_out / (column_out * column_out * column_out)
    shrink_down = total_g_down * m_down / (column_down * column_down * column_down)
    turned_out = (b_out * shrink_out).astype(bf16)
    radial_out = dot_nt(turned_out, w_out) + SCALING * dot(
        dot_nt(turned_out, b_out.astype(bf16)), a_out.T
    )
    radial_down = dot_nt((b_down * shrink_down).astype(bf16), wd_low)
    pb_out = lax.dynamic_slice_in_dim(early[112:128], k * near_width, near_width, 1)
    grad_a_out = SCALING * (pb_out - radial_out)
    grad_a_down = SCALING * (early_rows[16:32, :ff] - radial_down)
    grad_b_out = SCALING * (rank_rows(early, 5) - rank_rows(early, 3) * shrink_out)
    grad_b_down = SCALING * (rank_rows(early, 2) - rank_rows(early, 4) * shrink_down)

    g_rows = late_own[3 * RANK : 3 * RANK + 3].reshape(1, -1) / column_heads
    g_rows = [g_rows[0, i * near_width : (i + 1) * near_width] for i in range(3)]
    grad_m_gate, grad_m_up = separate(early_rows[32:33] / column_gu)
    grad_b_gate, grad_b_up = separate(early_rows[:16])
    return (
        result,
        grad_input,
        rank_rows(late, 2).T,
        rank_rows(late_own, 2),
        g_rows[2],
        rank_rows(late, 0).T,
        rank_rows(late_own, 0),
        g_rows[0],
        rank_rows(late, 1).T,
        rank_rows(late_own, 1),
        g_rows[1],
        grad_a_out.T,
        grad_b_out,
        (total_g_out / column_out)[0],
        rank_rows(early, 0).T,
        grad_b_gate,
        grad_m_gate[0],
        rank_rows(early, 1).T,
        grad_b_up,
        grad_m_up[0],
        grad_a_down.T,
        grad_b_down,
        (total_g_down / column_down)[0],
    )


def solution(mesh):
    rows = P(("doc", "seq"))
    split_columns = (P(None, "mp"), P(None, "mp"))
    column_layer = (P(), P(None, "mp"), P("mp"))
    row_layer = (P("mp", None), P(), P())
    in_specs = (
        P(("doc", "seq"), None),
        P(("doc", "seq"), None),
        rows,
        rows,
        P(),
        P(),
        P(),
        P(None, "mp"),
        P(None, "mp"),
        P(None, "mp"),
        P("mp", None),
        *split_columns,
        P("mp", None),
        *column_layer,
        *column_layer,
        *column_layer,
        *row_layer,
        *column_layer,
        *column_layer,
        *row_layer,
    )
    out_specs = (
        P(("doc", "seq", "mp"), None),
        P(("doc", "seq", "mp"), None),
        *column_layer,
        *column_layer,
        *column_layer,
        *row_layer,
        *column_layer,
        *column_layer,
        *row_layer,
    )
    return jax.shard_map(
        per_device, mesh=mesh, in_specs=in_specs, out_specs=out_specs, check_vma=False
    )
```

profile of v0, /device:TPU:0, one launch (start us, length us, event | category | flops | bytes accessed | tf_op | source)
XLA Modules:
  0.0 456.1 jit_solution(7075084587100161262)
XLA Ops:
  19.3 18.5 %project_heads.1 = (bf16[3,768,128]{2,1,0:T(8,128)(2,1)}, bf16[3,768,128]{2,1,0:T(8,128)(2,1)}, bf16[3,768,128]{2,1,0:T(8,128)(2,1)}, bf16[3,768,128]{2,1,0:T(8,...) custom-call(s32[1]{0:T(128)} %bitcast.1.scalars, ...), custom_call_target="tpu_custom_call" | custom-call | flops 1 | bytes 1 | tf_op jit(solution)/shard_map/project_heads/pallas_call | solution.py:789
  44.3 21.2 %merge_others.1 = (f32[1,2048]{1,0:T(1,128)}, f32[16,2048]{1,0:T(8,128)}, f32[1,2048]{1,0:T(1,128)}, f32[16,2048]{1,0:T(8,128)}, bf16[1408,2048]{1,0:T(8,128)(2,...) custom-call(bf16[512,2048]{1,0:T(8,128)(2,1)} %out_w, ...), custom_call_target="tpu_custom_call" | custom-call | flops 1 | bytes 1 | tf_op jit(solution)/shard_map/merge_others/pallas_call | solution.py:648
  69.5 17.5 %attend.1 = (bf16[768,128]{1,0:T(8,128)(2,1)}, bf16[768,128]{1,0:T(8,128)(2,1)}, bf16[768,128]{1,0:T(8,128)(2,1)}, bf16[768,128]{1,0:T(8,128)(2,1)}, f32[4,1,768]{2,1,0:T(1,128)}) custom-call(s32[17]{0:T(128)} %pad_add_fusion.scalars, bf16[3,768,128]{2,1,0:T(8,128)(2,1)} %get-tuple-element.140.refs_0_, bf16[3,768,128]{2,1,0:T(8,128)(2,1)} %copy-done.5, ...), custom_call_target="tpu_custom_call" | custom-call | flops 1 | bytes 1 | tf_op jit(solution)/shard_map/attend/pallas_call | solution.py:395
  90.6 4.3 collective-permute-done.6.refs_1_
  106.4 5.3 %collective-permute-done.10 = bf16[416,512]{1,0:T(8,128)(2,1)S(1)} collective-permute-done((bf16[416,512]{1,0:T(8,128)(2,1)}, bf16[416,512]{1,0:T(8,128)(2,1)S(1)}, u32[]{:S(2)}, u32[]{:S(2)}) %collective-permute-start.10) | collective-permute-done | bytes 426016 | tf_op jit(solution)/shard_map/ppermute | solution.py:113
  117.7 8.6 %collective-permute-done.13 = bf16[416,512]{1,0:T(8,128)(2,1)S(1)} collective-permute-done((bf16[416,512]{1,0:T(8,128)(2,1)S(1)}, bf16[416,512]{1,0:T(8,128)(2,1)S(1)}, u32[]{:S(2)}, u32[]{:S(2)}) %collective-permute-start.13) | collective-permute-done | bytes 426016 | tf_op jit(solution)/shard_map/ppermute | solution.py:114
  129.2 7.1 %collective-permute-done.14 = bf16[416,512]{1,0:T(8,128)(2,1)S(1)} collective-permute-done((bf16[416,512]{1,0:T(8,128)(2,1)S(1)}, bf16[416,512]{1,0:T(8,128)(2,1)S(1)}, u32[]{:S(2)}, u32[]{:S(2)}) %collective-permute-start.14) | collective-permute-done | bytes 426016 | tf_op jit(solution)/shard_map/ppermute | solution.py:114
  139.4 19.6 %out_project.2 = (bf16[384,2048]{1,0:T(8,128)(2,1)}, f32[96,2048]{1,0:T(8,128)}, f32[96,2048]{1,0:T(8,128)}, bf16[96,16]{1,0:T(8,128)(2,1)}, bf16[96,2048]{1,0:T(8,128)(2,1)}) custom-call(s32[1]{0:T(128)} %bitcast.scalars, bf16[416,512]{1,0:T(8,128)(2,1)} %get-tuple-element.149.refs_0_, bf16[416,512]{1,0:T(8,128)(2,1)} %broadcast_select_fusion.4.refs_1_, ...), custom_call_target="tpu_custom_call" | custom-call | flops 1 | bytes 1 | tf_op jit(solution)/shard_map/out_project/pallas_call | solution.py:972
  158.9 19.8 %feed_forward.2 = (bf16[384,1408]{1,0:T(8,128)(2,1)}, bf16[384,2816]{1,0:T(8,128)(2,1)}, f32[1,2816]{1,0:T(1,128)}, bf16[384,2048]{1,0:T(8,128)(2,1)}) custom-call(bf16[384,2048]{1,0:T(8,128)(2,1)} %get-tuple-element.197.hnorm_ref.refs_0_, bf16[4,2,96,2048]{3,2,1,0:T(8,128)(2,1)} %bitcast.124, f32[1,2048]{1,0:T(1,128)} %get-tuple-element.156.down_scale_ref.refs_4_, ...), custom_call_target="tpu_custom_call" | custom-call | flops 1 | bytes 1 | tf_op jit(solution)/shard_map/feed_forward/pallas_call | solution.py:1079
  181.2 11.9 %out_project.3 = (bf16[384,2048]{1,0:T(8,128)(2,1)}, f32[96,2048]{1,0:T(8,128)}, f32[96,2048]{1,0:T(8,128)}, bf16[96,16]{1,0:T(8,128)(2,1)}, bf16[96,2048]{1,0:T(8,128)(2,1)}) custom-call(s32[1]{0:T(128)} %bitcast.scalars, bf16[384,512]{1,0:T(8,128)(2,1)} %get-tuple-element.161.refs_0_, bf16[384,512]{1,0:T(8,128)(2,1)} %get-tuple-element.162.refs_1_, ...), custom_call_target="tpu_custom_call" | custom-call | flops 1 | bytes 1 | tf_op jit(solution)/shard_map/out_project/pallas_call | solution.py:972
  193.0 19.8 %feed_forward.3 = (bf16[384,1408]{1,0:T(8,128)(2,1)}, bf16[384,2816]{1,0:T(8,128)(2,1)}, f32[1,2816]{1,0:T(1,128)}, bf16[384,2048]{1,0:T(8,128)(2,1)}) custom-call(bf16[384,2048]{1,0:T(8,128)(2,1)} %get-tuple-element.198.hnorm_ref.refs_1_, bf16[4,2,96,2048]{3,2,1,0:T(8,128)(2,1)} %bitcast.125, f32[1,2048]{1,0:T(1,128)} %get-tuple-element.156.down_scale_ref.refs_4_, ...), custom_call_target="tpu_custom_call" | custom-call | flops 1 | bytes 1 | tf_op jit(solution)/shard_map/feed_forward/pallas_call | solution.py:1079
  215.0 13.2 %down_project.1 = (bf16[4,2,96,2048]{3,2,1,0:T(8,128)(2,1)}, f32[1,2048]{1,0:T(1,128)}, bf16[16,2048]{1,0:T(8,128)(2,1)}, bf16[16,1408]{1,0:T(8,128)(2,1)}) custom-call(bf16[384,1408]{1,0:T(8,128)(2,1)} %get-tuple-element.169.refs_0_, bf16[384,1408]{1,0:T(8,128)(2,1)} %get-tuple-element.170.refs_1_, bf16[1408,2048]{1,0:T(8,128)(2,1)} %get-tuple-element.159.wd_hbm.refs_2_, ...), custom_call_target="tpu_custom_call" | custom-call | flops 1 | bytes 1 | tf_op jit(solution)/shard_map/down_project/pallas_call | solution.py:1364
  228.2 8.5 %back_out.2 = (bf16[4,96,512]{2,1,0:T(8,128)(2,1)}, f32[96,2048]{1,0:T(8,128)}, bf16[96,2048]{1,0:T(8,128)(2,1)}, f32[1,2048]{1,0:T(1,128)}, f32[16,2048]{1,0:T(8,128)}, /*index=5*/f32[16,2048]{1,0:T(8,128)}) custom-call(s32[1]{0:T(128)} %bitcast.scalars, bf16[96,2048]{1,0:T(8,128)(2,1)} %reduce-scatter.5.cloned.1.call-done.refs_0_, ...), custom_call_target="tpu_custom_call" | custom-call | flops 1 | bytes 1 | tf_op jit(solution)/shard_map/back_out/pallas_call | solution.py:1149
  240.7 14.2 %reduce-scatter.7.cloned.1.call-done.refs_3_ = bf16[96,2048]{1,0:T(8,128)(2,1)} async-done(((bf16[384,2048]{1,0:T(8,128)(2,1)}), bf16[96,2048]{1,0:T(8,128)(2,1)}) %reduce-scatter.7.cloned.1.call-update) | async-done | bytes 393232 | tf_op jit(solution)/shard_map/reduce_scatter | solution.py:1650
  255.7 8.4 %back_out.3 = (bf16[4,96,512]{2,1,0:T(8,128)(2,1)}, f32[96,2048]{1,0:T(8,128)}, bf16[96,2048]{1,0:T(8,128)(2,1)}, f32[1,2048]{1,0:T(1,128)}, f32[16,2048]{1,0:T(8,128)}, /*index=5*/f32[16,2048]{1,0:T(8,128)}) custom-call(s32[1]{0:T(128)} %bitcast.scalars, f32[1,2048]{1,0:T(1,128)} %get-tuple-element.178.refs_0_, f32[16,2048]{1,0:T(8,128)} %get-tuple-element.179.refs_1_, ...), custom_call_target="tpu_custom_call" | custom-call | flops 1 | bytes 1 | tf_op jit(solution)/shard_map/back_out/pallas_call | solution.py:1149
  271.8 5.4 %collective-permute-done.19 = bf16[96,512]{1,0:T(8,128)(2,1)S(1)} collective-permute-done((bf16[96,512]{1,0:T(8,128)(2,1)S(1)}, bf16[96,512]{1,0:T(8,128)(2,1)S(1)}, u32[]{:S(2)}, u32[]{:S(2)}) %collective-permute-start.19) | collective-permute-done | bytes 98336 | tf_op jit(solution)/shard_map/ppermute | solution.py:1678
  291.6 24.8 %attend_back.1 = (bf16[3,768,128]{2,1,0:T(8,128)(2,1)}, bf16[3,768,128]{2,1,0:T(8,128)(2,1)}, bf16[3,768,128]{2,1,0:T(8,128)(2,1)}, bf16[3,768,128]{2,1,0:T(8,128)(2,1)}) custom-call(s32[17]{0:T(128)} %pad_add_fusion.scalars, bf16[3,768,128]{2,1,0:T(8,128)(2,1)} %get-tuple-element.140.refs_0_, bf16[3,768,128]{2,1,0:T(8,128)(2,1)} %copy-done.5, ...), custom_call_target="tpu_custom_call" | custom-call | flops 1 | bytes 1 | tf_op jit(solution)/shard_map/attend_back/pallas_call | solution.py:526
  321.9 15.7 %shares.2 = (bf16[32,2048]{1,0:T(8,128)(2,1)}, bf16[16,2816]{1,0:T(8,128)(2,1)}) custom-call(bf16[384,2048]{1,0:T(8,128)(2,1)} %get-tuple-element.197.hnorm_ref.refs_0_, bf16[384,2048]{1,0:T(8,128)(2,1)} %get-tuple-element.198.hnorm_ref.refs_1_, bf16[384,2816]{1,0:T(8,128)(2,1)} %get-tuple-element.199.refs_2_, bf16[384,2816]{1,0:T(8,128)(2,1)} %get-tuple-element.200.refs_3_, ...), custom_call_target="tpu_custom_call" | custom-call | flops 1 | bytes 1 | tf_op jit(solution)/shard_map/shares/pallas_call | solution.py:1294
  337.7 5.8 %collective-permute-done.25.refs_2_ = bf16[3,768,128]{2,1,0:T(8,128)(2,1)S(1)} collective-permute-done((bf16[3,768,128]{2,1,0:T(8,128)(2,1)}, bf16[3,768,128]{2,1,0:T(8,128)(2,1)S(1)}, u32[]{:S(2)}, u32[]{:S(2)}) %collective-permute-start.25) | collective-permute-done | bytes 589856 | tf_op jit(solution)/shard_map/ppermute | solution.py:52
  344.5 13.9 %unproject.1 = (bf16[768,1536]{1,0:T(8,128)(2,1)}, f32[1,1536]{1,0:T(1,128)}, bf16[768,2048]{1,0:T(8,128)(2,1)}) custom-call(s32[1]{0:T(128)} %bitcast.1.scalars, f32[768,128]{1,0:T(8,128)} %get-tuple-element.287.cos_ref, f32[768,128]{1,0:T(8,128)} %get-tuple-element.286.sin_ref, bf16[768,1536]{1,0:T(8,128)(2,1)} %get-tuple-element.134.raw_ref, ...), custom_call_target="tpu_custom_call" | custom-call | flops 1 | bytes 1 | tf_op jit(solution)/shard_map/unproject/pallas_call | solution.py:1218
  362.4 10.6 %shares.3 = (bf16[48,2048]{1,0:T(8,128)(2,1)}, bf16[16,1536]{1,0:T(8,128)(2,1)}) custom-call(bf16[768,2048]{1,0:T(8,128)(2,1)} %get-tuple-element.222.refs_0_, bf16[768,1536]{1,0:T(8,128)(2,1)} %get-tuple-element.223.refs_1_, bf16[48,2048]{1,0:T(8,128)(2,1)} %bitcast.135, f32[16,1536]{1,0:T(8,128)} %pad_maximum_fusion.4.refs_3_, ...), custom_call_target="tpu_custom_call" | custom-call | flops 1 | bytes 1 | tf_op jit(solution)/shard_map/shares/pallas_call | solution.py:1294
  378.4 4.3 collective-permute-done.38
  399.7 11.1 %collective-permute-done.31 = bf16[32,2048]{1,0:T(8,128)(2,1)S(1)} collective-permute-done((bf16[32,2048]{1,0:T(8,128)(2,1)S(1)}, bf16[32,2048]{1,0:T(8,128)(2,1)S(1)}, u32[]{:S(2)}, u32[]{:S(2)}) %collective-permute-start.31) | collective-permute-done | bytes 131104 | tf_op jit(solution)/shard_map/ppermute | solution.py:52
  411.1 10.4 %collective-permute-done.32 = bf16[32,2048]{1,0:T(8,128)(2,1)S(1)} collective-permute-done((bf16[32,2048]{1,0:T(8,128)(2,1)S(1)}, bf16[32,2048]{1,0:T(8,128)(2,1)S(1)}, u32[]{:S(2)}, u32[]{:S(2)}) %collective-permute-start.32) | collective-permute-done | bytes 131104 | tf_op jit(solution)/shard_map/ppermute | solution.py:52
  (308 shorter events, 140.7 us)
Async XLA Ops:
  7.2 132.2 %all-gather.4.cloned.1.call-start = ((), (), s32[]{:S(2)}) async-start(), calls=%async_computation.4 | async-start | bytes 9437184 | tf_op jit(solution)/shard_map/all_gather | solution.py:1522
  9.8 169.0 %all-gather.6.cloned.1.call-start = ((), (), s32[]{:S(2)}) async-start(), calls=%async_computation.9 | async-start | bytes 1966080 | tf_op jit(solution)/shard_map/all_gather | solution.py:1609
  37.9 30.4 %collective-permute-start.3 = (bf16[3,768,128]{2,1,0:T(8,128)(2,1)}, bf16[3,768,128]{2,1,0:T(8,128)(2,1)S(1)}, u32[]{:S(2)}, u32[]{:S(2)}) collective-permute-start(bf16[3,768,128]{2,1,0:T(8,128)(2,1)} %get-tuple-element.131), channel_id=1, source_target_pairs={{0,4},{4,0},{8,12},{12,8},{1,5},{5,1},{9,13},{13,9},{2,6},{6,2},{1... | collective-permute-start | bytes 1769480 | tf_op jit(solution)/shard_map/ppermute | solution.py:52
  39.9 28.4 %collective-permute-start.4 = (bf16[3,768,128]{2,1,0:T(8,128)(2,1)}, bf16[3,768,128]{2,1,0:T(8,128)(2,1)S(1)}, u32[]{:S(2)}, u32[]{:S(2)}) collective-permute-start(bf16[3,768,128]{2,1,0:T(8,128)(2,1)} %get-tuple-element.132), channel_id=1, source_target_pairs={{0,8},{4,12},{8,0},{12,4},{1,9},{5,13},{9,1},{13,5},{2,10},{6,14},... | collective-permute-start | bytes 1769480 | tf_op jit(solution)/shard_map/ppermute | solution.py:52
  41.4 26.9 %collective-permute-start.5 = (bf16[3,768,128]{2,1,0:T(8,128)(2,1)}, bf16[3,768,128]{2,1,0:T(8,128)(2,1)S(1)}, u32[]{:S(2)}, u32[]{:S(2)}) collective-permute-start(bf16[3,768,128]{2,1,0:T(8,128)(2,1)} %get-tuple-element.133), channel_id=1, source_target_pairs={{0,12},{4,8},{8,4},{12,0},{1,13},{5,9},{9,5},{13,1},{2,14},{6,10},... | collective-permute-start | bytes 1769480 | tf_op jit(solution)/shard_map/ppermute | solution.py:52
  101.6 10.0 %collective-permute-start.10 = (bf16[416,512]{1,0:T(8,128)(2,1)}, bf16[416,512]{1,0:T(8,128)(2,1)S(1)}, u32[]{:S(2)}, u32[]{:S(2)}) collective-permute-start(bf16[416,512]{1,0:T(8,128)(2,1)} %get-tuple-element.149.refs_0_), channel_id=1, source_target_pairs={{0,1},{1,2},{2,3},{4,5},{5,6},{6,7},{8,9},{9,10},{10,11},{12,13},{... | collective-permute-start | bytes 1277960 | tf_op jit(solution)/shard_map/ppermute | solution.py:113
  105.1 10.6 %collective-permute-start.9 = (bf16[416,512]{1,0:T(8,128)(2,1)}, bf16[416,512]{1,0:T(8,128)(2,1)S(1)}, u32[]{:S(2)}, u32[]{:S(2)}) collective-permute-start(bf16[416,512]{1,0:T(8,128)(2,1)} %get-tuple-element.149.refs_0_), channel_id=1, source_target_pairs={{1,0},{2,1},{3,2},{5,4},{6,5},{7,6},{9,8},{10,9},{11,10},{13,12},{... | collective-permute-start | bytes 1277960 | tf_op jit(solution)/shard_map/ppermute | solution.py:114
  115.7 10.6 %collective-permute-start.13 = (bf16[416,512]{1,0:T(8,128)(2,1)S(1)}, bf16[416,512]{1,0:T(8,128)(2,1)S(1)}, u32[]{:S(2)}, u32[]{:S(2)}) collective-permute-start(bf16[416,512]{1,0:T(8,128)(2,1)S(1)} %collective-permute-done.9), channel_id=1, source_target_pairs={{1,0},{2,1},{5,4},{6,5},{9,8},{10,9},{13,12},{14,13},{17,16},{18,1... | collective-permute-start | bytes 1277960 | tf_op jit(solution)/shard_map/ppermute | solution.py:114
  117.0 11.4 %collective-permute-start.12 = (bf16[416,512]{1,0:T(8,128)(2,1)S(1)}, bf16[416,512]{1,0:T(8,128)(2,1)S(1)}, u32[]{:S(2)}, u32[]{:S(2)}) collective-permute-start(bf16[416,512]{1,0:T(8,128)(2,1)S(1)} %collective-permute-done.11), channel_id=1, source_target_pairs={{2,3},{6,7},{10,11},{14,15},{18,19},{22,23},{26,27},{30,31}} | collective-permute-start | bytes 1277960 | tf_op jit(solution)/shard_map/ppermute | solution.py:113
  126.3 10.0 %collective-permute-start.14 = (bf16[416,512]{1,0:T(8,128)(2,1)S(1)}, bf16[416,512]{1,0:T(8,128)(2,1)S(1)}, u32[]{:S(2)}, u32[]{:S(2)}) collective-permute-start(bf16[416,512]{1,0:T(8,128)(2,1)S(1)} %collective-permute-done.13), channel_id=1, source_target_pairs={{1,0},{5,4},{9,8},{13,12},{17,16},{21,20},{25,24},{29,28}} | collective-permute-start | bytes 1277960 | tf_op jit(solution)/shard_map/ppermute | solution.py:114
  137.1 91.1 %reduce-scatter.5.cloned.1.call-start = ((), (), s32[]{:S(2)}) async-start(), calls=%async_computation.5 | async-start | bytes 1966080 | tf_op jit(solution)/shard_map/reduce_scatter | solution.py:1650
  178.8 76.2 %reduce-scatter.7.cloned.1.call-start = ((), (), s32[]{:S(2)}) async-start(), calls=%async_computation.6 | async-start | bytes 1966080 | tf_op jit(solution)/shard_map/reduce_scatter | solution.py:1650
  212.9 218.7 %reduce-scatter.9.cloned.1.call-start = ((), (), s32[]{:S(2)}) async-start(), calls=%async_computation.7 | async-start | bytes 3932160 | tf_op jit(solution)/shard_map/reduce_scatter | solution.py:1650
  237.7 17.2 %collective-permute-start.17 = (bf16[96,512]{1,0:T(8,128)(2,1)S(1)}, bf16[96,512]{1,0:T(8,128)(2,1)S(1)}, u32[]{:S(2)}, u32[]{:S(2)}) collective-permute-start(bf16[96,512]{1,0:T(8,128)(2,1)S(1)} %get-tuple-element.276), channel_id=1, source_target_pairs={{0,3},{1,0},{2,1},{3,2},{4,7},{5,4},{6,5},{7,6},{8,11},{9,8},{10,9... | collective-permute-start | bytes 294920 | tf_op jit(solution)/shard_map/ppermute | solution.py:1678
  238.7 17.0 %collective-permute-start.16 = (bf16[96,512]{1,0:T(8,128)(2,1)S(1)}, bf16[96,512]{1,0:T(8,128)(2,1)S(1)}, u32[]{:S(2)}, u32[]{:S(2)}) collective-permute-start(bf16[96,512]{1,0:T(8,128)(2,1)S(1)} %get-tuple-element.277), channel_id=1, source_target_pairs={{0,2},{1,3},{2,0},{3,1},{4,6},{5,7},{6,4},{7,5},{8,10},{9,11},{10,... | collective-permute-start | bytes 294920 | tf_op jit(solution)/shard_map/ppermute | solution.py:1678
  238.7 17.0 %collective-permute-start.15 = (bf16[96,512]{1,0:T(8,128)(2,1)S(1)}, bf16[96,512]{1,0:T(8,128)(2,1)S(1)}, u32[]{:S(2)}, u32[]{:S(2)}) collective-permute-start(bf16[96,512]{1,0:T(8,128)(2,1)S(1)} %get-tuple-element.278), channel_id=1, source_target_pairs={{0,1},{1,2},{2,3},{3,0},{4,5},{5,6},{6,7},{7,4},{8,9},{9,10},{10,1... | collective-permute-start | bytes 294920 | tf_op jit(solution)/shard_map/ppermute | solution.py:1678
  289.6 144.7 %reduce-scatter.11.cloned.1.call-start = ((), (), s32[]{:S(2)}) async-start(), calls=%async_computation.8 | async-start | bytes 3932160 | tf_op jit(solution)/shard_map/reduce_scatter | solution.py:1650
  316.4 21.2 %collective-permute-start.24 = (bf16[3,768,128]{2,1,0:T(8,128)(2,1)}, bf16[3,768,128]{2,1,0:T(8,128)(2,1)S(1)}, u32[]{:S(2)}, u32[]{:S(2)}) collective-permute-start(bf16[3,768,128]{2,1,0:T(8,128)(2,1)} %get-tuple-element.192), channel_id=1, source_target_pairs={{0,4},{4,0},{8,12},{12,8},{1,5},{5,1},{9,13},{13,9},{2,6},{6,2},{1... | collective-permute-start | bytes 1769480 | tf_op jit(solution)/shard_map/ppermute | solution.py:52
  318.2 25.3 %collective-permute-start.25 = (bf16[3,768,128]{2,1,0:T(8,128)(2,1)}, bf16[3,768,128]{2,1,0:T(8,128)(2,1)S(1)}, u32[]{:S(2)}, u32[]{:S(2)}) collective-permute-start(bf16[3,768,128]{2,1,0:T(8,128)(2,1)} %get-tuple-element.193), channel_id=1, source_target_pairs={{0,8},{4,12},{8,0},{12,4},{1,9},{5,13},{9,1},{13,5},{2,10},{6,14},... | collective-permute-start | bytes 1769480 | tf_op jit(solution)/shard_map/ppermute | solution.py:52
  319.7 23.8 %collective-permute-start.26 = (bf16[3,768,128]{2,1,0:T(8,128)(2,1)}, bf16[3,768,128]{2,1,0:T(8,128)(2,1)S(1)}, u32[]{:S(2)}, u32[]{:S(2)}) collective-permute-start(bf16[3,768,128]{2,1,0:T(8,128)(2,1)} %get-tuple-element.194), channel_id=1, source_target_pairs={{0,12},{4,8},{8,4},{12,0},{1,13},{5,9},{9,5},{13,1},{2,14},{6,10},... | collective-permute-start | bytes 1769480 | tf_op jit(solution)/shard_map/ppermute | solution.py:52
  362.4 14.7 %collective-permute-start.37 = (bf16[24,2816]{1,0:T(8,128)(2,1)S(1)}, bf16[24,2816]{1,0:T(8,128)(2,1)S(1)}, u32[]{:S(2)}, u32[]{:S(2)}) collective-permute-start(bf16[24,2816]{1,0:T(8,128)(2,1)S(1)} %constant_dynamic-slice_fusion.1), channel_id=1, source_target_pairs={{0,16},{16,0},{1,17},{17,1},{2,18},{18,2},{3,19},{19,3},{4,20},{20... | collective-permute-start | bytes 405512 | tf_op jit(solution)/shard_map/ppermute | solution.py:52
  376.6 11.4 %collective-permute-start.27 = (bf16[128,2048]{1,0:T(8,128)(2,1)S(1)}, bf16[128,2048]{1,0:T(8,128)(2,1)S(1)}, u32[]{:S(2)}, u32[]{:S(2)}) collective-permute-start(bf16[128,2048]{1,0:T(8,128)(2,1)S(1)} %constant_dynamic-slice_fusion.2), channel_id=1, source_target_pairs={{0,16},{16,0},{1,17},{17,1},{2,18},{18,2},{3,19},{19,3},{4,20},{20... | collective-permute-start | bytes 1572872 | tf_op jit(solution)/shard_map/ppermute | solution.py:52
  399.6 11.3 %collective-permute-start.31 = (bf16[32,2048]{1,0:T(8,128)(2,1)S(1)}, bf16[32,2048]{1,0:T(8,128)(2,1)S(1)}, u32[]{:S(2)}, u32[]{:S(2)}) collective-permute-start(bf16[32,2048]{1,0:T(8,128)(2,1)S(1)} %fusion.13), channel_id=1, source_target_pairs={{0,1},{1,0},{2,3},{3,2},{4,5},{5,4},{6,7},{7,6},{8,9},{9,8},{10,11... | collective-permute-start | bytes 393224 | tf_op jit(solution)/shard_map/ppermute | solution.py:52
  410.9 10.6 %collective-permute-start.32 = (bf16[32,2048]{1,0:T(8,128)(2,1)S(1)}, bf16[32,2048]{1,0:T(8,128)(2,1)S(1)}, u32[]{:S(2)}, u32[]{:S(2)}) collective-permute-start(bf16[32,2048]{1,0:T(8,128)(2,1)S(1)} %add.234), channel_id=1, source_target_pairs={{0,2},{1,3},{2,0},{3,1},{4,6},{5,7},{6,4},{7,5},{8,10},{9,11},{10,... | collective-permute-start | bytes 393224 | tf_op jit(solution)/shard_map/ppermute | solution.py:52
  (85 other events, 559.2 us)
Sparse Core Ops, SparseCore 0:
  10.2 84.7 all-gather.3
  137.3 34.9 all-gather.5
  178.9 33.2 reduce-scatter.4
  214.3 40.5 reduce-scatter.6
  289.1 59.2 reduce-scatter.8
  358.6 63.3 reduce-scatter.10
where the time goes:
time: 465 us; the launch traced here: 456 us
  Pallas kernels  231 us (50%)
  waiting for transfers between devices  108 us (23%)
  starting transfers between devices  44.5 us (10%)
  local copies, waits for them, and re-layouts  27.2 us (6%)
  other arithmetic  25.9 us (6%)
  between operations  15.6 us (3%)
    ppermute x29, waiting for transfers between devices, swap(): return lax.ppermute(value, axis, [(i, i ^ distance) for i in range(size)])  61.3 us
    pallas_call x2, Pallas kernels, feed_forward(): pl.pallas_call(functools.partial(hidden_kernel, sizes), grid=(1,), in_spe...  39.6 us
    pallas_call x2, Pallas kernels, out_project(): pl.pallas_call(out_kernel, grid_spec=pltpu.PrefetchScalarGridSpec(num_sca...  31.5 us
    ppermute x29, starting transfers between devices, swap(): return lax.ppermute(value, axis, [(i, i ^ distance) for i in range(size)])  29.7 us
    pallas_call x2, Pallas kernels, layer_shares(): pl.pallas_call(functools.partial(shares_kernel, count, chunks, span), gri...  26.3 us
    pallas_call x1, Pallas kernels, attention_backward(): pl.pallas_call(functools.partial(body, meta), grid_spec=pltpu.PrefetchSca...  24.8 us
    pallas_call x1, Pallas kernels, merge_others(): pl.pallas_call(functools.partial(merge_kernel, starts), grid=(starts[1] +...  21.2 us
    ppermute x3, waiting for transfers between devices, line_step(): lefts.append(lax.ppermute(left, 'mp', left_pairs))  19 us
  transfers between devices with their start and end apart: 47, of which 22 were waited for; matrix products, arithmetic and copies ran while one was open for 8% of the time, Pallas kernels for 49%

commit v1 on v0

--- a/solution.py
+++ b/solution.py
@@ -77,7 +77,7 @@
     return jnp.concatenate([first, second], axis=0)
 
 
-def spread_sum(value, peers, axes):
+def spread_sum(value, peers, axes, leading):
     me = lax.rem(lax.axis_index("seq"), peers)
     parts = value.reshape(peers, -1, value.shape[-1])
     piece = lambda index: lax.dynamic_index_in_dim(parts, index, 0, keepdims=False)
@@ -89,7 +89,7 @@
     while distance < lax.axis_size("seq"):
         mine = lax.optimization_barrier(mine + swap(mine, "seq", distance))
         distance *= 2
-    return butterfly(mine, axes)
+    return jnp.concatenate([butterfly(mine[:leading], axes), mine[leading:]], axis=0)
 
 
 def spread_join(mine, peers):
@@ -140,10 +140,10 @@
     return jnp.where((lane == segment) | (lane == 16), 1.0, 0.0).astype(bf16)
 
 
-def diagonal_scores(keys, query, first_key=0):
+def diagonal_scores(keys, query):
     marked = dot_nt(keys, query)
     plain = dot_nt(keys[:, :HD], query[:, :HD])
-    key_id = lax.broadcasted_iota(jnp.int32, marked.shape, 0) + first_key
+    key_id = lax.broadcasted_iota(jnp.int32, marked.shape, 0)
     query_id = lax.broadcasted_iota(jnp.int32, marked.shape, 1)
     return jnp.where(
         key_id < query_id, marked, jnp.where(key_id == query_id, plain, MASKED)
@@ -293,8 +293,7 @@
             return (new_peak, total, out)
 
         if m:
-            steps = m * tile // tile
-            peak, total, out = lax.fori_loop(0, steps, key_tile, (peak, total, out))
+            peak, total, out = lax.fori_loop(0, m, key_tile, (peak, total, out))
         lse_ref[m] = peak * INV_ROOT + jnp.log(total)
         o_all[here, :] = (out / total).T.astype(bf16)
 
@@ -354,18 +353,15 @@
                 dk_all[at, :] += dk
             return dq_turned + dot(k_turned[:, at], grad_score)
 
-        dq_turned = jnp.zeros((HD, tile), f32)
-        for t in range(tile // tile):
-            at = pl.ds(m * tile + t * tile, tile)
-            scores = diagonal_scores(k_all[at, :], query, t * tile)
-            dq_turned = key_tile(at, scores, dq_turned, True)
+        scores = diagonal_scores(k_all[here, :], query)
+        dq_turned = key_tile(here, scores, jnp.zeros((HD, tile), f32), True)
 
         def step(j, dq_turned):
             at = pl.ds(pl.multiple_of(j * tile, HD), tile)
             return key_tile(at, dot_nt(k_all[at, :], query), dq_turned, False)
 
         if m:
-            dq_turned = lax.fori_loop(0, m * tile // tile, step, dq_turned)
+            dq_turned = lax.fori_loop(0, m, step, dq_turned)
         o_all[here, :] = (dq_turned * INV_ROOT).T.astype(bf16)
 
     for d, half, rows, at in place_rows(scalars, peers, span):
@@ -918,100 +914,22 @@
     )(k, *blocks, m_out, m_down)
 
 
-def out_kernel(scalars, *refs):
+def block_kernel(sizes, size, scalars, *refs):
     take = taker(refs)
-    size = len(refs) - 13
     x_refs = take(size)
-    w_ref, a_ref, hid_ref, b_ref, scale_ref, gain_ref = take(6)
+    a_ref, hid_ref, b_ref, out_scale_ref, gain_ref = take(5)
+    cot_ref, down_scale_ref, scale_ref, wo_hbm, w_hbm, wd_hbm = take(6)
     hnorm_ref, resid_ref, raw_own_ref, low_ref, own_ref = take(5)
-    total, through = take(2)
-    step = pl.program_id(0)
-
-    @pl.when(step == 0)
-    def _():
-        total[...] = jnp.zeros_like(total)
-        through[...] = jnp.zeros_like(through)
-
-    for c, x_ref in enumerate(x_refs):
-
-        @pl.when(step == c)
-        def _(x_ref=x_ref):
-            x = x_ref[...]
-            total[...] += dot(x, w_ref[...])
-            through[...] += dot_nt(x, a_ref[...])
-            part, width = own_ref.shape[0], x_ref.shape[1]
-            mine = pl.ds(pl.multiple_of(scalars[0] * part, 16), part)
-            device = lax.rem(scalars[0] + c, size)
-            at = pl.ds(pl.multiple_of(device * width, HD), width)
-            own_ref[:, at] = x_ref[mine, :]
-
-    @pl.when(step == size - 1)
-    def _():
-        part = hid_ref.shape[2]
-        for piece in range(size):
-            at = pl.ds(piece * part, part)
-            low = through[at, :].astype(bf16)
-            raw = total[at, :] + dot(low, b_ref[...])
-            resid = hid_ref[piece, 0].astype(f32) + raw * scale_ref[...]
-            inverse = lax.rsqrt(jnp.mean(resid * resid, axis=-1, keepdims=True) + EPS)
-            hnorm_ref[at, :] = (resid * inverse * gain_ref[...]).astype(bf16)
-
-            @pl.when(scalars[0] == piece)
-            def _(resid=resid, raw=raw, low=low):
-                resid_ref[...] = resid
-                raw_own_ref[...] = raw
-                low_ref[...] = low
-
-
-def out_project(k, chunk, x, w, a_t, hidden, b2, scale, gain):
-    size = len(x)
-    width, wide = x[0].shape[1], w.shape[1]
-    part = hidden.shape[2]
-    rows = size * part
-    fixed = lambda *shape: pl.BlockSpec(shape, lambda i, s: (0,) * len(shape))
-    return pl.pallas_call(
-        out_kernel,
-        grid_spec=pltpu.PrefetchScalarGridSpec(
-            num_scalar_prefetch=1,
-            grid=(size,),
-            in_specs=[fixed(rows, width)] * size
-            + [
-                pl.BlockSpec((width, wide), lambda i, s: (lax.rem(i + s[0], size), 0)),
-                pl.BlockSpec((RANK, width), lambda i, s: (0, lax.rem(i + s[0], size))),
-                pl.BlockSpec((size, 1, part, wide), lambda i, s: (0, chunk, 0, 0)),
-                fixed(RANK, wide),
-                fixed(1, wide),
-                fixed(1, wide),
-            ],
-            out_specs=[
-                fixed(rows, wide),
-                fixed(part, wide),
-                fixed(part, wide),
-                fixed(part, RANK),
-                fixed(part, size * width),
-            ],
-            scratch_shapes=[
-                pltpu.VMEM((rows, wide), f32),
-                pltpu.VMEM((rows, RANK), f32),
-            ],
-        ),
-        out_shape=[
-            jax.ShapeDtypeStruct((rows, wide), bf16),
-            jax.ShapeDtypeStruct((part, wide), f32),
-            jax.ShapeDtypeStruct((part, wide), f32),
-            jax.ShapeDtypeStruct((part, RANK), bf16),
-            jax.ShapeDtypeStruct((part, size * width), bf16),
-        ],
-        compiler_params=pltpu.CompilerParams(vmem_limit_bytes=VMEM_LIMIT),
-        cost_estimate=cost(2 * rows * width * size * wide, 2 * width * size * wide),
-        name="out_project",
-    )(k, *x, w, a_t, hidden, b2, scale, gain)
-
-
-def hidden_kernel(sizes, hnorm_ref, cot_ref, down_scale_ref, scale_ref, w_hbm, wd_hbm,
-                  act_ref, dz_ref, g_ref, dh_ref, total, w_all, wd_all, dz_down, sem, down_sem):
-    rows = hnorm_ref.shape[0]
+    act_ref, dz_ref, g_ref, dh_ref = take(4)
+    total, through, dz_down, wo_all, w_all, wd_all, out_sem, sem, down_sem = take(9)
+    k = scalars[0]
+    rows, width = x_refs[0].shape
+    part = rows // size
     starts = [sum(sizes[:j]) for j in range(len(sizes))]
+
+    def out_copy(c):
+        source = pl.ds(pl.multiple_of(lax.rem(k + c, size) * width, HD), width)
+        return pltpu.make_async_copy(wo_hbm.at[source, :], wo_all.at[c], out_sem.at[c])
 
     def copies(j):
         both = pl.ds(2 * starts[j], 2 * sizes[j])
@@ -1021,13 +939,38 @@
             pltpu.make_async_copy(w_hbm.at[:, both], w_all.at[:, both], sem.at[j]),
         )
 
+    for c in range(size):
+        out_copy(c).start()
     for j in range(len(sizes)):
         for copy in copies(j):
             copy.start()
-    part = rows // cot_ref.shape[0]
-    for i in range(cot_ref.shape[0]):
+    for i in range(size):
         cot = cot_ref[i, 0].astype(f32)
         dz_down[i * part : (i + 1) * part, :] = (cot * down_scale_ref[...]).astype(bf16)
+
+    mine = pl.ds(pl.multiple_of(k * part, 16), part)
+    for c, x_ref in enumerate(x_refs):
+        at = pl.ds(pl.multiple_of(lax.rem(k + c, size) * width, HD), width)
+        own_ref[:, at] = x_ref[mine, :]
+        out_copy(c).wait()
+        x = x_ref[...]
+        product = dot(x, wo_all[c])
+        rank_part = dot_nt(x, a_ref[:, at])
+        total[...] = total[...] + product if c else product
+        through[...] = through[...] + rank_part if c else rank_part
+    for piece in range(size):
+        at = pl.ds(piece * part, part)
+        low = through[at, :].astype(bf16)
+        raw = total[at, :] + dot(low, b_ref[...])
+        resid = hid_ref[piece, 0].astype(f32) + raw * out_scale_ref[...]
+        inverse = lax.rsqrt(jnp.mean(resid * resid, axis=-1, keepdims=True) + EPS)
+        hnorm_ref[at, :] = (resid * inverse * gain_ref[...]).astype(bf16)
+
+        @pl.when(k == piece)
+        def _(resid=resid, raw=raw, low=low):
+            resid_ref[...] = resid
+            raw_own_ref[...] = raw
+            low_ref[...] = low
 
     def products(j):
         for copy in copies(j):
@@ -1060,52 +1003,62 @@
             g_ref[:, up_at] = jnp.sum(dup * raw_up, axis=0, keepdims=True)
             dz_ref[:, gate_at] = (dgate * scale_gate).astype(bf16)
             dz_ref[:, up_at] = (dup * scale_up).astype(bf16)
-        both = slice(2 * starts[j], 2 * (starts[j] + sizes[j]))
-        product = dot_nt(dz_ref[:, both], w_all[:, both])
-        if j == 0:
-            total[...] = product
-        elif j + 1 < len(sizes):
-            total[...] += product
-        else:
-            dh_ref[...] = (total[...] + product).astype(bf16)
-
-
-def feed_forward(chunk, hnorm, cotangent, down_scale, scale, w, wd):
-    rows, depth = hnorm.shape
+    dh_ref[...] = dot_nt(dz_ref[...], w_all[...]).astype(bf16)
+
+
+def block(k, chunk, x, a_t, hidden, b2, out_scale, gain, cotangent, down_scale, scale, wo, w, wd):
+    size, _, part, wide = hidden.shape
+    rows, width = size * part, x[0].shape[1]
     ff = wd.shape[0]
-    size, _, part, _ = cotangent.shape
-    sizes = [2 * HD] * (ff // (2 * HD)) + [HD] * (ff // HD % 2)
-    fixed = lambda *shape: pl.BlockSpec(shape, lambda i: (0,) * len(shape))
+    sizes = [ff]
+    fixed = lambda *shape: pl.BlockSpec(shape, lambda i, s: (0,) * len(shape))
+    view = pl.BlockSpec((size, 1, part, wide), lambda i, s: (0, chunk, 0, 0))
+    shapes = [
+        ((rows, wide), bf16),
+        ((part, wide), f32),
+        ((part, wide), f32),
+        ((part, RANK), bf16),
+        ((part, size * width), bf16),
+        ((rows, ff), bf16),
+        ((rows, 2 * ff), bf16),
+        ((1, 2 * ff), f32),
+        ((rows, wide), bf16),
+    ]
     return pl.pallas_call(
-        functools.partial(hidden_kernel, sizes),
-        grid=(1,),
-        in_specs=[
-            fixed(rows, depth),
-            pl.BlockSpec((size, 1, part, depth), lambda i: (0, chunk, 0, 0)),
-            fixed(1, depth),
-            fixed(1, 2 * ff),
-            pl.BlockSpec(memory_space=pl.ANY),
-            pl.BlockSpec(memory_space=pl.ANY),
-        ],
-        out_specs=[fixed(rows, ff), fixed(rows, 2 * ff), fixed(1, 2 * ff), fixed(rows, depth)],
-        out_shape=[
-            jax.ShapeDtypeStruct((rows, ff), bf16),
-            jax.ShapeDtypeStruct((rows, 2 * ff), bf16),
-            jax.ShapeDtypeStruct((1, 2 * ff), f32),
-            jax.ShapeDtypeStruct((rows, depth), bf16),
-        ],
-        scratch_shapes=[
-            pltpu.VMEM((rows, depth), f32),
-            pltpu.VMEM((depth, 2 * ff), bf16),
-            pltpu.VMEM((ff, depth), bf16),
-            pltpu.VMEM((rows, depth), bf16),
-            pltpu.SemaphoreType.DMA((len(sizes),)),
-            pltpu.SemaphoreType.DMA((len(sizes),)),
-        ],
-        compiler_params=pltpu.CompilerParams(vmem_limit_bytes=VMEM_LIMIT),
-        cost_estimate=cost(10 * rows * depth * ff, 6 * depth * ff),
-        name="feed_forward",
-    )(hnorm, cotangent, down_scale, scale, w, wd)
+        functools.partial(block_kernel, sizes, size),
+        grid_spec=pltpu.PrefetchScalarGridSpec(
+            num_scalar_prefetch=1,
+            grid=(1,),
+            in_specs=[fixed(rows, width)] * size
+            + [
+                fixed(RANK, size * width),
+                view,
+                fixed(RANK, wide),
+                fixed(1, wide),
+                fixed(1, wide),
+                view,
+                fixed(1, wide),
+                fixed(1, 2 * ff),
+            ]
+            + [pl.BlockSpec(memory_space=pl.ANY)] * 3,
+            out_specs=[fixed(*shape) for shape, _ in shapes],
+            scratch_shapes=[
+                pltpu.VMEM((rows, wide), f32),
+                pltpu.VMEM((rows, RANK), f32),
+                pltpu.VMEM((rows, wide), bf16),
+                pltpu.VMEM((size, width, wide), bf16),
+                pltpu.VMEM((wide, 2 * ff), bf16),
+                pltpu.VMEM((ff, wide), bf16),
+                pltpu.SemaphoreType.DMA((size,)),
+                pltpu.SemaphoreType.DMA((len(sizes),)),
+                pltpu.SemaphoreType.DMA((len(sizes),)),
+            ],
+        ),
+        out_shape=[jax.ShapeDtypeStruct(shape, kind) for shape, kind in shapes],
+        compiler_params=pltpu.CompilerParams(vmem_limit_bytes=60 * MIB),
+        cost_estimate=cost(10 * rows * wide * ff, 6 * wide * ff),
+        name="block",
+    )(k, *x, a_t, hidden, b2, out_scale, gain, cotangent, down_scale, scale, wo, w, wd)
 
 
 def back_out_kernel(scalars, *refs):
@@ -1214,7 +1167,7 @@
     operands = [cosine, sine, raw, scale]
     rows, wide = raw.shape
     depth = w.shape[0]
-    step = 2 * HD
+    step = 8 * HD
     return pl.pallas_call(
         functools.partial(unproject_kernel, len(grads)),
         grid_spec=pltpu.PrefetchScalarGridSpec(
@@ -1288,7 +1241,7 @@
     rows, depth = inputs[0].shape
     width = dz[0].shape[1]
     count = a_t.shape[0] // RANK
-    step = 2 * HD
+    step = width // count
     columns = lambda height: pl.BlockSpec((height, step), lambda i: (0, i))
     fixed = lambda x: pl.BlockSpec(x.shape, lambda i: (0, 0))
     return pl.pallas_call(
@@ -1386,29 +1339,28 @@
 def pack_kernel(plan, scalars, *refs):
     out_ref = refs[-1]
     out_ref[...] = jnp.zeros_like(out_ref)
-    row = 0
-    for ref, (parts, placed) in zip(refs[:-1], plan):
+    for ref, (parts, placed, rows) in zip(refs[:-1], plan):
         height, width = ref.shape
         wide = width // parts
-        short = -height % RANK
         lanes = slice(0, wide)
         if placed:
             lanes = pl.ds(pl.multiple_of(scalars[0] * wide, HD), wide)
         if height == 1:
             value = [ref[:, i * wide : (i + 1) * wide].astype(f32) for i in range(parts)]
             value.append(jnp.zeros((RANK - parts, wide), f32))
-            out_ref[row : row + RANK, lanes] = jnp.concatenate(value, axis=0).astype(bf16)
-            row += RANK
-        else:
-            for i in range(parts):
-                value = ref[:, i * wide : (i + 1) * wide].astype(bf16)
-                out_ref[row : row + height, lanes] = value
-                row += height
+            value = jnp.concatenate(value, axis=0).astype(bf16)
+            out_ref[rows[0] : rows[0] + RANK, lanes] = value
+            continue
+        for i in range(parts):
+            for j in range(height // RANK):
+                row = rows[i * (height // RANK) + j]
+                value = ref[j * RANK : (j + 1) * RANK, i * wide : (i + 1) * wide].astype(bf16)
+                out_ref[row : row + RANK, lanes] = value
 
 
 def pack(k, height, width, *entries):
-    arrays = [x for x, _, _ in entries]
-    plan = [(parts, placed) for _, parts, placed in entries]
+    arrays = [entry[0] for entry in entries]
+    plan = [entry[1:] for entry in entries]
     return pl.pallas_call(
         functools.partial(pack_kernel, plan),
         grid_spec=pltpu.PrefetchScalarGridSpec(
@@ -1452,8 +1404,7 @@
     return lax.rsqrt(jnp.mean(values * values, axis=-1, keepdims=True) + EPS)
 
 
-def rms_backward(values, gain_vec, grad_in):
-    inverse = inverse_rms(values)
+def rms_backward(values, gain_vec, grad_in, inverse):
     scaled = grad_in * gain_vec
     return inverse * scaled - values * inverse * inverse * inverse * jnp.mean(
         values * scaled, axis=-1, keepdims=True
@@ -1605,7 +1556,7 @@
         line_step(*lines, step)
     gathered_chunks = [line_blocks(*lines)]
     for c in range(1, chunks):
-        (near_next,) = after([near_chunks[c]], *gathered_chunks[0])
+        (near_next,) = after([near_chunks[c]], wo_all, *gathered_chunks[0])
         others = lax.all_gather(near_next, "mp", axis=0)
         gathered_chunks.append(
             [near_chunks[c]]
@@ -1622,19 +1573,21 @@
         gathered = gathered_chunks[c]
         if c > 0:
             gathered = after(gathered, dh_chunks[-1])
-        hnorm, resid, raw_out, out_low, own = out_project(
+        hnorm, resid, raw_out, out_low, own, act, dz_gu, g, dh = block(
             k_scalar,
             c,
             gathered,
-            wo_all,
             a_out_low,
             hid_view,
             (SCALING * b_out).astype(bf16),
             scale_out,
             gain_mlp[None, :],
-        )
-        act, dz_gu, g, dh = feed_forward(
-            c, hnorm, cot_view, scale_down, scale_gu, wgu_low, wd_low
+            cot_view,
+            scale_down,
+            scale_gu,
+            wo_all,
+            wgu_low,
+            wd_low,
         )
         g_gu = g_gu + g
         dh_chunks.append(dh)
@@ -1728,16 +1681,6 @@
     result = jnp.concatenate(resid_own, axis=0) + down_own.astype(f32) * scale_down
     hidden_own = lax.dynamic_slice_in_dim(hidden_in, k * share, share, 0).astype(f32)
 
-    early_rows = pack(
-        k_scalar,
-        48,
-        share_b_gu.shape[1],
-        (share_b_gu, 1, False),
-        (pb_down, 1, False),
-        (g_gu, 1, False),
-    )
-    (early_rows,) = after([early_rows], dnormed)
-    early_rows = doc_join(butterfly(doc_halve(early_rows), ["seq"])).astype(f32)
 
     share_a_heads, share_b_heads = layer_shares(
         [normed],
@@ -1751,37 +1694,47 @@
         m_heads,
         column_heads,
     )
-    late = pack(
+    parts = n_doc * peers
+    part_rows = 3 * RANK
+    summed = [(u // 2) * part_rows + (u % 2) * RANK for u in range(2 * parts)]
+    apart = [u * part_rows + 2 * RANK for u in range(parts)]
+    totals = pack(
         k_scalar,
-        256,
+        parts * part_rows,
         width,
-        (share_a_gu, 1, False),
-        (ap_down, 1, False),
-        (cross_out / copies, 1, False),
-        (cross_down / copies, 1, False),
-        (ap_out, 1, False),
-        (jnp.concatenate([g_down, g_out], axis=1), 2, False),
-        (pb_out, 1, False),
-        (share_a_heads, 1, False),
-        (share_b_heads, 3, True),
-        (g_heads, 3, True),
-    )
-    late = spread_join(spread_sum(doc_halve(late), peers, ["mp"]), peers)
-    (late,) = after([late], dnormed_own)
-    late = doc_join(late).astype(f32)
-    early, late = late[:128], late[128:]
-    late_columns = late[3 * RANK : 7 * RANK]
-    late_own = lax.dynamic_slice_in_dim(late_columns, k * near_width, near_width, 1)
+        (share_a_gu, 1, False, summed[0:2]),
+        (ap_down, 1, False, summed[2:3]),
+        (cross_out / copies, 1, False, summed[3:4]),
+        (cross_down / copies, 1, False, summed[4:5]),
+        (ap_out, 1, False, summed[5:6]),
+        (jnp.concatenate([g_down, g_out], axis=1), 2, False, summed[6:7]),
+        (pb_out, 1, False, summed[7:8]),
+        (share_a_heads, 1, False, summed[8:11]),
+        (share_b_heads, 3, True, summed[11:14]),
+        (g_heads, 3, True, summed[14:15]),
+        (share_b_gu, 2, False, apart[0:2]),
+        (pb_down, 1, False, apart[2:3]),
+        (g_gu, 2, False, apart[3:4]),
+    )
+    totals = spread_join(spread_sum(doc_halve(totals), peers, ["mp"], 2 * RANK), peers)
+    hidden_inverse = inverse_rms(hidden_own)
+    (totals,) = after([totals], dnormed_own, result, hidden_inverse)
+    totals = doc_join(totals).astype(f32)
+
+    def unit(index, rows=RANK):
+        return totals[summed[index] : summed[index] + rows]
+
+    def own_columns(values):
+        return lax.dynamic_slice_in_dim(values, k * near_width, near_width, 1)
+
+    def unit_apart(index, rows=RANK):
+        return totals[apart[index] : apart[index] + rows, : w_gate.shape[1]]
 
     grad_input = dresid_own + rms_backward(
-        hidden_own, gain_attn, dnormed_own.astype(f32)
-    )
-
-    def rank_rows(array, index):
-        return array[index * RANK : (index + 1) * RANK]
-
-    ff = w_gate.shape[1]
-    total_g_down, total_g_out = early[96:97], early[97:98]
+        hidden_own, gain_attn, dnormed_own.astype(f32), hidden_inverse
+    )
+
+    total_g_down, total_g_out = unit(6, 2)[:1], unit(6, 2)[1:]
     shrink_out = total_g_out * m_out / (column_out * column_out * column_out)
     shrink_down = total_g_down * m_down / (column_down * column_down * column_down)
     turned_out = (b_out * shrink_out).astype(bf16)
@@ -1789,35 +1742,37 @@
         dot_nt(turned_out, b_out.astype(bf16)), a_out.T
     )
     radial_down = dot_nt((b_down * shrink_down).astype(bf16), wd_low)
-    pb_out = lax.dynamic_slice_in_dim(early[112:128], k * near_width, near_width, 1)
-    grad_a_out = SCALING * (pb_out - radial_out)
-    grad_a_down = SCALING * (early_rows[16:32, :ff] - radial_down)
-    grad_b_out = SCALING * (rank_rows(early, 5) - rank_rows(early, 3) * shrink_out)
-    grad_b_down = SCALING * (rank_rows(early, 2) - rank_rows(early, 4) * shrink_down)
-
-    g_rows = late_own[3 * RANK : 3 * RANK + 3].reshape(1, -1) / column_heads
-    g_rows = [g_rows[0, i * near_width : (i + 1) * near_width] for i in range(3)]
-    grad_m_gate, grad_m_up = separate(early_rows[32:33] / column_gu)
-    grad_b_gate, grad_b_up = separate(early_rows[:16])
+    grad_a_out = SCALING * (own_columns(unit(7)) - radial_out)
+    grad_a_down = SCALING * (unit_apart(2) - radial_down)
+    grad_b_out = SCALING * (unit(5) - unit(3) * shrink_out)
+    grad_b_down = SCALING * (unit(2) - unit(4) * shrink_down)
+    g_rows = own_columns(unit(14, 3))
+    g_rows = [
+        g_rows[i] / column_heads[0, i * near_width : (i + 1) * near_width] for i in range(3)
+    ]
+    both = jnp.concatenate([unit_apart(0), unit_apart(1)], axis=1)
+    g_both = jnp.concatenate([unit_apart(3, 2)[:1], unit_apart(3, 2)[1:]], axis=1)
+    grad_m_gate, grad_m_up = separate(g_both / column_gu)
+    grad_b_gate, grad_b_up = separate(both)
     return (
         result,
         grad_input,
-        rank_rows(late, 2).T,
-        rank_rows(late_own, 2),
+        unit(10).T,
+        own_columns(unit(13)),
         g_rows[2],
-        rank_rows(late, 0).T,
-        rank_rows(late_own, 0),
+        unit(8).T,
+        own_columns(unit(11)),
         g_rows[0],
-        rank_rows(late, 1).T,
-        rank_rows(late_own, 1),
+        unit(9).T,
+        own_columns(unit(12)),
         g_rows[1],
         grad_a_out.T,
         grad_b_out,
         (total_g_out / column_out)[0],
-        rank_rows(early, 0).T,
+        unit(0).T,
         grad_b_gate,
         grad_m_gate[0],
-        rank_rows(early, 1).T,
+        unit(1).T,
         grad_b_up,
         grad_m_up[0],
         grad_a_down.T,

time: 465 us -> 458 us (0.985)
  Pallas kernels: 231 us -> 204 us
  waiting for transfers between devices: 108 us -> 132 us
    pallas_call x4 -> x2, Pallas kernels: 71.1 us -> 49.7 us  [block(): pl.pallas_call(functools.partial(block_kernel, sizes, size), grid_spec=pl...]
    ppermute x6, waiting for transfers between devices: 8.12 us -> 26.1 us  [per_device(): arrived.append(lax.ppermute(dattn[shift], 'mp', pairs))]
    reduce_scatter x4, waiting for transfers between devices: 14.3 us -> 4.25 us  [scatter(): return lax.psum_scatter(parts, 'mp', scatter_dimension=0, tiled=True)]
    ppermute x29 -> x25, waiting for transfers between devices: 61.3 us -> 70.3 us  [swap(): return lax.ppermute(value, axis, [(i, i ^ distance) for i in range(size)])]
    all_gather x1, waiting for transfers between devices: 0.02 us -> 7.46 us  [per_device(): others = lax.all_gather(near_next, 'mp', axis=0)]
    ppermute x29 -> x25, starting transfers between devices: 29.7 us -> 26 us  [swap(): return lax.ppermute(value, axis, [(i, i ^ distance) for i in range(size)])]
    unnamed x135 -> x125, local copies, waits for them, and re-layouts: 9.61 us -> 7.62 us
  transfers between devices with their start and end apart: 47 -> 43, of which waited for: 22 -> 24; matrix products, arithmetic and copies ran while one was open for 8% -> 8% of each run, Pallas kernels for 49% -> 43%
where the time goes in v1:
time: 458 us; the launch traced here: 450 us
  Pallas kernels  204 us (45%)
  waiting for transfers between devices  132 us (29%)
  starting transfers between devices  44.3 us (10%)
  other arithmetic  27.1 us (6%)
  local copies, waits for them, and re-layouts  23.1 us (5%)
  between operations  15.3 us (3%)
    ppermute x25, waiting for transfers between devices, swap(): return lax.ppermute(value, axis, [(i, i ^ distance) for i in range(size)])  70.3 us
    pallas_call x2, Pallas kernels, block(): pl.pallas_call(functools.partial(block_kernel, sizes, size), grid_spec=pl...  49.7 us
    ppermute x6, waiting for transfers between devices, per_device(): arrived.append(lax.ppermute(dattn[shift], 'mp', pairs))  26.1 us
    ppermute x25, starting transfers between devices, swap(): return lax.ppermute(value, axis, [(i, i ^ distance) for i in range(size)])  26 us
    pallas_call x1, Pallas kernels, attention_backward(): pl.pallas_call(functools.partial(body, meta), grid_spec=pltpu.PrefetchSca...  24.2 us
    pallas_call x2, Pallas kernels, layer_shares(): pl.pallas_call(functools.partial(shares_kernel, count, chunks, span), gri...  24.1 us
    pallas_call x1, Pallas kernels, merge_others(): pl.pallas_call(functools.partial(merge_kernel, starts), grid=(starts[1] +...  21.1 us
    ppermute x3, waiting for transfers between devices, line_step(): lefts.append(lax.ppermute(left, 'mp', left_pairs))  19 us
  transfers between devices with their start and end apart: 43, of which 24 were waited for; matrix products, arithmetic and copies ran while one was open for 8% of the time, Pallas kernels for 43%

profile of v1, /device:TPU:0, one launch (start us, length us, event | category | flops | bytes accessed | tf_op | source)
XLA Modules:
  0.0 449.9 jit_solution(9367657460790231084)
XLA Ops:
  19.3 18.6 %project_heads.1 = (bf16[3,768,128]{2,1,0:T(8,128)(2,1)}, bf16[3,768,128]{2,1,0:T(8,128)(2,1)}, bf16[3,768,128]{2,1,0:T(8,128)(2,1)}, bf16[3,768,128]{2,1,0:T(8,...) custom-call(s32[1]{0:T(128)} %bitcast.1.scalars, ...), custom_call_target="tpu_custom_call" | custom-call | flops 1 | bytes 1 | tf_op jit(solution)/shard_map/project_heads/pallas_call | solution.py:785
  44.3 21.1 %merge_others.1 = (f32[1,2048]{1,0:T(1,128)}, f32[16,2048]{1,0:T(8,128)}, f32[1,2048]{1,0:T(1,128)}, f32[16,2048]{1,0:T(8,128)}, bf16[1408,2048]{1,0:T(8,128)(2,...) custom-call(bf16[512,2048]{1,0:T(8,128)(2,1)} %out_w, ...), custom_call_target="tpu_custom_call" | custom-call | flops 1 | bytes 1 | tf_op jit(solution)/shard_map/merge_others/pallas_call | solution.py:644
  69.4 17.5 %attend.1 = (bf16[768,128]{1,0:T(8,128)(2,1)}, bf16[768,128]{1,0:T(8,128)(2,1)}, bf16[768,128]{1,0:T(8,128)(2,1)}, bf16[768,128]{1,0:T(8,128)(2,1)}, f32[4,1,768]{2,1,0:T(1,128)}) custom-call(s32[17]{0:T(128)} %pad_add_fusion.scalars, bf16[3,768,128]{2,1,0:T(8,128)(2,1)} %get-tuple-element.139.refs_0_, bf16[3,768,128]{2,1,0:T(8,128)(2,1)} %copy-done.5, ...), custom_call_target="tpu_custom_call" | custom-call | flops 1 | bytes 1 | tf_op jit(solution)/shard_map/attend/pallas_call | solution.py:391
  90.4 4.3 collective-permute-done.6.refs_1_
  106.2 5.3 %collective-permute-done.10 = bf16[416,512]{1,0:T(8,128)(2,1)S(1)} collective-permute-done((bf16[416,512]{1,0:T(8,128)(2,1)}, bf16[416,512]{1,0:T(8,128)(2,1)S(1)}, u32[]{:S(2)}, u32[]{:S(2)}) %collective-permute-start.10) | collective-permute-done | bytes 426016 | tf_op jit(solution)/shard_map/ppermute | solution.py:113
  117.5 8.5 %collective-permute-done.13 = bf16[416,512]{1,0:T(8,128)(2,1)S(1)} collective-permute-done((bf16[416,512]{1,0:T(8,128)(2,1)S(1)}, bf16[416,512]{1,0:T(8,128)(2,1)S(1)}, u32[]{:S(2)}, u32[]{:S(2)}) %collective-permute-start.13) | collective-permute-done | bytes 426016 | tf_op jit(solution)/shard_map/ppermute | solution.py:114
  129.0 7.1 %collective-permute-done.14 = bf16[416,512]{1,0:T(8,128)(2,1)S(1)} collective-permute-done((bf16[416,512]{1,0:T(8,128)(2,1)S(1)}, bf16[416,512]{1,0:T(8,128)(2,1)S(1)}, u32[]{:S(2)}, u32[]{:S(2)}) %collective-permute-start.14) | collective-permute-done | bytes 426016 | tf_op jit(solution)/shard_map/ppermute | solution.py:114
  139.5 24.8 %block.2 = (bf16[384,2048]{1,0:T(8,128)(2,1)}, f32[96,2048]{1,0:T(8,128)}, f32[96,2048]{1,0:T(8,128)}, bf16[96,16]{1,0:T(8,128)(2,1)}, bf16[96,2048]{1,0:T(8,128...) custom-call(s32[1]{0:T(128)} %bitcast.scalars, ...), custom_call_target="tpu_custom_call" | custom-call | flops 1 | bytes 1 | tf_op jit(solution)/shard_map/block/pallas_call | solution.py:1027
  164.6 7.5 %all-gather.6.cloned.1.call-done = bf16[1536,512]{1,0:T(8,128)(2,1)} async-done(((bf16[384,512]{1,0:T(8,128)(2,1)}), bf16[1536,512]{1,0:T(8,128)(2,1)}) %all-gather.6.cloned.1.call-update) | async-done | bytes 1572880 | tf_op jit(solution)/shard_map/all_gather | solution.py:1560
  174.4 24.9 %block.3 = (bf16[384,2048]{1,0:T(8,128)(2,1)}, f32[96,2048]{1,0:T(8,128)}, f32[96,2048]{1,0:T(8,128)}, bf16[96,16]{1,0:T(8,128)(2,1)}, bf16[96,2048]{1,0:T(8,128...) custom-call(s32[1]{0:T(128)} %bitcast.scalars, ...), custom_call_target="tpu_custom_call" | custom-call | flops 1 | bytes 1 | tf_op jit(solution)/shard_map/block/pallas_call | solution.py:1027
  201.4 13.1 %down_project.1 = (bf16[4,2,96,2048]{3,2,1,0:T(8,128)(2,1)}, f32[1,2048]{1,0:T(1,128)}, bf16[16,2048]{1,0:T(8,128)(2,1)}, bf16[16,1408]{1,0:T(8,128)(2,1)}) custom-call(bf16[384,1408]{1,0:T(8,128)(2,1)} %get-tuple-element.166.refs_0_, bf16[384,1408]{1,0:T(8,128)(2,1)} %get-tuple-element.167.refs_1_, bf16[1408,2048]{1,0:T(8,128)(2,1)} %get-tuple-element.154.refs_14_.refs_2_, ...), custom_call_target="tpu_custom_call" | custom-call | flops 1 | bytes 1 | tf_op jit(solution)/shard_map/down_project/pallas_call | solution.py:1317
  214.5 8.7 %back_out.2 = (bf16[4,96,512]{2,1,0:T(8,128)(2,1)}, f32[96,2048]{1,0:T(8,128)}, bf16[96,2048]{1,0:T(8,128)(2,1)}, f32[1,2048]{1,0:T(1,128)}, f32[16,2048]{1,0:T(8,128)}, /*index=5*/f32[16,2048]{1,0:T(8,128)}) custom-call(s32[1]{0:T(128)} %bitcast.scalars, bf16[96,2048]{1,0:T(8,128)(2,1)} %reduce-scatter.5.cloned.1.call-done.refs_0_, ...), custom_call_target="tpu_custom_call" | custom-call | flops 1 | bytes 1 | tf_op jit(solution)/shard_map/back_out/pallas_call | solution.py:1102
  229.0 5.0 %collective-permute-done.15 = bf16[96,512]{1,0:T(8,128)(2,1)S(1)} collective-permute-done((bf16[96,512]{1,0:T(8,128)(2,1)S(1)}, bf16[96,512]{1,0:T(8,128)(2,1)S(1)}, u32[]{:S(2)}, u32[]{:S(2)}) %collective-permute-start.15) | collective-permute-done | bytes 98336 | tf_op jit(solution)/shard_map/ppermute | solution.py:1631
  234.0 13.6 %collective-permute-done.16 = bf16[96,512]{1,0:T(8,128)(2,1)S(1)} collective-permute-done((bf16[96,512]{1,0:T(8,128)(2,1)S(1)}, bf16[96,512]{1,0:T(8,128)(2,1)S(1)}, u32[]{:S(2)}, u32[]{:S(2)}) %collective-permute-start.16) | collective-permute-done | bytes 98336 | tf_op jit(solution)/shard_map/ppermute | solution.py:1631
  251.9 8.4 %back_out.3 = (bf16[4,96,512]{2,1,0:T(8,128)(2,1)}, f32[96,2048]{1,0:T(8,128)}, bf16[96,2048]{1,0:T(8,128)(2,1)}, f32[1,2048]{1,0:T(1,128)}, f32[16,2048]{1,0:T(8,128)}, /*index=5*/f32[16,2048]{1,0:T(8,128)}) custom-call(s32[1]{0:T(128)} %bitcast.scalars, f32[1,2048]{1,0:T(1,128)} %get-tuple-element.175.refs_0_, f32[16,2048]{1,0:T(8,128)} %get-tuple-element.176.refs_1_, ...), custom_call_target="tpu_custom_call" | custom-call | flops 1 | bytes 1 | tf_op jit(solution)/shard_map/back_out/pallas_call | solution.py:1102
  268.9 5.3 %collective-permute-done.19 = bf16[96,512]{1,0:T(8,128)(2,1)S(1)} collective-permute-done((bf16[96,512]{1,0:T(8,128)(2,1)S(1)}, bf16[96,512]{1,0:T(8,128)(2,1)S(1)}, u32[]{:S(2)}, u32[]{:S(2)}) %collective-permute-start.19) | collective-permute-done | bytes 98336 | tf_op jit(solution)/shard_map/ppermute | solution.py:1631
  286.7 24.2 %attend_back.1 = (bf16[3,768,128]{2,1,0:T(8,128)(2,1)}, bf16[3,768,128]{2,1,0:T(8,128)(2,1)}, bf16[3,768,128]{2,1,0:T(8,128)(2,1)}, bf16[3,768,128]{2,1,0:T(8,128)(2,1)}) custom-call(s32[17]{0:T(128)} %pad_add_fusion.scalars, bf16[3,768,128]{2,1,0:T(8,128)(2,1)} %get-tuple-element.139.refs_0_, bf16[3,768,128]{2,1,0:T(8,128)(2,1)} %copy-done.5, ...), custom_call_target="tpu_custom_call" | custom-call | flops 1 | bytes 1 | tf_op jit(solution)/shard_map/attend_back/pallas_call | solution.py:522
  316.3 14.0 %shares.2 = (bf16[32,2048]{1,0:T(8,128)(2,1)}, bf16[16,2816]{1,0:T(8,128)(2,1)}) custom-call(bf16[384,2048]{1,0:T(8,128)(2,1)} %get-tuple-element.196.refs_0_, bf16[384,2048]{1,0:T(8,128)(2,1)} %get-tuple-element.197.refs_1_, bf16[384,2816]{1,0:T(8,128)(2,1)} %get-tuple-element.198.refs_2_, bf16[384,2816]{1,0:T(8,128)(2,1)} %get-tuple-element.199.refs_3_, ...), custom_call_target="tpu_custom_call" | custom-call | flops 1 | bytes 1 | tf_op jit(solution)/shard_map/shares/pallas_call | solution.py:1247
  330.4 8.0 %collective-permute-done.25.refs_2_ = bf16[3,768,128]{2,1,0:T(8,128)(2,1)S(1)} collective-permute-done((bf16[3,768,128]{2,1,0:T(8,128)(2,1)}, bf16[3,768,128]{2,1,0:T(8,128)(2,1)S(1)}, u32[]{:S(2)}, u32[]{:S(2)}) %collective-permute-start.25) | collective-permute-done | bytes 589856 | tf_op jit(solution)/shard_map/ppermute | solution.py:52
  339.3 12.2 %unproject.1 = (bf16[768,1536]{1,0:T(8,128)(2,1)}, f32[1,1536]{1,0:T(1,128)}, bf16[768,2048]{1,0:T(8,128)(2,1)}) custom-call(s32[1]{0:T(128)} %bitcast.1.scalars, f32[768,128]{1,0:T(8,128)} %get-tuple-element.286.cos_ref, f32[768,128]{1,0:T(8,128)} %get-tuple-element.285.sin_ref, bf16[768,1536]{1,0:T(8,128)(2,1)} %get-tuple-element.133.raw_ref, ...), custom_call_target="tpu_custom_call" | custom-call | flops 1 | bytes 1 | tf_op jit(solution)/shard_map/unproject/pallas_call | solution.py:1171
  354.2 10.1 %shares.3 = (bf16[48,2048]{1,0:T(8,128)(2,1)}, bf16[16,1536]{1,0:T(8,128)(2,1)}) custom-call(bf16[768,2048]{1,0:T(8,128)(2,1)} %get-tuple-element.221.refs_0_, bf16[768,1536]{1,0:T(8,128)(2,1)} %get-tuple-element.222.refs_1_, bf16[48,2048]{1,0:T(8,128)(2,1)} %bitcast.131, f32[16,1536]{1,0:T(8,128)} %pad_maximum_fusion.6.refs_3_, ...), custom_call_target="tpu_custom_call" | custom-call | flops 1 | bytes 1 | tf_op jit(solution)/shard_map/shares/pallas_call | solution.py:1247
  378.7 4.5 %collective-permute-done.30 = bf16[48,2048]{1,0:T(8,128)(2,1)S(1)} collective-permute-done((bf16[48,2048]{1,0:T(8,128)(2,1)S(1)}, bf16[48,2048]{1,0:T(8,128)(2,1)S(1)}, u32[]{:S(2)}, u32[]{:S(2)}) %collective-permute-start.30) | collective-permute-done | bytes 196640 | tf_op jit(solution)/shard_map/ppermute | solution.py:52
  384.8 11.4 %collective-permute-done.31 = bf16[32,2048]{1,0:T(8,128)(2,1)S(1)} collective-permute-done((bf16[32,2048]{1,0:T(8,128)(2,1)S(1)}, bf16[32,2048]{1,0:T(8,128)(2,1)S(1)}, u32[]{:S(2)}, u32[]{:S(2)}) %collective-permute-start.31) | collective-permute-done | bytes 131104 | tf_op jit(solution)/shard_map/ppermute | solution.py:52
  396.3 17.6 %collective-permute-done.32 = bf16[32,2048]{1,0:T(8,128)(2,1)S(1)} collective-permute-done((bf16[32,2048]{1,0:T(8,128)(2,1)S(1)}, bf16[32,2048]{1,0:T(8,128)(2,1)S(1)}, u32[]{:S(2)}, u32[]{:S(2)}) %collective-permute-start.32) | collective-permute-done | bytes 131104 | tf_op jit(solution)/shard_map/ppermute | solution.py:52
  (285 shorter events, 139.0 us)
Async XLA Ops:
  7.2 129.7 %all-gather.4.cloned.1.call-start = ((), (), s32[]{:S(2)}) async-start(), calls=%async_computation.4 | async-start | bytes 9437184 | tf_op jit(solution)/shard_map/all_gather | solution.py:1473
  9.8 162.3 %all-gather.6.cloned.1.call-start = ((), (), s32[]{:S(2)}) async-start(), calls=%async_computation.9 | async-start | bytes 1966080 | tf_op jit(solution)/shard_map/all_gather | solution.py:1560
  37.8 30.3 %collective-permute-start.3 = (bf16[3,768,128]{2,1,0:T(8,128)(2,1)}, bf16[3,768,128]{2,1,0:T(8,128)(2,1)S(1)}, u32[]{:S(2)}, u32[]{:S(2)}) collective-permute-start(bf16[3,768,128]{2,1,0:T(8,128)(2,1)} %get-tuple-element.130), channel_id=1, source_target_pairs={{0,4},{4,0},{8,12},{12,8},{1,5},{5,1},{9,13},{13,9},{2,6},{6,2},{1... | collective-permute-start | bytes 1769480 | tf_op jit(solution)/shard_map/ppermute | solution.py:52
  39.8 28.4 %collective-permute-start.4 = (bf16[3,768,128]{2,1,0:T(8,128)(2,1)}, bf16[3,768,128]{2,1,0:T(8,128)(2,1)S(1)}, u32[]{:S(2)}, u32[]{:S(2)}) collective-permute-start(bf16[3,768,128]{2,1,0:T(8,128)(2,1)} %get-tuple-element.131), channel_id=1, source_target_pairs={{0,8},{4,12},{8,0},{12,4},{1,9},{5,13},{9,1},{13,5},{2,10},{6,14},... | collective-permute-start | bytes 1769480 | tf_op jit(solution)/shard_map/ppermute | solution.py:52
  41.3 26.9 %collective-permute-start.5 = (bf16[3,768,128]{2,1,0:T(8,128)(2,1)}, bf16[3,768,128]{2,1,0:T(8,128)(2,1)S(1)}, u32[]{:S(2)}, u32[]{:S(2)}) collective-permute-start(bf16[3,768,128]{2,1,0:T(8,128)(2,1)} %get-tuple-element.132), channel_id=1, source_target_pairs={{0,12},{4,8},{8,4},{12,0},{1,13},{5,9},{9,5},{13,1},{2,14},{6,10},... | collective-permute-start | bytes 1769480 | tf_op jit(solution)/shard_map/ppermute | solution.py:52
  101.5 10.0 %collective-permute-start.10 = (bf16[416,512]{1,0:T(8,128)(2,1)}, bf16[416,512]{1,0:T(8,128)(2,1)S(1)}, u32[]{:S(2)}, u32[]{:S(2)}) collective-permute-start(bf16[416,512]{1,0:T(8,128)(2,1)} %get-tuple-element.148.refs_0_), channel_id=1, source_target_pairs={{0,1},{1,2},{2,3},{4,5},{5,6},{6,7},{8,9},{9,10},{10,11},{12,13},{... | collective-permute-start | bytes 1277960 | tf_op jit(solution)/shard_map/ppermute | solution.py:113
  104.9 10.6 %collective-permute-start.9 = (bf16[416,512]{1,0:T(8,128)(2,1)}, bf16[416,512]{1,0:T(8,128)(2,1)S(1)}, u32[]{:S(2)}, u32[]{:S(2)}) collective-permute-start(bf16[416,512]{1,0:T(8,128)(2,1)} %get-tuple-element.148.refs_0_), channel_id=1, source_target_pairs={{1,0},{2,1},{3,2},{5,4},{6,5},{7,6},{9,8},{10,9},{11,10},{13,12},{... | collective-permute-start | bytes 1277960 | tf_op jit(solution)/shard_map/ppermute | solution.py:114
  115.5 10.5 %collective-permute-start.13 = (bf16[416,512]{1,0:T(8,128)(2,1)S(1)}, bf16[416,512]{1,0:T(8,128)(2,1)S(1)}, u32[]{:S(2)}, u32[]{:S(2)}) collective-permute-start(bf16[416,512]{1,0:T(8,128)(2,1)S(1)} %collective-permute-done.9), channel_id=1, source_target_pairs={{1,0},{2,1},{5,4},{6,5},{9,8},{10,9},{13,12},{14,13},{17,16},{18,1... | collective-permute-start | bytes 1277960 | tf_op jit(solution)/shard_map/ppermute | solution.py:114
  116.8 11.3 %collective-permute-start.12 = (bf16[416,512]{1,0:T(8,128)(2,1)S(1)}, bf16[416,512]{1,0:T(8,128)(2,1)S(1)}, u32[]{:S(2)}, u32[]{:S(2)}) collective-permute-start(bf16[416,512]{1,0:T(8,128)(2,1)S(1)} %collective-permute-done.11), channel_id=1, source_target_pairs={{2,3},{6,7},{10,11},{14,15},{18,19},{22,23},{26,27},{30,31}} | collective-permute-start | bytes 1277960 | tf_op jit(solution)/shard_map/ppermute | solution.py:113
  126.0 10.0 %collective-permute-start.14 = (bf16[416,512]{1,0:T(8,128)(2,1)S(1)}, bf16[416,512]{1,0:T(8,128)(2,1)S(1)}, u32[]{:S(2)}, u32[]{:S(2)}) collective-permute-start(bf16[416,512]{1,0:T(8,128)(2,1)S(1)} %collective-permute-done.13), channel_id=1, source_target_pairs={{1,0},{5,4},{9,8},{13,12},{17,16},{21,20},{25,24},{29,28}} | collective-permute-start | bytes 1277960 | tf_op jit(solution)/shard_map/ppermute | solution.py:114
  136.9 77.6 %reduce-scatter.5.cloned.1.call-start = ((), (), s32[]{:S(2)}) async-start(), calls=%async_computation.5 | async-start | bytes 1966080 | tf_op jit(solution)/shard_map/reduce_scatter | solution.py:1603
  164.4 87.5 %reduce-scatter.7.cloned.1.call-start = ((), (), s32[]{:S(2)}) async-start(), calls=%async_computation.6 | async-start | bytes 1966080 | tf_op jit(solution)/shard_map/reduce_scatter | solution.py:1603
  199.3 225.0 %reduce-scatter.9.cloned.1.call-start = ((), (), s32[]{:S(2)}) async-start(), calls=%async_computation.7 | async-start | bytes 3932160 | tf_op jit(solution)/shard_map/reduce_scatter | solution.py:1603
  224.2 9.8 %collective-permute-start.15 = (bf16[96,512]{1,0:T(8,128)(2,1)S(1)}, bf16[96,512]{1,0:T(8,128)(2,1)S(1)}, u32[]{:S(2)}, u32[]{:S(2)}) collective-permute-start(bf16[96,512]{1,0:T(8,128)(2,1)S(1)} %get-tuple-element.279), channel_id=1, source_target_pairs={{0,1},{1,2},{2,3},{3,0},{4,5},{5,6},{6,7},{7,4},{8,9},{9,10},{10,1... | collective-permute-start | bytes 294920 | tf_op jit(solution)/shard_map/ppermute | solution.py:1631
  225.3 22.3 %collective-permute-start.17 = (bf16[96,512]{1,0:T(8,128)(2,1)S(1)}, bf16[96,512]{1,0:T(8,128)(2,1)S(1)}, u32[]{:S(2)}, u32[]{:S(2)}) collective-permute-start(bf16[96,512]{1,0:T(8,128)(2,1)S(1)} %get-tuple-element.277), channel_id=1, source_target_pairs={{0,3},{1,0},{2,1},{3,2},{4,7},{5,4},{6,5},{7,6},{8,11},{9,8},{10,9... | collective-permute-start | bytes 294920 | tf_op jit(solution)/shard_map/ppermute | solution.py:1631
  229.0 18.7 %collective-permute-start.16 = (bf16[96,512]{1,0:T(8,128)(2,1)S(1)}, bf16[96,512]{1,0:T(8,128)(2,1)S(1)}, u32[]{:S(2)}, u32[]{:S(2)}) collective-permute-start(bf16[96,512]{1,0:T(8,128)(2,1)S(1)} %get-tuple-element.278), channel_id=1, source_target_pairs={{0,2},{1,3},{2,0},{3,1},{4,6},{5,7},{6,4},{7,5},{8,10},{9,11},{10,... | collective-permute-start | bytes 294920 | tf_op jit(solution)/shard_map/ppermute | solution.py:1631
  286.7 140.8 %reduce-scatter.11.cloned.1.call-start = ((), (), s32[]{:S(2)}) async-start(), calls=%async_computation.8 | async-start | bytes 3932160 | tf_op jit(solution)/shard_map/reduce_scatter | solution.py:1603
  310.8 19.5 %collective-permute-start.24 = (bf16[3,768,128]{2,1,0:T(8,128)(2,1)}, bf16[3,768,128]{2,1,0:T(8,128)(2,1)S(1)}, u32[]{:S(2)}, u32[]{:S(2)}) collective-permute-start(bf16[3,768,128]{2,1,0:T(8,128)(2,1)} %get-tuple-element.189), channel_id=1, source_target_pairs={{0,4},{4,0},{8,12},{12,8},{1,5},{5,1},{9,13},{13,9},{2,6},{6,2},{1... | collective-permute-start | bytes 1769480 | tf_op jit(solution)/shard_map/ppermute | solution.py:52
  312.3 26.0 %collective-permute-start.25 = (bf16[3,768,128]{2,1,0:T(8,128)(2,1)}, bf16[3,768,128]{2,1,0:T(8,128)(2,1)S(1)}, u32[]{:S(2)}, u32[]{:S(2)}) collective-permute-start(bf16[3,768,128]{2,1,0:T(8,128)(2,1)} %get-tuple-element.190), channel_id=1, source_target_pairs={{0,8},{4,12},{8,0},{12,4},{1,9},{5,13},{9,1},{13,5},{2,10},{6,14},... | collective-permute-start | bytes 1769480 | tf_op jit(solution)/shard_map/ppermute | solution.py:52
  313.8 24.5 %collective-permute-start.26 = (bf16[3,768,128]{2,1,0:T(8,128)(2,1)}, bf16[3,768,128]{2,1,0:T(8,128)(2,1)S(1)}, u32[]{:S(2)}, u32[]{:S(2)}) collective-permute-start(bf16[3,768,128]{2,1,0:T(8,128)(2,1)} %get-tuple-element.191), channel_id=1, source_target_pairs={{0,12},{4,8},{8,4},{12,0},{1,13},{5,9},{9,5},{13,1},{2,14},{6,10},... | collective-permute-start | bytes 1769480 | tf_op jit(solution)/shard_map/ppermute | solution.py:52
  372.0 11.2 %collective-permute-start.30 = (bf16[48,2048]{1,0:T(8,128)(2,1)S(1)}, bf16[48,2048]{1,0:T(8,128)(2,1)S(1)}, u32[]{:S(2)}, u32[]{:S(2)}) collective-permute-start(bf16[48,2048]{1,0:T(8,128)(2,1)S(1)} %get-tuple-element.268), channel_id=1, source_target_pairs={{0,12},{4,8},{8,4},{12,0},{1,13},{5,9},{9,5},{13,1},{2,14},{6,10},... | collective-permute-start | bytes 589832 | tf_op jit(solution)/shard_map/ppermute | solution.py:52
  374.0 10.6 %collective-permute-start.29 = (bf16[48,2048]{1,0:T(8,128)(2,1)S(1)}, bf16[48,2048]{1,0:T(8,128)(2,1)S(1)}, u32[]{:S(2)}, u32[]{:S(2)}) collective-permute-start(bf16[48,2048]{1,0:T(8,128)(2,1)S(1)} %get-tuple-element.269), channel_id=1, source_target_pairs={{0,8},{4,12},{8,0},{12,4},{1,9},{5,13},{9,1},{13,5},{2,10},{6,14},... | collective-permute-start | bytes 589832 | tf_op jit(solution)/shard_map/ppermute | solution.py:52
  384.7 11.5 %collective-permute-start.31 = (bf16[32,2048]{1,0:T(8,128)(2,1)S(1)}, bf16[32,2048]{1,0:T(8,128)(2,1)S(1)}, u32[]{:S(2)}, u32[]{:S(2)}) collective-permute-start(bf16[32,2048]{1,0:T(8,128)(2,1)S(1)} %slice.192), channel_id=1, source_target_pairs={{0,1},{1,0},{2,3},{3,2},{4,5},{5,4},{6,7},{7,6},{8,9},{9,8},{10,11... | collective-permute-start | bytes 393224 | tf_op jit(solution)/shard_map/ppermute | solution.py:52
  396.2 17.7 %collective-permute-start.32 = (bf16[32,2048]{1,0:T(8,128)(2,1)S(1)}, bf16[32,2048]{1,0:T(8,128)(2,1)S(1)}, u32[]{:S(2)}, u32[]{:S(2)}) collective-permute-start(bf16[32,2048]{1,0:T(8,128)(2,1)S(1)} %slice_add_fusion), channel_id=1, source_target_pairs={{0,2},{1,3},{2,0},{3,1},{4,6},{5,7},{6,4},{7,5},{8,10},{9,11},{10,... | collective-permute-start | bytes 393224 | tf_op jit(solution)/shard_map/ppermute | solution.py:52
  (77 other events, 482.5 us)
Sparse Core Ops, SparseCore 0:
  10.2 84.7 all-gather.3
  137.0 35.0 all-gather.5
  174.4 34.1 reduce-scatter.4
  211.3 40.5 reduce-scatter.6
  286.1 59.1 reduce-scatter.8
  351.7 63.2 reduce-scatter.10

commit v2 on v1

--- a/solution.py
+++ b/solution.py
@@ -1626,6 +1626,7 @@
             out_sums,
         )
         arrived.append(dattn[0])
+        (dattn,) = after([dattn], *pieces)
         for shift in range(1, n_mp):
             pairs = [(i, (i + shift) % n_mp) for i in range(n_mp)]
             arrived.append(lax.ppermute(dattn[shift], "mp", pairs))
@@ -1637,7 +1638,7 @@
             raw_down, g_down, ap_down, pb_down = down_project(
                 acts_next, wd_low, cot_view, scale_down, a_down.T, b_down
             )
-            earlier = (g_down, *arrived[1:])
+            earlier = g_down
     arrived = jnp.concatenate(arrived, axis=0)
     by_head = [arrived[:, h * HD : (h + 1) * HD] for h in range(peers)]
     grad_blocks = seq_exchange([pick_blocks(by_head, me ^ d) for d in range(peers)])

time: 458 us -> 452 us (0.987)
  waiting for transfers between devices: 132 us -> 126 us
    ppermute x6, waiting for transfers between devices: 26.1 us -> 6.59 us  [per_device(): arrived.append(lax.ppermute(dattn[shift], 'mp', pairs))]
    reduce_scatter x4, waiting for transfers between devices: 4.25 us -> 21.6 us  [scatter(): return lax.psum_scatter(parts, 'mp', scatter_dimension=0, tiled=True)]
  transfers between devices with their start and end apart: 43 -> 43, of which waited for: 24 -> 23; matrix products, arithmetic and copies ran while one was open for 8% -> 8% of each run, Pallas kernels for 43% -> 46%
where the time goes in v2:
time: 452 us; the launch traced here: 444 us
  Pallas kernels  203 us (45%)
  waiting for transfers between devices  126 us (28%)
  starting transfers between devices  44.6 us (10%)
  other arithmetic  27.1 us (6%)
  local copies, waits for them, and re-layouts  23.1 us (5%)
  between operations  15.3 us (3%)
    ppermute x25, waiting for transfers between devices, swap(): return lax.ppermute(value, axis, [(i, i ^ distance) for i in range(size)])  66.4 us
    pallas_call x2, Pallas kernels, block(): pl.pallas_call(functools.partial(block_kernel, sizes, size), grid_spec=pl...  49.7 us
    ppermute x25, starting transfers between devices, swap(): return lax.ppermute(value, axis, [(i, i ^ distance) for i in range(size)])  27.7 us
    pallas_call x1, Pallas kernels, attention_backward(): pl.pallas_call(functools.partial(body, meta), grid_spec=pltpu.PrefetchSca...  24.2 us
    pallas_call x2, Pallas kernels, layer_shares(): pl.pallas_call(functools.partial(shares_kernel, count, chunks, span), gri...  23.7 us
    reduce_scatter x4, waiting for transfers between devices, scatter(): return lax.psum_scatter(parts, 'mp', scatter_dimension=0, tiled=True)  21.6 us
    pallas_call x1, Pallas kernels, merge_others(): pl.pallas_call(functools.partial(merge_kernel, starts), grid=(starts[1] +...  21.1 us
    ppermute x3, waiting for transfers between devices, line_step(): lefts.append(lax.ppermute(left, 'mp', left_pairs))  18.9 us
  transfers between devices with their start and end apart: 43, of which 23 were waited for; matrix products, arithmetic and copies ran while one was open for 8% of the time, Pallas kernels for 46%

profile of v2, /device:TPU:0, one launch (start us, length us, event | category | flops | bytes accessed | tf_op | source)
XLA Modules:
  0.0 443.5 jit_solution(16739676759952303231)
XLA Ops:
  19.3 18.6 %project_heads.1 = (bf16[3,768,128]{2,1,0:T(8,128)(2,1)}, bf16[3,768,128]{2,1,0:T(8,128)(2,1)}, bf16[3,768,128]{2,1,0:T(8,128)(2,1)}, bf16[3,768,128]{2,1,0:T(8,...) custom-call(s32[1]{0:T(128)} %bitcast.1.scalars, ...), custom_call_target="tpu_custom_call" | custom-call | flops 1 | bytes 1 | tf_op jit(solution)/shard_map/project_heads/pallas_call | solution.py:785
  44.3 21.1 %merge_others.1 = (f32[1,2048]{1,0:T(1,128)}, f32[16,2048]{1,0:T(8,128)}, f32[1,2048]{1,0:T(1,128)}, f32[16,2048]{1,0:T(8,128)}, bf16[1408,2048]{1,0:T(8,128)(2,...) custom-call(bf16[512,2048]{1,0:T(8,128)(2,1)} %out_w, ...), custom_call_target="tpu_custom_call" | custom-call | flops 1 | bytes 1 | tf_op jit(solution)/shard_map/merge_others/pallas_call | solution.py:644
  69.4 17.5 %attend.1 = (bf16[768,128]{1,0:T(8,128)(2,1)}, bf16[768,128]{1,0:T(8,128)(2,1)}, bf16[768,128]{1,0:T(8,128)(2,1)}, bf16[768,128]{1,0:T(8,128)(2,1)}, f32[4,1,768]{2,1,0:T(1,128)}) custom-call(s32[17]{0:T(128)} %pad_add_fusion.scalars, bf16[3,768,128]{2,1,0:T(8,128)(2,1)} %get-tuple-element.141.refs_0_, bf16[3,768,128]{2,1,0:T(8,128)(2,1)} %copy-done.5, ...), custom_call_target="tpu_custom_call" | custom-call | flops 1 | bytes 1 | tf_op jit(solution)/shard_map/attend/pallas_call | solution.py:391
  90.4 4.3 collective-permute-done.6.refs_1_
  106.2 5.3 %collective-permute-done.10 = bf16[416,512]{1,0:T(8,128)(2,1)S(1)} collective-permute-done((bf16[416,512]{1,0:T(8,128)(2,1)}, bf16[416,512]{1,0:T(8,128)(2,1)S(1)}, u32[]{:S(2)}, u32[]{:S(2)}) %collective-permute-start.10) | collective-permute-done | bytes 426016 | tf_op jit(solution)/shard_map/ppermute | solution.py:113
  117.5 8.5 %collective-permute-done.13 = bf16[416,512]{1,0:T(8,128)(2,1)S(1)} collective-permute-done((bf16[416,512]{1,0:T(8,128)(2,1)S(1)}, bf16[416,512]{1,0:T(8,128)(2,1)S(1)}, u32[]{:S(2)}, u32[]{:S(2)}) %collective-permute-start.13) | collective-permute-done | bytes 426016 | tf_op jit(solution)/shard_map/ppermute | solution.py:114
  128.9 7.1 %collective-permute-done.14 = bf16[416,512]{1,0:T(8,128)(2,1)S(1)} collective-permute-done((bf16[416,512]{1,0:T(8,128)(2,1)S(1)}, bf16[416,512]{1,0:T(8,128)(2,1)S(1)}, u32[]{:S(2)}, u32[]{:S(2)}) %collective-permute-start.14) | collective-permute-done | bytes 426016 | tf_op jit(solution)/shard_map/ppermute | solution.py:114
  139.5 24.8 %block.2 = (bf16[384,2048]{1,0:T(8,128)(2,1)}, f32[96,2048]{1,0:T(8,128)}, f32[96,2048]{1,0:T(8,128)}, bf16[96,16]{1,0:T(8,128)(2,1)}, bf16[96,2048]{1,0:T(8,128...) custom-call(s32[1]{0:T(128)} %bitcast.scalars, ...), custom_call_target="tpu_custom_call" | custom-call | flops 1 | bytes 1 | tf_op jit(solution)/shard_map/block/pallas_call | solution.py:1027
  164.6 7.5 %all-gather.6.cloned.1.call-done = bf16[1536,512]{1,0:T(8,128)(2,1)} async-done(((bf16[384,512]{1,0:T(8,128)(2,1)}), bf16[1536,512]{1,0:T(8,128)(2,1)}) %all-gather.6.cloned.1.call-update) | async-done | bytes 1572880 | tf_op jit(solution)/shard_map/all_gather | solution.py:1560
  174.4 24.9 %block.3 = (bf16[384,2048]{1,0:T(8,128)(2,1)}, f32[96,2048]{1,0:T(8,128)}, f32[96,2048]{1,0:T(8,128)}, bf16[96,16]{1,0:T(8,128)(2,1)}, bf16[96,2048]{1,0:T(8,128...) custom-call(s32[1]{0:T(128)} %bitcast.scalars, ...), custom_call_target="tpu_custom_call" | custom-call | flops 1 | bytes 1 | tf_op jit(solution)/shard_map/block/pallas_call | solution.py:1027
  201.4 13.1 %down_project.1 = (bf16[4,2,96,2048]{3,2,1,0:T(8,128)(2,1)}, f32[1,2048]{1,0:T(1,128)}, bf16[16,2048]{1,0:T(8,128)(2,1)}, bf16[16,1408]{1,0:T(8,128)(2,1)}) custom-call(bf16[384,1408]{1,0:T(8,128)(2,1)} %get-tuple-element.168.refs_0_, bf16[384,1408]{1,0:T(8,128)(2,1)} %get-tuple-element.169.refs_1_, bf16[1408,2048]{1,0:T(8,128)(2,1)} %get-tuple-element.156.refs_14_.refs_2_, ...), custom_call_target="tpu_custom_call" | custom-call | flops 1 | bytes 1 | tf_op jit(solution)/shard_map/down_project/pallas_call | solution.py:1317
  214.5 8.7 %back_out.2 = (bf16[4,96,512]{2,1,0:T(8,128)(2,1)}, f32[96,2048]{1,0:T(8,128)}, bf16[96,2048]{1,0:T(8,128)(2,1)}, f32[1,2048]{1,0:T(1,128)}, f32[16,2048]{1,0:T(8,128)}, /*index=5*/f32[16,2048]{1,0:T(8,128)}) custom-call(s32[1]{0:T(128)} %bitcast.scalars, bf16[96,2048]{1,0:T(8,128)(2,1)} %reduce-scatter.5.cloned.1.call-done.refs_0_, ...), custom_call_target="tpu_custom_call" | custom-call | flops 1 | bytes 1 | tf_op jit(solution)/shard_map/back_out/pallas_call | solution.py:1102
  224.1 21.5 %reduce-scatter.7.cloned.1.call-done.refs_3_ = bf16[96,2048]{1,0:T(8,128)(2,1)} async-done(((bf16[384,2048]{1,0:T(8,128)(2,1)}), bf16[96,2048]{1,0:T(8,128)(2,1)}) %reduce-scatter.7.cloned.1.call-update) | async-done | bytes 393232 | tf_op jit(solution)/shard_map/reduce_scatter | solution.py:1603
  250.1 8.4 %back_out.3 = (bf16[4,96,512]{2,1,0:T(8,128)(2,1)}, f32[96,2048]{1,0:T(8,128)}, bf16[96,2048]{1,0:T(8,128)(2,1)}, f32[1,2048]{1,0:T(1,128)}, f32[16,2048]{1,0:T(8,128)}, /*index=5*/f32[16,2048]{1,0:T(8,128)}) custom-call(s32[1]{0:T(128)} %bitcast.scalars, f32[1,2048]{1,0:T(1,128)} %get-tuple-element.178.refs_0_, f32[16,2048]{1,0:T(8,128)} %get-tuple-element.179.refs_1_, ...), custom_call_target="tpu_custom_call" | custom-call | flops 1 | bytes 1 | tf_op jit(solution)/shard_map/back_out/pallas_call | solution.py:1102
  264.0 4.8 %collective-permute-done.18 = bf16[96,512]{1,0:T(8,128)(2,1)S(1)} collective-permute-done((bf16[96,512]{1,0:T(8,128)(2,1)S(1)}, bf16[96,512]{1,0:T(8,128)(2,1)S(1)}, u32[]{:S(2)}, u32[]{:S(2)}) %collective-permute-start.18) | collective-permute-done | bytes 98336 | tf_op jit(solution)/shard_map/ppermute | solution.py:1632
  282.8 24.2 %attend_back.1 = (bf16[3,768,128]{2,1,0:T(8,128)(2,1)}, bf16[3,768,128]{2,1,0:T(8,128)(2,1)}, bf16[3,768,128]{2,1,0:T(8,128)(2,1)}, bf16[3,768,128]{2,1,0:T(8,128)(2,1)}) custom-call(s32[17]{0:T(128)} %pad_add_fusion.scalars, bf16[3,768,128]{2,1,0:T(8,128)(2,1)} %get-tuple-element.141.refs_0_, bf16[3,768,128]{2,1,0:T(8,128)(2,1)} %copy-done.5, ...), custom_call_target="tpu_custom_call" | custom-call | flops 1 | bytes 1 | tf_op jit(solution)/shard_map/attend_back/pallas_call | solution.py:522
  312.5 14.0 %shares.2 = (bf16[32,2048]{1,0:T(8,128)(2,1)}, bf16[16,2816]{1,0:T(8,128)(2,1)}) custom-call(bf16[384,2048]{1,0:T(8,128)(2,1)} %get-tuple-element.200.refs_0_, bf16[384,2048]{1,0:T(8,128)(2,1)} %get-tuple-element.201.refs_1_, bf16[384,2816]{1,0:T(8,128)(2,1)} %get-tuple-element.202.refs_2_, bf16[384,2816]{1,0:T(8,128)(2,1)} %get-tuple-element.203.refs_3_, ...), custom_call_target="tpu_custom_call" | custom-call | flops 1 | bytes 1 | tf_op jit(solution)/shard_map/shares/pallas_call | solution.py:1247
  326.5 6.9 %collective-permute-done.25.refs_2_ = bf16[3,768,128]{2,1,0:T(8,128)(2,1)S(1)} collective-permute-done((bf16[3,768,128]{2,1,0:T(8,128)(2,1)}, bf16[3,768,128]{2,1,0:T(8,128)(2,1)S(1)}, u32[]{:S(2)}, u32[]{:S(2)}) %collective-permute-start.25) | collective-permute-done | bytes 589856 | tf_op jit(solution)/shard_map/ppermute | solution.py:52
  334.4 12.1 %unproject.1 = (bf16[768,1536]{1,0:T(8,128)(2,1)}, f32[1,1536]{1,0:T(1,128)}, bf16[768,2048]{1,0:T(8,128)(2,1)}) custom-call(s32[1]{0:T(128)} %bitcast.1.scalars, f32[768,128]{1,0:T(8,128)} %get-tuple-element.290.cos_ref, f32[768,128]{1,0:T(8,128)} %get-tuple-element.289.sin_ref, bf16[768,1536]{1,0:T(8,128)(2,1)} %get-tuple-element.135.raw_ref, ...), custom_call_target="tpu_custom_call" | custom-call | flops 1 | bytes 1 | tf_op jit(solution)/shard_map/unproject/pallas_call | solution.py:1171
  349.2 9.7 %shares.3 = (bf16[48,2048]{1,0:T(8,128)(2,1)}, bf16[16,1536]{1,0:T(8,128)(2,1)}) custom-call(bf16[768,2048]{1,0:T(8,128)(2,1)} %get-tuple-element.225.refs_0_, bf16[768,1536]{1,0:T(8,128)(2,1)} %get-tuple-element.226.refs_1_, bf16[48,2048]{1,0:T(8,128)(2,1)} %bitcast.131, f32[16,1536]{1,0:T(8,128)} %pad_maximum_fusion.6.refs_3_, ...), custom_call_target="tpu_custom_call" | custom-call | flops 1 | bytes 1 | tf_op jit(solution)/shard_map/shares/pallas_call | solution.py:1247
  369.1 4.3 collective-permute-done.28
  373.3 4.0 collective-permute-done.30
  380.0 11.0 %collective-permute-done.31 = bf16[32,2048]{1,0:T(8,128)(2,1)S(1)} collective-permute-done((bf16[32,2048]{1,0:T(8,128)(2,1)S(1)}, bf16[32,2048]{1,0:T(8,128)(2,1)S(1)}, u32[]{:S(2)}, u32[]{:S(2)}) %collective-permute-start.31) | collective-permute-done | bytes 131104 | tf_op jit(solution)/shard_map/ppermute | solution.py:52
  391.6 15.4 %collective-permute-done.32 = bf16[32,2048]{1,0:T(8,128)(2,1)S(1)} collective-permute-done((bf16[32,2048]{1,0:T(8,128)(2,1)S(1)}, bf16[32,2048]{1,0:T(8,128)(2,1)S(1)}, u32[]{:S(2)}, u32[]{:S(2)}) %collective-permute-start.32) | collective-permute-done | bytes 131104 | tf_op jit(solution)/shard_map/ppermute | solution.py:52
  (285 shorter events, 130.7 us)
Async XLA Ops:
  7.2 129.7 %all-gather.4.cloned.1.call-start = ((), (), s32[]{:S(2)}) async-start(), calls=%async_computation.4 | async-start | bytes 9437184 | tf_op jit(solution)/shard_map/all_gather | solution.py:1473
  9.8 162.3 %all-gather.6.cloned.1.call-start = ((), (), s32[]{:S(2)}) async-start(), calls=%async_computation.9 | async-start | bytes 1966080 | tf_op jit(solution)/shard_map/all_gather | solution.py:1560
  37.8 30.3 %collective-permute-start.3 = (bf16[3,768,128]{2,1,0:T(8,128)(2,1)}, bf16[3,768,128]{2,1,0:T(8,128)(2,1)S(1)}, u32[]{:S(2)}, u32[]{:S(2)}) collective-permute-start(bf16[3,768,128]{2,1,0:T(8,128)(2,1)} %get-tuple-element.132), channel_id=1, source_target_pairs={{0,4},{4,0},{8,12},{12,8},{1,5},{5,1},{9,13},{13,9},{2,6},{6,2},{1... | collective-permute-start | bytes 1769480 | tf_op jit(solution)/shard_map/ppermute | solution.py:52
  39.8 28.4 %collective-permute-start.4 = (bf16[3,768,128]{2,1,0:T(8,128)(2,1)}, bf16[3,768,128]{2,1,0:T(8,128)(2,1)S(1)}, u32[]{:S(2)}, u32[]{:S(2)}) collective-permute-start(bf16[3,768,128]{2,1,0:T(8,128)(2,1)} %get-tuple-element.133), channel_id=1, source_target_pairs={{0,8},{4,12},{8,0},{12,4},{1,9},{5,13},{9,1},{13,5},{2,10},{6,14},... | collective-permute-start | bytes 1769480 | tf_op jit(solution)/shard_map/ppermute | solution.py:52
  41.3 26.9 %collective-permute-start.5 = (bf16[3,768,128]{2,1,0:T(8,128)(2,1)}, bf16[3,768,128]{2,1,0:T(8,128)(2,1)S(1)}, u32[]{:S(2)}, u32[]{:S(2)}) collective-permute-start(bf16[3,768,128]{2,1,0:T(8,128)(2,1)} %get-tuple-element.134), channel_id=1, source_target_pairs={{0,12},{4,8},{8,4},{12,0},{1,13},{5,9},{9,5},{13,1},{2,14},{6,10},... | collective-permute-start | bytes 1769480 | tf_op jit(solution)/shard_map/ppermute | solution.py:52
  101.4 10.0 %collective-permute-start.10 = (bf16[416,512]{1,0:T(8,128)(2,1)}, bf16[416,512]{1,0:T(8,128)(2,1)S(1)}, u32[]{:S(2)}, u32[]{:S(2)}) collective-permute-start(bf16[416,512]{1,0:T(8,128)(2,1)} %get-tuple-element.150.refs_0_), channel_id=1, source_target_pairs={{0,1},{1,2},{2,3},{4,5},{5,6},{6,7},{8,9},{9,10},{10,11},{12,13},{... | collective-permute-start | bytes 1277960 | tf_op jit(solution)/shard_map/ppermute | solution.py:113
  104.9 10.6 %collective-permute-start.9 = (bf16[416,512]{1,0:T(8,128)(2,1)}, bf16[416,512]{1,0:T(8,128)(2,1)S(1)}, u32[]{:S(2)}, u32[]{:S(2)}) collective-permute-start(bf16[416,512]{1,0:T(8,128)(2,1)} %get-tuple-element.150.refs_0_), channel_id=1, source_target_pairs={{1,0},{2,1},{3,2},{5,4},{6,5},{7,6},{9,8},{10,9},{11,10},{13,12},{... | collective-permute-start | bytes 1277960 | tf_op jit(solution)/shard_map/ppermute | solution.py:114
  115.5 10.5 %collective-permute-start.13 = (bf16[416,512]{1,0:T(8,128)(2,1)S(1)}, bf16[416,512]{1,0:T(8,128)(2,1)S(1)}, u32[]{:S(2)}, u32[]{:S(2)}) collective-permute-start(bf16[416,512]{1,0:T(8,128)(2,1)S(1)} %collective-permute-done.9), channel_id=1, source_target_pairs={{1,0},{2,1},{5,4},{6,5},{9,8},{10,9},{13,12},{14,13},{17,16},{18,1... | collective-permute-start | bytes 1277960 | tf_op jit(solution)/shard_map/ppermute | solution.py:114
  116.8 11.3 %collective-permute-start.12 = (bf16[416,512]{1,0:T(8,128)(2,1)S(1)}, bf16[416,512]{1,0:T(8,128)(2,1)S(1)}, u32[]{:S(2)}, u32[]{:S(2)}) collective-permute-start(bf16[416,512]{1,0:T(8,128)(2,1)S(1)} %collective-permute-done.11), channel_id=1, source_target_pairs={{2,3},{6,7},{10,11},{14,15},{18,19},{22,23},{26,27},{30,31}} | collective-permute-start | bytes 1277960 | tf_op jit(solution)/shard_map/ppermute | solution.py:113
  136.9 77.6 %reduce-scatter.5.cloned.1.call-start = ((), (), s32[]{:S(2)}) async-start(), calls=%async_computation.5 | async-start | bytes 1966080 | tf_op jit(solution)/shard_map/reduce_scatter | solution.py:1603
  164.4 81.3 %reduce-scatter.7.cloned.1.call-start = ((), (), s32[]{:S(2)}) async-start(), calls=%async_computation.6 | async-start | bytes 1966080 | tf_op jit(solution)/shard_map/reduce_scatter | solution.py:1603
  199.3 218.7 %reduce-scatter.9.cloned.1.call-start = ((), (), s32[]{:S(2)}) async-start(), calls=%async_computation.7 | async-start | bytes 3932160 | tf_op jit(solution)/shard_map/reduce_scatter | solution.py:1603
  246.6 16.5 %collective-permute-start.17 = (bf16[96,512]{1,0:T(8,128)(2,1)S(1)}, bf16[96,512]{1,0:T(8,128)(2,1)S(1)}, u32[]{:S(2)}, u32[]{:S(2)}) collective-permute-start(bf16[96,512]{1,0:T(8,128)(2,1)S(1)} %get-tuple-element.281), channel_id=1, source_target_pairs={{0,3},{1,0},{2,1},{3,2},{4,7},{5,4},{6,5},{7,6},{8,11},{9,8},{10,9... | collective-permute-start | bytes 294920 | tf_op jit(solution)/shard_map/ppermute | solution.py:1632
  248.1 15.0 %collective-permute-start.16 = (bf16[96,512]{1,0:T(8,128)(2,1)S(1)}, bf16[96,512]{1,0:T(8,128)(2,1)S(1)}, u32[]{:S(2)}, u32[]{:S(2)}) collective-permute-start(bf16[96,512]{1,0:T(8,128)(2,1)S(1)} %get-tuple-element.282), channel_id=1, source_target_pairs={{0,2},{1,3},{2,0},{3,1},{4,6},{5,7},{6,4},{7,5},{8,10},{9,11},{10,... | collective-permute-start | bytes 294920 | tf_op jit(solution)/shard_map/ppermute | solution.py:1632
  248.5 13.9 %collective-permute-start.15 = (bf16[96,512]{1,0:T(8,128)(2,1)S(1)}, bf16[96,512]{1,0:T(8,128)(2,1)S(1)}, u32[]{:S(2)}, u32[]{:S(2)}) collective-permute-start(bf16[96,512]{1,0:T(8,128)(2,1)S(1)} %get-tuple-element.283), channel_id=1, source_target_pairs={{0,1},{1,2},{2,3},{3,0},{4,5},{5,6},{6,7},{7,4},{8,9},{9,10},{10,1... | collective-permute-start | bytes 294920 | tf_op jit(solution)/shard_map/ppermute | solution.py:1632
  259.5 11.2 %collective-permute-start.20 = (bf16[96,512]{1,0:T(8,128)(2,1)S(1)}, bf16[96,512]{1,0:T(8,128)(2,1)S(1)}, u32[]{:S(2)}, u32[]{:S(2)}) collective-permute-start(bf16[96,512]{1,0:T(8,128)(2,1)S(1)} %get-tuple-element.278), channel_id=1, source_target_pairs={{0,3},{1,0},{2,1},{3,2},{4,7},{5,4},{6,5},{7,6},{8,11},{9,8},{10,9... | collective-permute-start | bytes 294920 | tf_op jit(solution)/shard_map/ppermute | solution.py:1632
  282.8 138.3 %reduce-scatter.11.cloned.1.call-start = ((), (), s32[]{:S(2)}) async-start(), calls=%async_computation.8 | async-start | bytes 3932160 | tf_op jit(solution)/shard_map/reduce_scatter | solution.py:1603
  307.0 19.5 %collective-permute-start.24 = (bf16[3,768,128]{2,1,0:T(8,128)(2,1)}, bf16[3,768,128]{2,1,0:T(8,128)(2,1)S(1)}, u32[]{:S(2)}, u32[]{:S(2)}) collective-permute-start(bf16[3,768,128]{2,1,0:T(8,128)(2,1)} %get-tuple-element.193), channel_id=1, source_target_pairs={{0,4},{4,0},{8,12},{12,8},{1,5},{5,1},{9,13},{13,9},{2,6},{6,2},{1... | collective-permute-start | bytes 1769480 | tf_op jit(solution)/shard_map/ppermute | solution.py:52
  308.1 25.3 %collective-permute-start.25 = (bf16[3,768,128]{2,1,0:T(8,128)(2,1)}, bf16[3,768,128]{2,1,0:T(8,128)(2,1)S(1)}, u32[]{:S(2)}, u32[]{:S(2)}) collective-permute-start(bf16[3,768,128]{2,1,0:T(8,128)(2,1)} %get-tuple-element.194), channel_id=1, source_target_pairs={{0,8},{4,12},{8,0},{12,4},{1,9},{5,13},{9,1},{13,5},{2,10},{6,14},... | collective-permute-start | bytes 1769480 | tf_op jit(solution)/shard_map/ppermute | solution.py:52
  309.6 23.9 %collective-permute-start.26 = (bf16[3,768,128]{2,1,0:T(8,128)(2,1)}, bf16[3,768,128]{2,1,0:T(8,128)(2,1)S(1)}, u32[]{:S(2)}, u32[]{:S(2)}) collective-permute-start(bf16[3,768,128]{2,1,0:T(8,128)(2,1)} %get-tuple-element.195), channel_id=1, source_target_pairs={{0,12},{4,8},{8,4},{12,0},{1,13},{5,9},{9,5},{13,1},{2,14},{6,10},... | collective-permute-start | bytes 1769480 | tf_op jit(solution)/shard_map/ppermute | solution.py:52
  367.2 10.1 %collective-permute-start.30 = (bf16[48,2048]{1,0:T(8,128)(2,1)S(1)}, bf16[48,2048]{1,0:T(8,128)(2,1)S(1)}, u32[]{:S(2)}, u32[]{:S(2)}) collective-permute-start(bf16[48,2048]{1,0:T(8,128)(2,1)S(1)} %get-tuple-element.272), channel_id=1, source_target_pairs={{0,12},{4,8},{8,4},{12,0},{1,13},{5,9},{9,5},{13,1},{2,14},{6,10},... | collective-permute-start | bytes 589832 | tf_op jit(solution)/shard_map/ppermute | solution.py:52
  368.1 10.6 %collective-permute-start.29 = (bf16[48,2048]{1,0:T(8,128)(2,1)S(1)}, bf16[48,2048]{1,0:T(8,128)(2,1)S(1)}, u32[]{:S(2)}, u32[]{:S(2)}) collective-permute-start(bf16[48,2048]{1,0:T(8,128)(2,1)S(1)} %get-tuple-element.273), channel_id=1, source_target_pairs={{0,8},{4,12},{8,0},{12,4},{1,9},{5,13},{9,1},{13,5},{2,10},{6,14},... | collective-permute-start | bytes 589832 | tf_op jit(solution)/shard_map/ppermute | solution.py:52
  378.8 12.2 %collective-permute-start.31 = (bf16[32,2048]{1,0:T(8,128)(2,1)S(1)}, bf16[32,2048]{1,0:T(8,128)(2,1)S(1)}, u32[]{:S(2)}, u32[]{:S(2)}) collective-permute-start(bf16[32,2048]{1,0:T(8,128)(2,1)S(1)} %slice.192), channel_id=1, source_target_pairs={{0,1},{1,0},{2,3},{3,2},{4,5},{5,4},{6,7},{7,6},{8,9},{9,8},{10,11... | collective-permute-start | bytes 393224 | tf_op jit(solution)/shard_map/ppermute | solution.py:52
  391.0 16.0 %collective-permute-start.32 = (bf16[32,2048]{1,0:T(8,128)(2,1)S(1)}, bf16[32,2048]{1,0:T(8,128)(2,1)S(1)}, u32[]{:S(2)}, u32[]{:S(2)}) collective-permute-start(bf16[32,2048]{1,0:T(8,128)(2,1)S(1)} %slice_add_fusion), channel_id=1, source_target_pairs={{0,2},{1,3},{2,0},{3,1},{4,6},{5,7},{6,4},{7,5},{8,10},{9,11},{10,... | collective-permute-start | bytes 393224 | tf_op jit(solution)/shard_map/ppermute | solution.py:52
  (77 other events, 476.2 us)
Sparse Core Ops, SparseCore 0:
  10.2 84.7 all-gather.3
  137.0 35.0 all-gather.5
  174.4 34.1 reduce-scatter.4
  211.3 34.2 reduce-scatter.6
  282.3 59.5 reduce-scatter.8
  346.7 65.1 reduce-scatter.10

commit v3 on v2

--- a/solution.py
+++ b/solution.py
@@ -1684,7 +1684,7 @@
 
 
     share_a_heads, share_b_heads = layer_shares(
-        [normed],
+        after([normed], result),
         a_heads.reshape(3 * RANK, width),
         [dz_heads],
         jnp.concatenate(b_heads, axis=1),

time: 452 us -> 456 us (level)
  transfers between devices with their start and end apart: 43 -> 43, of which waited for: 23 -> 23; matrix products, arithmetic and copies ran while one was open for 8% -> 8% of each run, Pallas kernels for 46% -> 45%
where the time goes in v3:
time: 456 us; the launch traced here: 448 us
  Pallas kernels  203 us (45%)
  waiting for transfers between devices  126 us (28%)
  starting transfers between devices  44.7 us (10%)
  other arithmetic  29.9 us (7%)
  local copies, waits for them, and re-layouts  24.9 us (5%)
  between operations  15.3 us (3%)
    ppermute x25, waiting for transfers between devices, swap(): return lax.ppermute(value, axis, [(i, i ^ distance) for i in range(size)])  66.5 us
    pallas_call x2, Pallas kernels, block(): pl.pallas_call(functools.partial(block_kernel, sizes, size), grid_spec=pl...  49.7 us
    ppermute x25, starting transfers between devices, swap(): return lax.ppermute(value, axis, [(i, i ^ distance) for i in range(size)])  27.7 us
    pallas_call x1, Pallas kernels, attention_backward(): pl.pallas_call(functools.partial(body, meta), grid_spec=pltpu.PrefetchSca...  24.2 us
    pallas_call x2, Pallas kernels, layer_shares(): pl.pallas_call(functools.partial(shares_kernel, count, chunks, span), gri...  23.6 us
    reduce_scatter x4, waiting for transfers between devices, scatter(): return lax.psum_scatter(parts, 'mp', scatter_dimension=0, tiled=True)  21.6 us
    pallas_call x1, Pallas kernels, merge_others(): pl.pallas_call(functools.partial(merge_kernel, starts), grid=(starts[1] +...  21.1 us
    ppermute x3, waiting for transfers between devices, line_step(): lefts.append(lax.ppermute(left, 'mp', left_pairs))  19.1 us
  transfers between devices with their start and end apart: 43, of which 23 were waited for; matrix products, arithmetic and copies ran while one was open for 8% of the time, Pallas kernels for 45%

profile of v3, /device:TPU:0, one launch (start us, length us, event | category | flops | bytes accessed | tf_op | source)
XLA Modules:
  0.0 448.1 jit_solution(1156206212600322030)
XLA Ops:
  19.3 18.6 %project_heads.1 = (bf16[3,768,128]{2,1,0:T(8,128)(2,1)}, bf16[3,768,128]{2,1,0:T(8,128)(2,1)}, bf16[3,768,128]{2,1,0:T(8,128)(2,1)}, bf16[3,768,128]{2,1,0:T(8,...) custom-call(s32[1]{0:T(128)} %bitcast.1.scalars, ...), custom_call_target="tpu_custom_call" | custom-call | flops 1 | bytes 1 | tf_op jit(solution)/shard_map/project_heads/pallas_call | solution.py:785
  44.3 21.1 %merge_others.1 = (f32[1,2048]{1,0:T(1,128)}, f32[16,2048]{1,0:T(8,128)}, f32[1,2048]{1,0:T(1,128)}, f32[16,2048]{1,0:T(8,128)}, bf16[1408,2048]{1,0:T(8,128)(2,...) custom-call(bf16[512,2048]{1,0:T(8,128)(2,1)} %out_w, ...), custom_call_target="tpu_custom_call" | custom-call | flops 1 | bytes 1 | tf_op jit(solution)/shard_map/merge_others/pallas_call | solution.py:644
  69.4 17.5 %attend.1 = (bf16[768,128]{1,0:T(8,128)(2,1)}, bf16[768,128]{1,0:T(8,128)(2,1)}, bf16[768,128]{1,0:T(8,128)(2,1)}, bf16[768,128]{1,0:T(8,128)(2,1)}, f32[4,1,768]{2,1,0:T(1,128)}) custom-call(s32[17]{0:T(128)} %pad_add_fusion.scalars, bf16[3,768,128]{2,1,0:T(8,128)(2,1)} %get-tuple-element.142.refs_0_, bf16[3,768,128]{2,1,0:T(8,128)(2,1)} %copy-done.7, ...), custom_call_target="tpu_custom_call" | custom-call | flops 1 | bytes 1 | tf_op jit(solution)/shard_map/attend/pallas_call | solution.py:391
  106.3 5.3 %collective-permute-done.10 = bf16[416,512]{1,0:T(8,128)(2,1)S(1)} collective-permute-done((bf16[416,512]{1,0:T(8,128)(2,1)}, bf16[416,512]{1,0:T(8,128)(2,1)S(1)}, u32[]{:S(2)}, u32[]{:S(2)}) %collective-permute-start.10) | collective-permute-done | bytes 426016 | tf_op jit(solution)/shard_map/ppermute | solution.py:113
  117.7 8.6 %collective-permute-done.13 = bf16[416,512]{1,0:T(8,128)(2,1)S(1)} collective-permute-done((bf16[416,512]{1,0:T(8,128)(2,1)S(1)}, bf16[416,512]{1,0:T(8,128)(2,1)S(1)}, u32[]{:S(2)}, u32[]{:S(2)}) %collective-permute-start.13) | collective-permute-done | bytes 426016 | tf_op jit(solution)/shard_map/ppermute | solution.py:114
  129.2 7.1 %collective-permute-done.14 = bf16[416,512]{1,0:T(8,128)(2,1)S(1)} collective-permute-done((bf16[416,512]{1,0:T(8,128)(2,1)S(1)}, bf16[416,512]{1,0:T(8,128)(2,1)S(1)}, u32[]{:S(2)}, u32[]{:S(2)}) %collective-permute-start.14) | collective-permute-done | bytes 426016 | tf_op jit(solution)/shard_map/ppermute | solution.py:114
  139.8 24.9 %block.2 = (bf16[384,2048]{1,0:T(8,128)(2,1)}, f32[96,2048]{1,0:T(8,128)}, f32[96,2048]{1,0:T(8,128)}, bf16[96,16]{1,0:T(8,128)(2,1)}, bf16[96,2048]{1,0:T(8,128...) custom-call(s32[1]{0:T(128)} %bitcast.scalars, ...), custom_call_target="tpu_custom_call" | custom-call | flops 1 | bytes 1 | tf_op jit(solution)/shard_map/block/pallas_call | solution.py:1027
  164.9 7.3 %all-gather.6.cloned.1.call-done = bf16[1536,512]{1,0:T(8,128)(2,1)} async-done(((bf16[384,512]{1,0:T(8,128)(2,1)}), bf16[1536,512]{1,0:T(8,128)(2,1)}) %all-gather.6.cloned.1.call-update) | async-done | bytes 1572880 | tf_op jit(solution)/shard_map/all_gather | solution.py:1560
  174.5 24.9 %block.3 = (bf16[384,2048]{1,0:T(8,128)(2,1)}, f32[96,2048]{1,0:T(8,128)}, f32[96,2048]{1,0:T(8,128)}, bf16[96,16]{1,0:T(8,128)(2,1)}, bf16[96,2048]{1,0:T(8,128...) custom-call(s32[1]{0:T(128)} %bitcast.scalars, ...), custom_call_target="tpu_custom_call" | custom-call | flops 1 | bytes 1 | tf_op jit(solution)/shard_map/block/pallas_call | solution.py:1027
  201.5 13.1 %down_project.1 = (bf16[4,2,96,2048]{3,2,1,0:T(8,128)(2,1)}, f32[1,2048]{1,0:T(1,128)}, bf16[16,2048]{1,0:T(8,128)(2,1)}, bf16[16,1408]{1,0:T(8,128)(2,1)}) custom-call(bf16[384,1408]{1,0:T(8,128)(2,1)} %get-tuple-element.169.refs_0_, bf16[384,1408]{1,0:T(8,128)(2,1)} %get-tuple-element.170.refs_1_, bf16[1408,2048]{1,0:T(8,128)(2,1)} %get-tuple-element.157.refs_14_.refs_2_, ...), custom_call_target="tpu_custom_call" | custom-call | flops 1 | bytes 1 | tf_op jit(solution)/shard_map/down_project/pallas_call | solution.py:1317
  214.6 8.7 %back_out.2 = (bf16[4,96,512]{2,1,0:T(8,128)(2,1)}, f32[96,2048]{1,0:T(8,128)}, bf16[96,2048]{1,0:T(8,128)(2,1)}, f32[1,2048]{1,0:T(1,128)}, f32[16,2048]{1,0:T(8,128)}, /*index=5*/f32[16,2048]{1,0:T(8,128)}) custom-call(s32[1]{0:T(128)} %bitcast.scalars, bf16[96,2048]{1,0:T(8,128)(2,1)} %reduce-scatter.5.cloned.1.call-done.refs_0_, ...), custom_call_target="tpu_custom_call" | custom-call | flops 1 | bytes 1 | tf_op jit(solution)/shard_map/back_out/pallas_call | solution.py:1102
  224.2 21.5 %reduce-scatter.7.cloned.1.call-done.refs_3_ = bf16[96,2048]{1,0:T(8,128)(2,1)} async-done(((bf16[384,2048]{1,0:T(8,128)(2,1)}), bf16[96,2048]{1,0:T(8,128)(2,1)}) %reduce-scatter.7.cloned.1.call-update) | async-done | bytes 393232 | tf_op jit(solution)/shard_map/reduce_scatter | solution.py:1603
  250.2 8.3 %back_out.3 = (bf16[4,96,512]{2,1,0:T(8,128)(2,1)}, f32[96,2048]{1,0:T(8,128)}, bf16[96,2048]{1,0:T(8,128)(2,1)}, f32[1,2048]{1,0:T(1,128)}, f32[16,2048]{1,0:T(8,128)}, /*index=5*/f32[16,2048]{1,0:T(8,128)}) custom-call(s32[1]{0:T(128)} %bitcast.scalars, f32[1,2048]{1,0:T(1,128)} %get-tuple-element.179.refs_0_, f32[16,2048]{1,0:T(8,128)} %get-tuple-element.180.refs_1_, ...), custom_call_target="tpu_custom_call" | custom-call | flops 1 | bytes 1 | tf_op jit(solution)/shard_map/back_out/pallas_call | solution.py:1102
  264.1 4.8 %collective-permute-done.18 = bf16[96,512]{1,0:T(8,128)(2,1)S(1)} collective-permute-done((bf16[96,512]{1,0:T(8,128)(2,1)S(1)}, bf16[96,512]{1,0:T(8,128)(2,1)S(1)}, u32[]{:S(2)}, u32[]{:S(2)}) %collective-permute-start.18) | collective-permute-done | bytes 98336 | tf_op jit(solution)/shard_map/ppermute | solution.py:1632
  282.9 24.2 %attend_back.1 = (bf16[3,768,128]{2,1,0:T(8,128)(2,1)}, bf16[3,768,128]{2,1,0:T(8,128)(2,1)}, bf16[3,768,128]{2,1,0:T(8,128)(2,1)}, bf16[3,768,128]{2,1,0:T(8,128)(2,1)}) custom-call(s32[17]{0:T(128)} %pad_add_fusion.scalars, bf16[3,768,128]{2,1,0:T(8,128)(2,1)} %get-tuple-element.142.refs_0_, bf16[3,768,128]{2,1,0:T(8,128)(2,1)} %copy-done.7, ...), custom_call_target="tpu_custom_call" | custom-call | flops 1 | bytes 1 | tf_op jit(solution)/shard_map/attend_back/pallas_call | solution.py:522
  311.8 13.9 %shares.2 = (bf16[32,2048]{1,0:T(8,128)(2,1)}, bf16[16,2816]{1,0:T(8,128)(2,1)}) custom-call(bf16[384,2048]{1,0:T(8,128)(2,1)} %get-tuple-element.201.refs_0_, bf16[384,2048]{1,0:T(8,128)(2,1)} %get-tuple-element.202.refs_1_, bf16[384,2816]{1,0:T(8,128)(2,1)} %get-tuple-element.203.refs_2_, bf16[384,2816]{1,0:T(8,128)(2,1)} %get-tuple-element.204.refs_3_, ...), custom_call_target="tpu_custom_call" | custom-call | flops 1 | bytes 1 | tf_op jit(solution)/shard_map/shares/pallas_call | solution.py:1247
  325.8 7.7 %collective-permute-done.25.refs_2_ = bf16[3,768,128]{2,1,0:T(8,128)(2,1)S(1)} collective-permute-done((bf16[3,768,128]{2,1,0:T(8,128)(2,1)}, bf16[3,768,128]{2,1,0:T(8,128)(2,1)S(1)}, u32[]{:S(2)}, u32[]{:S(2)}) %collective-permute-start.25) | collective-permute-done | bytes 589856 | tf_op jit(solution)/shard_map/ppermute | solution.py:52
  334.5 12.1 %unproject.1 = (bf16[768,1536]{1,0:T(8,128)(2,1)}, f32[1,1536]{1,0:T(1,128)}, bf16[768,2048]{1,0:T(8,128)(2,1)}) custom-call(s32[1]{0:T(128)} %bitcast.1.scalars, f32[768,128]{1,0:T(8,128)} %get-tuple-element.292.cos_ref, f32[768,128]{1,0:T(8,128)} %get-tuple-element.291.sin_ref, bf16[768,1536]{1,0:T(8,128)(2,1)} %get-tuple-element.136.raw_ref, ...), custom_call_target="tpu_custom_call" | custom-call | flops 1 | bytes 1 | tf_op jit(solution)/shard_map/unproject/pallas_call | solution.py:1171
  352.5 9.6 %shares.3 = (bf16[48,2048]{1,0:T(8,128)(2,1)}, bf16[16,1536]{1,0:T(8,128)(2,1)}) custom-call(bf16[768,2048]{1,0:T(8,128)(2,1)} %get-tuple-element.227.refs_0_, bf16[768,1536]{1,0:T(8,128)(2,1)} %get-tuple-element.228.refs_1_, bf16[48,2048]{1,0:T(8,128)(2,1)} %bitcast.131, f32[16,1536]{1,0:T(8,128)} %pad_maximum_fusion.6.refs_3_, ...), custom_call_target="tpu_custom_call" | custom-call | flops 1 | bytes 1 | tf_op jit(solution)/shard_map/shares/pallas_call | solution.py:1247
  373.8 4.6 %collective-permute-done.28 = bf16[48,2048]{1,0:T(8,128)(2,1)} collective-permute-done((bf16[48,2048]{1,0:T(8,128)(2,1)}, bf16[48,2048]{1,0:T(8,128)(2,1)}, u32[]{:S(2)}, u32[]{:S(2)}) %collective-permute-start.28) | collective-permute-done | bytes 196640 | tf_op jit(solution)/shard_map/ppermute | solution.py:52
  378.4 4.3 collective-permute-done.30
  386.6 9.7 %collective-permute-done.31 = bf16[32,2048]{1,0:T(8,128)(2,1)S(1)} collective-permute-done((bf16[32,2048]{1,0:T(8,128)(2,1)S(1)}, bf16[32,2048]{1,0:T(8,128)(2,1)S(1)}, u32[]{:S(2)}, u32[]{:S(2)}) %collective-permute-start.31) | collective-permute-done | bytes 131104 | tf_op jit(solution)/shard_map/ppermute | solution.py:52
  397.5 14.0 %collective-permute-done.32 = bf16[32,2048]{1,0:T(8,128)(2,1)} collective-permute-done((bf16[32,2048]{1,0:T(8,128)(2,1)}, bf16[32,2048]{1,0:T(8,128)(2,1)}, u32[]{:S(2)}, u32[]{:S(2)}) %collective-permute-start.32) | collective-permute-done | bytes 131104 | tf_op jit(solution)/shard_map/ppermute | solution.py:52
  421.3 4.3 collective-permute-done.34
  (291 shorter events, 136.8 us)
Async XLA Ops:
  7.2 129.9 %all-gather.4.cloned.1.call-start = ((), (), s32[]{:S(2)}) async-start(), calls=%async_computation.4 | async-start | bytes 9437184 | tf_op jit(solution)/shard_map/all_gather | solution.py:1473
  9.8 162.4 %all-gather.6.cloned.1.call-start = ((), (), s32[]{:S(2)}) async-start(), calls=%async_computation.9 | async-start | bytes 1966080 | tf_op jit(solution)/shard_map/all_gather | solution.py:1560
  37.9 30.3 %collective-permute-start.3 = (bf16[3,768,128]{2,1,0:T(8,128)(2,1)}, bf16[3,768,128]{2,1,0:T(8,128)(2,1)S(1)}, u32[]{:S(2)}, u32[]{:S(2)}) collective-permute-start(bf16[3,768,128]{2,1,0:T(8,128)(2,1)} %get-tuple-element.133), channel_id=1, source_target_pairs={{0,4},{4,0},{8,12},{12,8},{1,5},{5,1},{9,13},{13,9},{2,6},{6,2},{1... | collective-permute-start | bytes 1769480 | tf_op jit(solution)/shard_map/ppermute | solution.py:52
  39.9 28.3 %collective-permute-start.4 = (bf16[3,768,128]{2,1,0:T(8,128)(2,1)}, bf16[3,768,128]{2,1,0:T(8,128)(2,1)S(1)}, u32[]{:S(2)}, u32[]{:S(2)}) collective-permute-start(bf16[3,768,128]{2,1,0:T(8,128)(2,1)} %get-tuple-element.134), channel_id=1, source_target_pairs={{0,8},{4,12},{8,0},{12,4},{1,9},{5,13},{9,1},{13,5},{2,10},{6,14},... | collective-permute-start | bytes 1769480 | tf_op jit(solution)/shard_map/ppermute | solution.py:52
  41.4 26.8 %collective-permute-start.5 = (bf16[3,768,128]{2,1,0:T(8,128)(2,1)}, bf16[3,768,128]{2,1,0:T(8,128)(2,1)S(1)}, u32[]{:S(2)}, u32[]{:S(2)}) collective-permute-start(bf16[3,768,128]{2,1,0:T(8,128)(2,1)} %get-tuple-element.135), channel_id=1, source_target_pairs={{0,12},{4,8},{8,4},{12,0},{1,13},{5,9},{9,5},{13,1},{2,14},{6,10},... | collective-permute-start | bytes 1769480 | tf_op jit(solution)/shard_map/ppermute | solution.py:52
  105.0 10.7 %collective-permute-start.9 = (bf16[416,512]{1,0:T(8,128)(2,1)}, bf16[416,512]{1,0:T(8,128)(2,1)S(1)}, u32[]{:S(2)}, u32[]{:S(2)}) collective-permute-start(bf16[416,512]{1,0:T(8,128)(2,1)} %get-tuple-element.151.refs_0_), channel_id=1, source_target_pairs={{1,0},{2,1},{3,2},{5,4},{6,5},{7,6},{9,8},{10,9},{11,10},{13,12},{... | collective-permute-start | bytes 1277960 | tf_op jit(solution)/shard_map/ppermute | solution.py:114
  115.6 10.6 %collective-permute-start.13 = (bf16[416,512]{1,0:T(8,128)(2,1)S(1)}, bf16[416,512]{1,0:T(8,128)(2,1)S(1)}, u32[]{:S(2)}, u32[]{:S(2)}) collective-permute-start(bf16[416,512]{1,0:T(8,128)(2,1)S(1)} %collective-permute-done.9), channel_id=1, source_target_pairs={{1,0},{2,1},{5,4},{6,5},{9,8},{10,9},{13,12},{14,13},{17,16},{18,1... | collective-permute-start | bytes 1277960 | tf_op jit(solution)/shard_map/ppermute | solution.py:114
  116.9 11.4 %collective-permute-start.12 = (bf16[416,512]{1,0:T(8,128)(2,1)S(1)}, bf16[416,512]{1,0:T(8,128)(2,1)S(1)}, u32[]{:S(2)}, u32[]{:S(2)}) collective-permute-start(bf16[416,512]{1,0:T(8,128)(2,1)S(1)} %collective-permute-done.11), channel_id=1, source_target_pairs={{2,3},{6,7},{10,11},{14,15},{18,19},{22,23},{26,27},{30,31}} | collective-permute-start | bytes 1277960 | tf_op jit(solution)/shard_map/ppermute | solution.py:113
  137.1 77.4 %reduce-scatter.5.cloned.1.call-start = ((), (), s32[]{:S(2)}) async-start(), calls=%async_computation.5 | async-start | bytes 1966080 | tf_op jit(solution)/shard_map/reduce_scatter | solution.py:1603
  164.7 81.1 %reduce-scatter.7.cloned.1.call-start = ((), (), s32[]{:S(2)}) async-start(), calls=%async_computation.6 | async-start | bytes 1966080 | tf_op jit(solution)/shard_map/reduce_scatter | solution.py:1603
  199.4 150.6 %reduce-scatter.9.cloned.1.call-start = ((), (), s32[]{:S(2)}) async-start(), calls=%async_computation.7 | async-start | bytes 3932160 | tf_op jit(solution)/shard_map/reduce_scatter | solution.py:1603
  246.7 16.5 %collective-permute-start.17 = (bf16[96,512]{1,0:T(8,128)(2,1)S(1)}, bf16[96,512]{1,0:T(8,128)(2,1)S(1)}, u32[]{:S(2)}, u32[]{:S(2)}) collective-permute-start(bf16[96,512]{1,0:T(8,128)(2,1)S(1)} %get-tuple-element.283), channel_id=1, source_target_pairs={{0,3},{1,0},{2,1},{3,2},{4,7},{5,4},{6,5},{7,6},{8,11},{9,8},{10,9... | collective-permute-start | bytes 294920 | tf_op jit(solution)/shard_map/ppermute | solution.py:1632
  248.2 15.0 %collective-permute-start.16 = (bf16[96,512]{1,0:T(8,128)(2,1)S(1)}, bf16[96,512]{1,0:T(8,128)(2,1)S(1)}, u32[]{:S(2)}, u32[]{:S(2)}) collective-permute-start(bf16[96,512]{1,0:T(8,128)(2,1)S(1)} %get-tuple-element.284), channel_id=1, source_target_pairs={{0,2},{1,3},{2,0},{3,1},{4,6},{5,7},{6,4},{7,5},{8,10},{9,11},{10,... | collective-permute-start | bytes 294920 | tf_op jit(solution)/shard_map/ppermute | solution.py:1632
  248.6 14.0 %collective-permute-start.15 = (bf16[96,512]{1,0:T(8,128)(2,1)S(1)}, bf16[96,512]{1,0:T(8,128)(2,1)S(1)}, u32[]{:S(2)}, u32[]{:S(2)}) collective-permute-start(bf16[96,512]{1,0:T(8,128)(2,1)S(1)} %get-tuple-element.285), channel_id=1, source_target_pairs={{0,1},{1,2},{2,3},{3,0},{4,5},{5,6},{6,7},{7,4},{8,9},{9,10},{10,1... | collective-permute-start | bytes 294920 | tf_op jit(solution)/shard_map/ppermute | solution.py:1632
  259.5 11.2 %collective-permute-start.20 = (bf16[96,512]{1,0:T(8,128)(2,1)S(1)}, bf16[96,512]{1,0:T(8,128)(2,1)S(1)}, u32[]{:S(2)}, u32[]{:S(2)}) collective-permute-start(bf16[96,512]{1,0:T(8,128)(2,1)S(1)} %get-tuple-element.280), channel_id=1, source_target_pairs={{0,3},{1,0},{2,1},{3,2},{4,7},{5,4},{6,5},{7,6},{8,11},{9,8},{10,9... | collective-permute-start | bytes 294920 | tf_op jit(solution)/shard_map/ppermute | solution.py:1632
  282.9 133.8 %reduce-scatter.11.cloned.1.call-start = ((), (), s32[]{:S(2)}) async-start(), calls=%async_computation.8 | async-start | bytes 3932160 | tf_op jit(solution)/shard_map/reduce_scatter | solution.py:1603
  307.0 18.7 %collective-permute-start.24 = (bf16[3,768,128]{2,1,0:T(8,128)(2,1)}, bf16[3,768,128]{2,1,0:T(8,128)(2,1)S(1)}, u32[]{:S(2)}, u32[]{:S(2)}) collective-permute-start(bf16[3,768,128]{2,1,0:T(8,128)(2,1)} %get-tuple-element.194), channel_id=1, source_target_pairs={{0,4},{4,0},{8,12},{12,8},{1,5},{5,1},{9,13},{13,9},{2,6},{6,2},{1... | collective-permute-start | bytes 1769480 | tf_op jit(solution)/shard_map/ppermute | solution.py:52
  308.2 25.3 %collective-permute-start.25 = (bf16[3,768,128]{2,1,0:T(8,128)(2,1)}, bf16[3,768,128]{2,1,0:T(8,128)(2,1)S(1)}, u32[]{:S(2)}, u32[]{:S(2)}) collective-permute-start(bf16[3,768,128]{2,1,0:T(8,128)(2,1)} %get-tuple-element.195), channel_id=1, source_target_pairs={{0,8},{4,12},{8,0},{12,4},{1,9},{5,13},{9,1},{13,5},{2,10},{6,14},... | collective-permute-start | bytes 1769480 | tf_op jit(solution)/shard_map/ppermute | solution.py:52
  309.6 23.9 %collective-permute-start.26 = (bf16[3,768,128]{2,1,0:T(8,128)(2,1)}, bf16[3,768,128]{2,1,0:T(8,128)(2,1)S(1)}, u32[]{:S(2)}, u32[]{:S(2)}) collective-permute-start(bf16[3,768,128]{2,1,0:T(8,128)(2,1)} %get-tuple-element.196), channel_id=1, source_target_pairs={{0,12},{4,8},{8,4},{12,0},{1,13},{5,9},{9,5},{13,1},{2,14},{6,10},... | collective-permute-start | bytes 1769480 | tf_op jit(solution)/shard_map/ppermute | solution.py:52
  372.0 10.7 %collective-permute-start.30 = (bf16[48,2048]{1,0:T(8,128)(2,1)}, bf16[48,2048]{1,0:T(8,128)(2,1)}, u32[]{:S(2)}, u32[]{:S(2)}) collective-permute-start(bf16[48,2048]{1,0:T(8,128)(2,1)} %get-tuple-element.274), channel_id=1, source_target_pairs={{0,12},{4,8},{8,4},{12,0},{1,13},{5,9},{9,5},{13,1},{2,14},{6,10},... | collective-permute-start | bytes 589832 | tf_op jit(solution)/shard_map/ppermute | solution.py:52
  373.2 10.7 %collective-permute-start.29 = (bf16[48,2048]{1,0:T(8,128)(2,1)S(1)}, bf16[48,2048]{1,0:T(8,128)(2,1)}, u32[]{:S(2)}, u32[]{:S(2)}) collective-permute-start(bf16[48,2048]{1,0:T(8,128)(2,1)S(1)} %get-tuple-element.275), channel_id=1, source_target_pairs={{0,8},{4,12},{8,0},{12,4},{1,9},{5,13},{9,1},{13,5},{2,10},{6,14},... | collective-permute-start | bytes 589832 | tf_op jit(solution)/shard_map/ppermute | solution.py:52
  385.2 11.1 %collective-permute-start.31 = (bf16[32,2048]{1,0:T(8,128)(2,1)S(1)}, bf16[32,2048]{1,0:T(8,128)(2,1)S(1)}, u32[]{:S(2)}, u32[]{:S(2)}) collective-permute-start(bf16[32,2048]{1,0:T(8,128)(2,1)S(1)} %slice.192), channel_id=1, source_target_pairs={{0,1},{1,0},{2,3},{3,2},{4,5},{5,4},{6,7},{7,6},{8,9},{9,8},{10,11... | collective-permute-start | bytes 393224 | tf_op jit(solution)/shard_map/ppermute | solution.py:52
  397.0 14.5 %collective-permute-start.32 = (bf16[32,2048]{1,0:T(8,128)(2,1)}, bf16[32,2048]{1,0:T(8,128)(2,1)}, u32[]{:S(2)}, u32[]{:S(2)}) collective-permute-start(bf16[32,2048]{1,0:T(8,128)(2,1)} %slice_add_fusion), channel_id=1, source_target_pairs={{0,2},{1,3},{2,0},{3,1},{4,6},{5,7},{6,4},{7,5},{8,10},{9,11},{10,... | collective-permute-start | bytes 393224 | tf_op jit(solution)/shard_map/ppermute | solution.py:52
  414.7 11.0 %collective-permute-start.34 = (bf16[48,2048]{1,0:T(8,128)(2,1)}, bf16[48,2048]{1,0:T(8,128)(2,1)}, u32[]{:S(2)}, u32[]{:S(2)}) collective-permute-start(bf16[48,2048]{1,0:T(8,128)(2,1)} %pad_maximum_fusion.2), channel_id=1, source_target_pairs={{0,8},{4,12},{8,0},{12,4},{1,9},{5,13},{9,1},{13,5},{2,10},{6,14},... | collective-permute-start | bytes 589832 | tf_op jit(solution)/shard_map/ppermute | solution.py:52
  (80 other events, 578.0 us)
Sparse Core Ops, SparseCore 0:
  10.2 84.7 all-gather.3
  137.3 34.8 all-gather.5
  174.5 34.1 reduce-scatter.4
  211.4 34.2 reduce-scatter.6
  282.3 59.6 reduce-scatter.8
  346.8 65.2 reduce-scatter.10
